TPU v7x, 256 devices: a whole 4x4x8 slice. The times are simulated.
256 devices in a mesh: context: 32 (over x, z_hi, y), tensor: 8 (over z_lo, core).
Axes of the slice: x: 4, y: 4, z: 8 (z_hi: 2, z_lo: 4; z = z_hi * 4 + z_lo), core: 2. Of those that a mesh axis runs over, the one named last changes fastest.
Arguments:
- q_proj: bfloat16 [8192, 8192], P('tensor', 'context'), may hold values from -6 to 6
- k_proj: bfloat16 [8192, 8192], P('tensor', 'context'), may hold values from -6 to 6
- v_proj: bfloat16 [8192, 8192], P('tensor', 'context'), may hold values from -6 to 6
- filter_taps: bfloat16 [512, 128], P('tensor'), may hold values from -0.5 to 0.5
- out_weight: bfloat16 [8192, 4096], P('tensor'), may hold values from -0.09375 to 0.09375
- cotangent: bfloat16 [8192, 4096], P('context', 'tensor'), may hold values from -6 to 6
Outputs:
- block_output: bfloat16 [8192, 4096], P('context', 'tensor')
- q_grad: bfloat16 [8192, 8192], P('tensor', 'context')
- k_grad: bfloat16 [8192, 8192], P('tensor', 'context')
- v_grad: bfloat16 [8192, 8192], P('tensor', 'context')
- filter_grad: float32 [512, 128], P('tensor')
All inputs are finite; a program needn't handle non-finite values.
Results may differ from a plain program's by a relative error of at most 0.0064.
Values may be sent and summed in bfloat16 or wider, within the bound.
No kernel may reach another device: no remote copies, remote signals or barrier semaphores. Data moves between devices by JAX's collectives and lax.ppermute only.
A program may use at most 128 MiB of HBM per device.

v0:
```python
import math

import jax
import jax.numpy as jnp
from jax import lax
from jax.sharding import PartitionSpec as P

D = 8192
GROUPS = 512


def toeplitz(taps_here):
    group_count, tap_count = taps_here.shape
    zero_head = jnp.zeros((group_count, tap_count), taps_here.dtype)
    zero_tail = jnp.zeros((group_count, tap_count + 1), taps_here.dtype)
    extended = jnp.concatenate([zero_head, taps_here[:, ::-1], zero_tail], axis=1)
    tiled = jnp.tile(extended, (1, tap_count))[:, : 3 * tap_count * tap_count]
    sheared = tiled.reshape(group_count, tap_count, 3 * tap_count)
    return sheared[:, :, tap_count - 1 : 3 * tap_count - 1]


def filter_forward(banded, window):
    tap_count = banded.shape[1]
    within = jnp.einsum(
        "gij,gcbj->gcbi",
        banded[:, :, tap_count:],
        window[:, :, 1:],
        preferred_element_type=jnp.float32,
    )
    before = jnp.einsum(
        "gij,gcbj->gcbi",
        banded[:, :, :tap_count],
        window[:, :, :-1],
        preferred_element_type=jnp.float32,
    )
    return within + before


def filter_backward(banded, grad_window):
    tap_count = banded.shape[1]
    within = jnp.einsum(
        "gij,gcbi->gcbj",
        banded[:, :, tap_count:],
        grad_window[:, :, :-1],
        preferred_element_type=jnp.float32,
    )
    after = jnp.einsum(
        "gij,gcbi->gcbj",
        banded[:, :, :tap_count],
        grad_window[:, :, 1:],
        preferred_element_type=jnp.float32,
    )
    return within + after


def taps_gradient(grad_blocks, window):
    group_count, tap_count = (grad_blocks.shape[0], grad_blocks.shape[3])
    before = jnp.einsum(
        "gcbi,gcbj->gij", grad_blocks, window[:, :, :-1], preferred_element_type=jnp.float32
    )
    within = jnp.einsum(
        "gcbi,gcbj->gij", grad_blocks, window[:, :, 1:], preferred_element_type=jnp.float32
    )
    moments = jnp.concatenate([before, within], axis=2)[:, :, ::-1]
    padded = jnp.pad(moments, ((0, 0), (0, 0), (0, tap_count)))
    flattened = padded.reshape(group_count, 3 * tap_count * tap_count)[
        :, : tap_count * (3 * tap_count - 1)
    ]
    sheared = flattened.reshape(group_count, tap_count, 3 * tap_count - 1)
    return jnp.sum(sheared, axis=1)[:, tap_count - 1 : 2 * tap_count - 1]


def body(q_proj, k_proj, v_proj, filter_taps, out_weight, cotangent):
    chan_count, tok_count = q_proj.shape
    tap_count = filter_taps.shape[1]
    group_size = D // GROUPS
    seq_total = tok_count * lax.axis_size("context")
    norm_scale = 1.0 / math.sqrt(group_size * seq_total)
    q_wide = q_proj.astype(jnp.float32)
    k_wide = k_proj.astype(jnp.float32)
    v_wide = v_proj.astype(jnp.float32)
    product = (k_wide * v_wide).astype(jnp.bfloat16)
    lane_count = lax.axis_size("context")
    local_chans = chan_count // lane_count
    local_groups = local_chans // group_size
    columns = lax.all_to_all(product, "context", split_axis=0, concat_axis=1, tiled=True)
    own_taps = lax.dynamic_slice_in_dim(
        filter_taps, lax.axis_index("context") * local_groups, local_groups, 0
    )
    banded = toeplitz(own_taps)
    blocks = columns.reshape(local_groups, group_size, seq_total // tap_count, tap_count)
    window = jnp.concatenate([jnp.zeros_like(blocks[:, :, :1]), blocks], axis=2)
    filtered_cols = (
        filter_forward(banded, window).reshape(local_chans, seq_total).astype(jnp.bfloat16)
    )
    filtered = lax.all_to_all(filtered_cols, "context", split_axis=1, concat_axis=0, tiled=True)
    filtered_wide = filtered.astype(jnp.float32)
    gated = (q_wide * filtered_wide).astype(jnp.bfloat16)
    partial_out = lax.dot_general(
        gated, out_weight, (((0,), (0,)), ((), ())), preferred_element_type=jnp.float32
    )
    block_output = lax.psum_scatter(partial_out, "tensor", scatter_dimension=1, tiled=True).astype(
        jnp.bfloat16
    )
    gated_grad = lax.dot_general(
        out_weight,
        lax.all_gather(cotangent, "tensor", axis=1, tiled=True),
        (((1,), (1,)), ((), ())),
        preferred_element_type=jnp.float32,
    )
    q_grad = (gated_grad * filtered_wide).astype(jnp.bfloat16)
    filtered_grad = (gated_grad * q_wide).astype(jnp.bfloat16)
    grad_columns = lax.all_to_all(filtered_grad, "context", split_axis=0, concat_axis=1, tiled=True)
    grad_blocks = grad_columns.reshape(local_groups, group_size, seq_total // tap_count, tap_count)
    grad_window = jnp.concatenate([grad_blocks, jnp.zeros_like(grad_blocks[:, :, :1])], axis=2)
    signal_cols = (
        filter_backward(banded, grad_window).reshape(local_chans, seq_total).astype(jnp.bfloat16)
    )
    product_grad = lax.all_to_all(signal_cols, "context", split_axis=1, concat_axis=0, tiled=True)
    local_taps = taps_gradient(grad_blocks, window) * norm_scale
    filter_grad = lax.all_gather(local_taps, "context", axis=0, tiled=True)
    product_wide = product_grad.astype(jnp.float32)
    k_grad = (product_wide * v_wide).astype(jnp.bfloat16)
    v_grad = (product_wide * k_wide).astype(jnp.bfloat16)
    return (block_output, q_grad, k_grad, v_grad, filter_grad)


def solution(mesh):
    placed = (
        P("tensor", "context"),
        P("tensor", "context"),
        P("tensor", "context"),
        P("tensor", None),
        P("tensor", None),
        P("context", "tensor"),
    )
    return jax.shard_map(
        body,
        mesh=mesh,
        in_specs=placed,
        out_specs=(
            P("context", "tensor"),
            P("tensor", "context"),
            P("tensor", "context"),
            P("tensor", "context"),
            P("tensor", None),
        ),
        check_vma=False,
    )
```

profile of v0, /device:TPU:8, one launch (start us, length us, event | category | flops | bytes accessed | tf_op | source)
XLA Modules:
  0.0 254.7 jit_solution(16635656503538143786)
XLA Ops:
  7.2 0.7 all-gather.3.cloned.1.call-update
  7.9 2.1 fusion.5
  10.1 14.2 %all-to-all-start = ((bf16[32,32,256]{2,1,0:T(8,128)(2,1)}), bf16[32,32,256]{2,1,0:T(8,128)(2,1)S(1)}, u32[]{:S(2)}, u32[]{:S(2)}) async-start(bf16[32,32,256]{2,1,0:T(8,128)(2,1)} %bitcast), calls=%async_computation | async-start | bytes 1048576 | tf_op jit(solution)/shard_map/all_to_all | solution.py:86
  24.5 0.7 tile.10
  25.4 23.7 %all-to-all-done = bf16[32,32,256]{2,1,0:T(8,128)(2,1)S(1)} async-done(((bf16[32,32,256]{2,1,0:T(8,128)(2,1)}), bf16[32,32,256]{2,1,0:T(8,128)(2,1)S(1)}, u32[]{:S(2)}, u32[]{:S(2)}) %all-to-all-start) | async-done | bytes 524320 | tf_op jit(solution)/shard_map/all_to_all | solution.py:86
  49.5 0.4 fusion.9
  49.9 0.4 fusion
  50.5 0.3 copy.21
  50.8 23.3 %all_to_all.52 = bf16[32,32,256]{2,0,1:T(8,128)(2,1)S(1)} all-to-all(bf16[32,32,256]{2,0,1:T(8,128)(2,1)S(1)} %copy.21), channel_id=1, replica_groups=mesh['context'=32,'tensor'=8] {'context'}, dimensions={1} | all-to-all | bytes 1048576 | tf_op jit(solution)/shard_map/all_to_all | solution.py:96
  74.0 7.2 %fusion.3 = (bf16[1024,256]{1,0:T(8,128)(2,1)S(1)}, bf16[1024,256]{1,0:T(8,128)(2,1)}, bf16[1024,256]{1,0:T(8,128)(2,1)S(1)}) fusion(bf16[1024,256]{1,0:T(8,128)(2,1)S(1)} %copy-done.3, bf16[32,32,256]{2,0,1:T(8,128)(2,1)S(1)} %all_to_all.52, bf16[1024,4096]{1,0:T(8,128)(2,1)} %param.10, bf16[256,4096]{1,0:T(8,128)(2,1)} %all-gather.3.cloned.1.call-done), kind=kOutput, calls=%fused_computation.12 | convolution fusion | flops 2149580800 | bytes 13107200 | tf_op jit(solution)/shard_map/dot_general | solution.py:105
  81.3 7.7 %fusion.14 = f32[256,4096]{1,0:T(8,128)} fusion(bf16[1024,256]{1,0:T(8,128)(2,1)S(1)} %get-tuple-element.7, bf16[1024,4096]{1,0:T(8,128)(2,1)} %param.10), kind=kOutput, calls=%fused_computation.34 | convolution fusion | flops 2147483648 | bytes 13107200 | tf_op jit(solution)/shard_map/dot_general | solution.py:99
  89.0 27.9 %all_to_all.53 = bf16[32,32,256]{2,1,0:T(8,128)(2,1)S(1)} all-to-all(bf16[32,32,256]{2,1,0:T(8,128)(2,1)S(1)} %bitcast.65), channel_id=1, replica_groups=mesh['context'=32,'tensor'=8] {'context'}, dimensions={0} | all-to-all | bytes 1048576 | tf_op jit(solution)/shard_map/all_to_all | solution.py:113
  117.4 0.4 fusion.8
  117.7 0.4 fusion.1
  118.3 1.1 copy.23
  119.4 5.9 %all-to-all-start.3 = ((bf16[32,32,256]{2,0,1:T(8,128)(2,1)}), bf16[32,32,256]{2,0,1:T(8,128)(2,1)S(1)}, u32[]{:S(2)}, u32[]{:S(2)}) async-start(bf16[32,32,256]{2,0,1:T(8,128)(2,1)} %copy.23), calls=%async_computation.4 | async-start | bytes 1048576 | tf_op jit(solution)/shard_map/all_to_all | solution.py:119
  125.3 0.4 convolution_bitcast_fusion.1
  125.7 0.3 convolution_bitcast_fusion
  126.4 0.3 copy.31
  126.7 0.5 reshape.57
  127.4 116.8 %all-gather = f32[32,2,128]{2,1,0:T(2,128)S(1)} all-gather(f32[1,2,128]{2,1,0:T(2,128)S(1)} %fusion.10), channel_id=1, replica_groups=mesh['context'=32,'tensor'=8] {'context'}, dimensions={0}, use_global_device_ids=true | all-gather | bytes 33792 | tf_op jit(solution)/shard_map/all_gather | solution.py:121
  244.2 1.2 fusion.4
  245.5 1.8 convert_element_type.74
  247.2 0.6 copy.35
  (37 shorter events, 2.2 us)
Async XLA Ops:
  7.2 17.1 %copy-start = (bf16[64,128]{1,0:T(8,128)(2,1)S(1)}, bf16[64,128]{1,0:T(8,128)(2,1)}, u32[]{:S(2)}) copy-start(bf16[64,128]{1,0:T(8,128)(2,1)} %param.9) | copy-start | bytes 49156
  7.2 66.8 %copy-start.3 = (bf16[1024,256]{1,0:T(8,128)(2,1)S(1)}, bf16[1024,256]{1,0:T(8,128)(2,1)}, u32[]{:S(2)}) copy-start(bf16[1024,256]{1,0:T(8,128)(2,1)} %param.6) | copy-start | bytes 1572868
  7.2 66.8 %all-gather.3.cloned.1.call-start = ((), (), s32[]{:S(2)}) async-start(), calls=%async_computation.6 | async-start | bytes 2359296 | tf_op jit(solution)/shard_map/all_gather | solution.py:107
  10.1 39.0 %all-to-all-start = ((bf16[32,32,256]{2,1,0:T(8,128)(2,1)}), bf16[32,32,256]{2,1,0:T(8,128)(2,1)S(1)}, u32[]{:S(2)}, u32[]{:S(2)}) async-start(bf16[32,32,256]{2,1,0:T(8,128)(2,1)} %bitcast), calls=%async_computation | async-start | bytes 1048576 | tf_op jit(solution)/shard_map/all_to_all | solution.py:86
  24.2 221.2 %reduce-scatter.2.cloned.1.call-start = ((), (), s32[]{:S(2)}) async-start(), calls=%async_computation.5 | async-start | bytes 4718592 | tf_op jit(solution)/shard_map/reduce_scatter | solution.py:102
  116.9 127.3 %copy-start.1 = (bf16[1024,256]{1,0:T(8,128)(2,1)S(1)}, bf16[1024,256]{1,0:T(8,128)(2,1)}, u32[]{:S(2)}) copy-start(bf16[1024,256]{1,0:T(8,128)(2,1)} %param.8) | copy-start | bytes 1572868
  116.9 127.3 %copy-start.2 = (bf16[1024,256]{1,0:T(8,128)(2,1)S(1)}, bf16[1024,256]{1,0:T(8,128)(2,1)}, u32[]{:S(2)}) copy-start(bf16[1024,256]{1,0:T(8,128)(2,1)} %param.7) | copy-start | bytes 1572868
  119.4 124.8 %all-to-all-start.3 = ((bf16[32,32,256]{2,0,1:T(8,128)(2,1)}), bf16[32,32,256]{2,0,1:T(8,128)(2,1)S(1)}, u32[]{:S(2)}, u32[]{:S(2)}) async-start(bf16[32,32,256]{2,0,1:T(8,128)(2,1)} %copy.23), calls=%async_computation.4 | async-start | bytes 1048576 | tf_op jit(solution)/shard_map/all_to_all | solution.py:119
Sparse Core Ops, SparseCore 0:
  9.8 50.0 all-gather.2
  89.1 69.4 reduce-scatter.1
where the time goes:
time: 255 us
  blocking collectives  168 us (66%)
  waiting for transfers between devices  24.4 us (10%)
  starting transfers between devices  20.2 us (8%)
  matrix products  17.1 us (7%)
  between operations  14.3 us (6%)
  local copies, waits for them, and re-layouts  5.49 us (2%)
  other arithmetic  5.26 us (2%)
    all_gather x1, blocking collectives, body(): filter_grad = lax.all_gather(local_taps, 'context', axis=0, tiled=True)  117 us
    all_to_all x1, blocking collectives, body(): lax.all_to_all(filtered_grad, 'context', split_axis=0, concat_axis=1, til...  27.9 us
    all_to_all x1, waiting for transfers between devices, body(): lax.all_to_all(product, 'context', split_axis=0, concat_axis=1, tiled=True)  23.7 us
    all_to_all x1, blocking collectives, body(): lax.all_to_all(filtered_cols, 'context', split_axis=1, concat_axis=0, til...  23.3 us
    all_to_all x1, starting transfers between devices, body(): lax.all_to_all(product, 'context', split_axis=0, concat_axis=1, tiled=True)  14.2 us
    dot_general x1, matrix products, body(): lax.dot_general(gated, out_weight, (((0,), (0,)), ((), ())), preferred_el...  7.71 us
    dot_general x1, matrix products, body(): lax.dot_general(out_weight, lax.all_gather(cotangent, 'tensor', axis=1, t...  7.23 us
    all_to_all x1, starting transfers between devices, body(): lax.all_to_all(signal_cols, 'context', split_axis=1, concat_axis=0, tiled...  5.92 us
  transfers between devices with their start and end apart: 4, of which 1 were waited for; matrix products, arithmetic and copies ran while one was open for 4% of the time, Pallas kernels for 0%

commit v1 on v0

v1 whole, which is shorter than its diff:
```python
import math

import jax
import jax.numpy as jnp
from jax import lax
from jax.experimental import pallas as pl
from jax.experimental.pallas import tpu as pltpu
from jax.sharding import PartitionSpec as P

D = 8192
GROUPS = 512
FL = 128
GS = D // GROUPS
F32 = jnp.float32
BF = jnp.bfloat16
VM = pl.BlockSpec(memory_space=pltpu.VMEM)
SM = pl.BlockSpec(memory_space=pltpu.SMEM)
PARAMS = pltpu.CompilerParams(vmem_limit_bytes=24 << 20)


def call(kernel, outs, args, specs=None, scratch=(), name=None, flops=0, bytes_=0):
    return pl.pallas_call(
        kernel,
        out_shape=outs,
        in_specs=[VM] * len(args) if specs is None else specs,
        out_specs=jax.tree.map(lambda _: VM, outs),
        scratch_shapes=list(scratch),
        compiler_params=PARAMS,
        cost_estimate=pl.CostEstimate(flops=flops, bytes_accessed=bytes_, transcendentals=0),
        name=name,
    )(*args)


def shape(*dims, dt=BF):
    return jax.ShapeDtypeStruct(dims, dt)


def shear(row):
    return pltpu.roll(jnp.broadcast_to(row, (FL, 2 * FL)), 0, 1, stride=1, stride_axis=0)


def product_kernel(k_ref, v_ref, p0_ref, p1_ref):
    for half, ref in ((0, p0_ref), (1, p1_ref)):
        cols = slice(half * FL, (half + 1) * FL)
        ref[...] = (k_ref[:, cols].astype(F32) * v_ref[:, cols].astype(F32)).astype(BF)


def bands_kernel(taps_ref, fwd_ref, bwd_ref):
    taps = taps_ref[...].astype(F32)
    ahead = jnp.concatenate([taps, jnp.zeros_like(taps)], axis=1)
    row = lax.broadcasted_iota(jnp.int32, (FL, 2 * FL), 0)
    col = lax.broadcasted_iota(jnp.int32, (FL, 2 * FL), 1)
    mirror = ((row + col) % (2 * FL) == 0).astype(BF)
    back = jnp.dot(taps_ref[...], mirror, preferred_element_type=F32)
    for g in range(taps_ref.shape[0]):
        fwd = shear(ahead[g : g + 1]).astype(BF)
        bwd = shear(back[g : g + 1]).astype(BF)
        fwd_ref[g, :FL, :] = fwd[:, FL:]
        fwd_ref[g, FL:, :] = fwd[:, :FL]
        bwd_ref[g, :FL, :] = bwd[:, :FL]
        bwd_ref[g, FL:, :] = bwd[:, FL:]


def forward_kernel(half, place_ref, prev_ref, cur_ref, q_ref, band_ref, w_ref, fil_ref, mine_ref, other_ref, gated_t):
    cols = slice(half * FL, (half + 1) * FL)
    for g in range(band_ref.shape[0]):
        rows = slice(g * GS, (g + 1) * GS)
        window = jnp.concatenate([prev_ref[rows, :], cur_ref[rows, :]], axis=1)
        fil_ref[rows, :] = jnp.dot(window, band_ref[g], preferred_element_type=F32).astype(BF)
    gated = (q_ref[:, cols].astype(F32) * fil_ref[...].astype(F32)).astype(BF)
    gated_t[...] = gated.T
    z, core = place_ref[0], place_ref[1]
    width = mine_ref.shape[2]
    for k in range(mine_ref.shape[0]):
        for ref, side in ((mine_ref, core), (other_ref, 1 - core)):
            start = pl.multiple_of((2 * (z ^ k) + side) * width, width)
            ref[k] = jnp.dot(
                gated_t[...], w_ref[:, pl.ds(start, width)], preferred_element_type=F32
            ).astype(BF)


def gather_cot(place_ref, own_ref, own_other_ref, got_refs, got_other_ref, cot_t):
    z, core = place_ref[0], place_ref[1]
    width = own_ref.shape[1]
    for k in range(4):
        piece = own_ref[...] if k == 0 else got_refs[k - 1][...]
        other = own_other_ref[...] if k == 0 else got_other_ref[k - 1]
        for part, side in ((piece, core), (other, 1 - core)):
            start = pl.multiple_of((2 * (z ^ k) + side) * width, width)
            cot_t[pl.ds(start, width), :] = part.T


def grad_first_kernel(place_ref, own, own_other, g1, g2, g3, got_other, w_ref, q_ref, gg_ref, fg_ref, cot_t):
    gather_cot(place_ref, own, own_other, (g1, g2, g3), got_other, cot_t)
    gg = jnp.dot(w_ref[...], cot_t[...], preferred_element_type=F32)
    gg_ref[...] = gg
    fg_ref[...] = (gg * q_ref[:, :FL].astype(F32)).astype(BF)


def grad_second_kernel(
    place_ref, own, own_other, g1, g2, g3, got_other, w_ref, q_ref, gg0_ref, fg0_ref, fil0_ref, fil1_ref,
    halo_ref, p0_ref, p1_ref, qg_ref, fg_ref, taps_ref, cot_t, flip0, flip1,
):
    gather_cot(place_ref, own, own_other, (g1, g2, g3), got_other, cot_t)
    gg = jnp.dot(w_ref[...], cot_t[...], preferred_element_type=F32)
    fg = (gg * q_ref[:, FL:].astype(F32)).astype(BF)
    fg_ref[...] = fg
    qg_ref[:, FL:] = (gg * fil1_ref[...].astype(F32)).astype(BF)
    qg_ref[:, :FL] = (gg0_ref[...] * fil0_ref[...].astype(F32)).astype(BF)
    row = lax.broadcasted_iota(jnp.int32, (FL, FL), 0)
    col = lax.broadcasted_iota(jnp.int32, (FL, FL), 1)
    mirror = (row + col == FL - 1).astype(BF)
    flip0[...] = jnp.dot(fg0_ref[...], mirror, preferred_element_type=F32).astype(BF)
    flip1[...] = jnp.dot(fg_ref[...], mirror, preferred_element_type=F32).astype(BF)
    for g in range(taps_ref.shape[0]):
        rows = slice(g * GS, (g + 1) * GS)
        p0 = p0_ref[rows, :]
        grads = jnp.concatenate([flip0[rows, :], flip1[rows, :]], axis=0)
        window = jnp.concatenate(
            [
                jnp.concatenate([halo_ref[rows, :], p0], axis=1),
                jnp.concatenate([p0, p1_ref[rows, :]], axis=1),
            ],
            axis=0,
        )
        moments = lax.dot_general(
            grads, window, (((0,), (0,)), ((), ())), preferred_element_type=F32
        )
        sheared = pltpu.roll(moments, 0, 1, stride=1, stride_axis=0)
        taps_ref[g : g + 1, :] = jnp.sum(sheared[:, FL:], axis=0, keepdims=True)


def backward_kernel(fg0_ref, fg1_ref, next_ref, band_ref, k_ref, v_ref, kg_ref, vg_ref):
    for g in range(band_ref.shape[0]):
        rows = slice(g * GS, (g + 1) * GS)
        fg1 = fg1_ref[rows, :]
        window = jnp.concatenate(
            [
                jnp.concatenate([fg0_ref[rows, :], fg1], axis=1),
                jnp.concatenate([fg1, next_ref[rows, :]], axis=1),
            ],
            axis=0,
        )
        both = jnp.dot(window, band_ref[g], preferred_element_type=F32).astype(BF).astype(F32)
        pg = jnp.concatenate([both[:GS], both[GS:]], axis=1)
        kg_ref[rows, :] = (pg * v_ref[rows, :].astype(F32)).astype(BF)
        vg_ref[rows, :] = (pg * k_ref[rows, :].astype(F32)).astype(BF)


def body(q_proj, k_proj, v_proj, filter_taps, out_weight, cotangent):
    chans, toks = q_proj.shape
    groups = filter_taps.shape[0]
    feats = out_weight.shape[1]
    width = cotangent.shape[1]
    n_ctx, n_ten = lax.axis_size("context"), lax.axis_size("tensor")
    scale = 1.0 / math.sqrt(GS * toks * n_ctx)
    zs = n_ten // 2
    me = lax.axis_index("tensor")
    place = jnp.stack([me // 2, me % 2]).astype(jnp.int32)

    def across(array, k):
        return lax.ppermute(array, "tensor", [(j, j ^ k) for j in range(n_ten)])

    p0, p1 = call(product_kernel, [shape(chans, FL)] * 2, (k_proj, v_proj), name="product")
    halo = lax.ppermute(p1, "context", [(i, i + 1) for i in range(n_ctx - 1)])

    cots = []
    for half in range(2):
        own = cotangent[half * FL : (half + 1) * FL]
        own_other = across(own, 1)
        got = [across(own, 2 * k) for k in range(1, zs)]
        got_other = across(jnp.stack(got), 1)
        cots.append((own, own_other, *got, got_other))

    band_f, band_b = call(bands_kernel, [shape(groups, 2 * FL, FL)] * 2, (filter_taps,), name="bands")

    def forward(half, prev, cur):
        fil, mine, other = call(
            lambda *refs: forward_kernel(half, *refs),
            [shape(chans, FL), shape(zs, FL, width), shape(zs, FL, width)],
            (place, prev, cur, q_proj, band_f, out_weight),
            specs=[SM] + [VM] * 5,
            scratch=[pltpu.VMEM((FL, chans), BF)],
            name=f"forward{half}",
            flops=2 * chans * FL * feats,
        )
        swapped = across(other, 1)
        total = mine.astype(F32) + swapped.astype(F32)
        rest = [across(total[k].astype(BF), 2 * k) for k in range(1, zs)]
        return fil, (total[0], rest)

    def finish(total, rest):
        for r in rest:
            total = total + r.astype(F32)
        return total.astype(BF)

    fil1, out1 = forward(1, p0, p1)

    n_cot = len(cots[0])
    gg0, fg0 = call(
        grad_first_kernel,
        [shape(chans, FL, dt=F32), shape(chans, FL)],
        (place, *cots[0], out_weight, q_proj),
        specs=[SM] + [VM] * (n_cot + 2),
        scratch=[pltpu.VMEM((feats, FL), BF)],
        name="grad0",
        flops=2 * chans * FL * feats,
    )
    after = lax.ppermute(fg0, "context", [(i + 1, i) for i in range(n_ctx - 1)])

    fil0, out0 = forward(0, halo, p0)

    q_grad, fg1, taps_part = call(
        grad_second_kernel,
        [shape(chans, toks), shape(chans, FL), shape(groups, FL, dt=F32)],
        (place, *cots[1], out_weight, q_proj, gg0, fg0, fil0, fil1, halo, p0, p1),
        specs=[SM] + [VM] * (n_cot + 9),
        scratch=[pltpu.VMEM((feats, FL), BF), pltpu.VMEM((chans, FL), BF), pltpu.VMEM((chans, FL), BF)],
        name="grad1",
        flops=2 * chans * FL * feats,
    )
    step = 1
    while step < n_ctx:
        taps_part = taps_part + lax.ppermute(
            taps_part, "context", [(i, i ^ step) for i in range(n_ctx)]
        )
        step *= 2
    filter_grad = taps_part[:, ::-1] * scale

    k_grad, v_grad = call(
        backward_kernel,
        [shape(chans, toks)] * 2,
        (fg0, fg1, after, band_b, k_proj, v_proj),
        name="backward",
    )
    block_output = jnp.concatenate([finish(*out0), finish(*out1)], axis=0)
    return (block_output, q_grad, k_grad, v_grad, filter_grad)


def solution(mesh):
    placed = (
        P("tensor", "context"),
        P("tensor", "context"),
        P("tensor", "context"),
        P("tensor", None),
        P("tensor", None),
        P("context", "tensor"),
    )
    return jax.shard_map(
        body,
        mesh=mesh,
        in_specs=placed,
        out_specs=(
            P("context", "tensor"),
            P("tensor", "context"),
            P("tensor", "context"),
            P("tensor", "context"),
            P("tensor", None),
        ),
        check_vma=False,
    )
```

time: 255 us -> 111 us (0.44)
  the two profiles are of different devices: /device:TPU:8 before, /device:TPU:6 now
where the time goes in v1:
time: 111 us; the launch traced here: 110 us
  waiting for transfers between devices  36.4 us (33%)
  starting transfers between devices  35.6 us (32%)
  Pallas kernels  19.8 us (18%)
  local copies, waits for them, and re-layouts  13.8 us (12%)
  other arithmetic  3.4 us (3%)
    ppermute x18, starting transfers between devices, across(): return lax.ppermute(array, 'tensor', [(j, j ^ k) for j in range(n_ten)])  20.8 us
    pallas_call x7, Pallas kernels, call(): pl.pallas_call(kernel, out_shape=outs, in_specs=[VM] * len(args) if specs...  19.8 us
    ppermute x5, waiting for transfers between devices, body(): lax.ppermute(taps_part, 'context', [(i, i ^ step) for i in range(n_ctx)])  18.4 us
    ppermute x1, waiting for transfers between devices, body(): halo = lax.ppermute(p1, 'context', [(i, i + 1) for i in range(n_ctx - 1)])  16.5 us
    unnamed x20, local copies, waits for them, and re-layouts  11.4 us
    ppermute x1, starting transfers between devices, body(): after = lax.ppermute(fg0, 'context', [(i + 1, i) for i in range(n_ctx - 1)])  6.97 us
    ppermute x5, starting transfers between devices, body(): lax.ppermute(taps_part, 'context', [(i, i ^ step) for i in range(n_ctx)])  4.39 us
    ppermute x1, starting transfers between devices, body(): halo = lax.ppermute(p1, 'context', [(i, i + 1) for i in range(n_ctx - 1)])  3.48 us
  transfers between devices with their start and end apart: 25, of which 6 were waited for; matrix products, arithmetic and copies ran while one was open for 4% of the time, Pallas kernels for 18%

profile of v1, /device:TPU:6, one launch (start us, length us, event | category | flops | bytes accessed | tf_op | source)
XLA Modules:
  0.0 109.9 jit_solution(10303778987618635854)
XLA Ops:
  1.6 2.0 %collective-permute-start.15 = (bf16[128,512]{1,0:T(8,128)(2,1)S(1)}, bf16[128,512]{1,0:T(8,128)(2,1)S(1)}, u32[]{:S(2)}, u32[]{:S(2)}) collective-permute-start(bf16[128,512]{1,0:T(8,128)(2,1)S(1)} %get-tuple-element.49.own), channel_id=1, source_target_pairs={{0,2},{1,3},{2,0},{3,1},{4,6},{5,7},{6,4},{7,5},{8,10},{9,11},{10,... | collective-permute-start | bytes 393224 | tf_op jit(solution)/shard_map/ppermute | solution.py:162
  3.6 3.3 %collective-permute-start.16 = (bf16[128,512]{1,0:T(8,128)(2,1)S(1)}, bf16[128,512]{1,0:T(8,128)(2,1)S(1)}, u32[]{:S(2)}, u32[]{:S(2)}) collective-permute-start(bf16[128,512]{1,0:T(8,128)(2,1)S(1)} %get-tuple-element.49.own), channel_id=1, source_target_pairs={{0,4},{1,5},{2,6},{3,7},{4,0},{5,1},{6,2},{7,3},{8,12},{9,13},{10,... | collective-permute-start | bytes 393224 | tf_op jit(solution)/shard_map/ppermute | solution.py:162
  7.5 3.8 %collective-permute-start.11 = (bf16[128,512]{1,0:T(8,128)(2,1)S(1)}, bf16[128,512]{1,0:T(8,128)(2,1)S(1)}, u32[]{:S(2)}, u32[]{:S(2)}) collective-permute-start(bf16[128,512]{1,0:T(8,128)(2,1)S(1)} %get-tuple-element.50.own), channel_id=1, source_target_pairs={{0,4},{1,5},{2,6},{3,7},{4,0},{5,1},{6,2},{7,3},{8,12},{9,13},{10,... | collective-permute-start | bytes 393224 | tf_op jit(solution)/shard_map/ppermute | solution.py:162
  12.1 1.9 %bands.1 = (bf16[64,256,128]{2,1,0:T(8,128)(2,1)S(1)}, bf16[64,256,128]{2,1,0:T(8,128)(2,1)S(1)}) custom-call(bf16[64,128]{1,0:T(8,128)(2,1)S(1)} %copy-done.9), custom_call_target="tpu_custom_call" | custom-call | tf_op jit(solution)/shard_map/bands/pallas_call | solution.py:22
  14.0 1.9 %copy-done.3 = bf16[64,256,128]{2,1,0:T(8,128)(2,1)} copy-done((bf16[64,256,128]{2,1,0:T(8,128)(2,1)}, bf16[64,256,128]{2,1,0:T(8,128)(2,1)S(1)}, u32[]{:S(2)}) %copy-start.3) | copy-done | bytes 4194328
  18.2 3.4 %copy-done = bf16[1024,4096]{1,0:T(8,128)(2,1)S(1)} copy-done((bf16[1024,4096]{1,0:T(8,128)(2,1)S(1)}, bf16[1024,4096]{1,0:T(8,128)(2,1)}, u32[]{:S(2)}) %copy-start) | copy-done | bytes 8388632
  22.7 2.4 %forward1.1 = (bf16[1024,128]{1,0:T(8,128)(2,1)S(1)}, bf16[4,128,512]{2,1,0:T(8,128)(2,1)S(1)}, bf16[4,128,512]{2,1,0:T(8,128)(2,1)S(1)}) custom-call(s32[2]{0:T(128)S(1)} %pad_add_fusion.refs_0_.place_ref, bf16[1024,128]{1,0:T(8,128)(2,1)S(1)} %get-tuple-element.23.refs_2_.refs_1_.p0_ref, bf16[1024,128]{1,0:T(8,128)(2,1)S(1)} %get-tuple-element.22.refs_2_.p1_ref, ...), custom_call_target="tpu_custom_call" | custom-call | flops 1073741824 | tf_op jit(solution)/shard_map/forward1/pallas_call | solution.py:22
  25.1 3.5 %collective-permute-start = (bf16[1024,128]{1,0:T(8,128)(2,1)S(1)}, bf16[1024,128]{1,0:T(8,128)(2,1)S(1)}, u32[]{:S(2)}, u32[]{:S(2)}) collective-permute-start(bf16[1024,128]{1,0:T(8,128)(2,1)S(1)} %get-tuple-element.22.refs_2_.p1_ref), channel_id=1, source_target_pairs={{0,8},{8,16},{16,24},{24,32},{32,40},{40,48},{48,56},{56,64},{64,7... | collective-permute-start | bytes 786440 | tf_op jit(solution)/shard_map/ppermute | solution.py:165
  30.0 16.5 %collective-permute-done.refs_1_.halo_ref = bf16[1024,128]{1,0:T(8,128)(2,1)S(1)} collective-permute-done((bf16[1024,128]{1,0:T(8,128)(2,1)S(1)}, bf16[1024,128]{1,0:T(8,128)(2,1)S(1)}, u32[]{:S(2)}, u32[]{:S(2)}) %collective-permute-start) | collective-permute-done | bytes 262176 | tf_op jit(solution)/shard_map/ppermute | solution.py:165
  46.5 2.4 %forward0.1 = (bf16[1024,128]{1,0:T(8,128)(2,1)S(1)}, bf16[4,128,512]{2,1,0:T(8,128)(2,1)S(1)}, bf16[4,128,512]{2,1,0:T(8,128)(2,1)S(1)}) custom-call(s32[2]{0:T(128)S(1)} %pad_add_fusion.refs_0_.place_ref, bf16[1024,128]{1,0:T(8,128)(2,1)S(1)} %collective-permute-done.refs_1_.halo_ref, bf16[1024,128]{1,0:T(8,128)(2,1)S(1)} %get-tuple-element.23.refs_2_.refs_1_.p0_ref, ...), custom_call_target="tpu_custom_call" | custom-call | flops 1073741824 | tf_op jit(solution)/shard_map/forward0/pallas_call | solution.py:22
  49.7 3.2 %grad0.1 = (f32[1024,128]{1,0:T(8,128)S(1)}, bf16[1024,128]{1,0:T(8,128)(2,1)S(1)}) custom-call(s32[2]{0:T(128)S(1)} %pad_add_fusion.refs_0_.place_ref, bf16[128,512]{1,0:T(8,128)(2,1)S(1)} %get-tuple-element.49.own, bf16[128,512]{1,0:T(8,128)(2,1)S(1)} %collective-permute-done.14.own_other, bf16[128,512]{1,0:T(8,128)(2,1)S(1)} %collective-permute-done.15.g1, ...), custom_call_target="tpu_custom_call" | custom-call | flops 1073741824 | tf_op jit(solution)/shard_map/grad0/pallas_call | solution.py:22
  52.9 8.1 %grad1.1 = (bf16[1024,256]{1,0:T(8,128)(2,1)}, bf16[1024,128]{1,0:T(8,128)(2,1)S(1)}, f32[64,128]{1,0:T(8,128)S(1)}) custom-call(s32[2]{0:T(128)S(1)} %pad_add_fusion.refs_0_.place_ref, bf16[128,512]{1,0:T(8,128)(2,1)S(1)} %get-tuple-element.50.own, bf16[128,512]{1,0:T(8,128)(2,1)S(1)} %collective-permute-done.9.own_other, ...), custom_call_target="tpu_custom_call" | custom-call | flops 1073741824 | tf_op jit(solution)/shard_map/grad1/pallas_call | solution.py:22
  61.3 3.8 %collective-permute-start.7 = (bf16[128,512]{1,0:T(8,128)(2,1)S(1)}, bf16[128,512]{1,0:T(8,128)(2,1)S(1)}, u32[]{:S(2)}, u32[]{:S(2)}) collective-permute-start(bf16[128,512]{1,0:T(8,128)(2,1)S(1)} %get-tuple-element.48), channel_id=1, source_target_pairs={{0,4},{1,5},{2,6},{3,7},{4,0},{5,1},{6,2},{7,3},{8,12},{9,13},{10,... | collective-permute-start | bytes 393224 | tf_op jit(solution)/shard_map/ppermute | solution.py:162
  65.8 5.4 %collective-permute-done.21 = f32[64,128]{1,0:T(8,128)S(1)} collective-permute-done((f32[64,128]{1,0:T(8,128)S(1)}, f32[64,128]{1,0:T(8,128)S(1)}, u32[]{:S(2)}, u32[]{:S(2)}) %collective-permute-start.21) | collective-permute-done | bytes 32800 | tf_op jit(solution)/shard_map/ppermute | solution.py:224
  71.2 2.3 %collective-permute-start.22 = (f32[64,128]{1,0:T(8,128)S(1)}, f32[64,128]{1,0:T(8,128)S(1)}, u32[]{:S(2)}, u32[]{:S(2)}) collective-permute-start(f32[64,128]{1,0:T(8,128)S(1)} %add.54), channel_id=1, source_target_pairs={{0,32},{8,40},{16,48},{24,56},{32,0},{40,8},{48,16},{56,24},{64,96... | collective-permute-start | bytes 98312 | tf_op jit(solution)/shard_map/ppermute | solution.py:224
  73.5 5.6 %collective-permute-done.22 = f32[64,128]{1,0:T(8,128)S(1)} collective-permute-done((f32[64,128]{1,0:T(8,128)S(1)}, f32[64,128]{1,0:T(8,128)S(1)}, u32[]{:S(2)}, u32[]{:S(2)}) %collective-permute-start.22) | collective-permute-done | bytes 32800 | tf_op jit(solution)/shard_map/ppermute | solution.py:224
  79.8 3.2 %collective-permute-done.23 = f32[64,128]{1,0:T(8,128)S(1)} collective-permute-done((f32[64,128]{1,0:T(8,128)S(1)}, f32[64,128]{1,0:T(8,128)S(1)}, u32[]{:S(2)}, u32[]{:S(2)}) %collective-permute-start.23) | collective-permute-done | bytes 32800 | tf_op jit(solution)/shard_map/ppermute | solution.py:224
  83.1 7.0 %collective-permute-start.19 = (bf16[1024,128]{1,0:T(8,128)(2,1)S(1)}, bf16[1024,128]{1,0:T(8,128)(2,1)S(1)}, u32[]{:S(2)}, u32[]{:S(2)}) collective-permute-start(bf16[1024,128]{1,0:T(8,128)(2,1)S(1)} %get-tuple-element.30.fg0_ref), channel_id=1, source_target_pairs={{8,0},{16,8},{24,16},{32,24},{40,32},{48,40},{56,48},{64,56},{72,6... | collective-permute-start | bytes 786440 | tf_op jit(solution)/shard_map/ppermute | solution.py:209
  91.4 4.1 %collective-permute-done.24 = f32[64,128]{1,0:T(8,128)S(1)} collective-permute-done((f32[64,128]{1,0:T(8,128)S(1)}, f32[64,128]{1,0:T(8,128)S(1)}, u32[]{:S(2)}, u32[]{:S(2)}) %collective-permute-start.24) | collective-permute-done | bytes 32800 | tf_op jit(solution)/shard_map/ppermute | solution.py:224
  98.0 2.1 %collective-permute-start.3 = (bf16[128,512]{1,0:T(8,128)(2,1)S(1)}, bf16[128,512]{1,0:T(8,128)(2,1)S(1)}, u32[]{:S(2)}, u32[]{:S(2)}) collective-permute-start(bf16[128,512]{1,0:T(8,128)(2,1)S(1)} %get-tuple-element.45), channel_id=1, source_target_pairs={{0,4},{1,5},{2,6},{3,7},{4,0},{5,1},{6,2},{7,3},{8,12},{9,13},{10,... | collective-permute-start | bytes 393224 | tf_op jit(solution)/shard_map/ppermute | solution.py:162
  100.1 2.2 %collective-permute-start.4 = (bf16[128,512]{1,0:T(8,128)(2,1)S(1)}, bf16[128,512]{1,0:T(8,128)(2,1)S(1)}, u32[]{:S(2)}, u32[]{:S(2)}) collective-permute-start(bf16[128,512]{1,0:T(8,128)(2,1)S(1)} %get-tuple-element.44), channel_id=1, source_target_pairs={{0,6},{1,7},{2,4},{3,5},{4,2},{5,3},{6,0},{7,1},{8,14},{9,15},{10,... | collective-permute-start | bytes 393224 | tf_op jit(solution)/shard_map/ppermute | solution.py:162
  103.7 2.2 %copy-done.4 = bf16[64,256,128]{2,1,0:T(8,128)(2,1)S(1)} copy-done((bf16[64,256,128]{2,1,0:T(8,128)(2,1)S(1)}, bf16[64,256,128]{2,1,0:T(8,128)(2,1)}, u32[]{:S(2)}) %copy-start.4) | copy-done | bytes 4194328
  105.9 1.8 %backward.1 = (bf16[1024,256]{1,0:T(8,128)(2,1)}, bf16[1024,256]{1,0:T(8,128)(2,1)}) custom-call(bf16[1024,128]{1,0:T(8,128)(2,1)S(1)} %get-tuple-element.30.fg0_ref, bf16[1024,128]{1,0:T(8,128)(2,1)S(1)} %get-tuple-element.34.fg1_ref, bf16[1024,128]{1,0:T(8,128)(2,1)S(1)} %collective-permute-done.19.next_ref, bf16[64,256,128]{2,1,0:T(8,128)(2,1)S(1)} %copy-done.4, ...), custom_call_target="tpu_custom_call" | custom-call | tf_op jit(solution)/shard_map/backward/pallas_call | solution.py:22
  107.7 1.5 %collective-permute-done.3 = bf16[128,512]{1,0:T(8,128)(2,1)S(1)} collective-permute-done((bf16[128,512]{1,0:T(8,128)(2,1)S(1)}, bf16[128,512]{1,0:T(8,128)(2,1)S(1)}, u32[]{:S(2)}, u32[]{:S(2)}) %collective-permute-start.3) | collective-permute-done | bytes 131104 | tf_op jit(solution)/shard_map/ppermute | solution.py:162
  (71 shorter events, 15.5 us)
Async XLA Ops:
  1.6 16.5 %collective-permute-start.15 = (bf16[128,512]{1,0:T(8,128)(2,1)S(1)}, bf16[128,512]{1,0:T(8,128)(2,1)S(1)}, u32[]{:S(2)}, u32[]{:S(2)}) collective-permute-start(bf16[128,512]{1,0:T(8,128)(2,1)S(1)} %get-tuple-element.49.own), channel_id=1, source_target_pairs={{0,2},{1,3},{2,0},{3,1},{4,6},{5,7},{6,4},{7,5},{8,10},{9,11},{10,... | collective-permute-start | bytes 393224 | tf_op jit(solution)/shard_map/ppermute | solution.py:162
  3.6 21.4 %collective-permute-start.16 = (bf16[128,512]{1,0:T(8,128)(2,1)S(1)}, bf16[128,512]{1,0:T(8,128)(2,1)S(1)}, u32[]{:S(2)}, u32[]{:S(2)}) collective-permute-start(bf16[128,512]{1,0:T(8,128)(2,1)S(1)} %get-tuple-element.49.own), channel_id=1, source_target_pairs={{0,4},{1,5},{2,6},{3,7},{4,0},{5,1},{6,2},{7,3},{8,12},{9,13},{10,... | collective-permute-start | bytes 393224 | tf_op jit(solution)/shard_map/ppermute | solution.py:162
  6.9 21.7 %collective-permute-start.17 = (bf16[128,512]{1,0:T(8,128)(2,1)S(1)}, bf16[128,512]{1,0:T(8,128)(2,1)S(1)}, u32[]{:S(2)}, u32[]{:S(2)}) collective-permute-start(bf16[128,512]{1,0:T(8,128)(2,1)S(1)} %get-tuple-element.49.own), channel_id=1, source_target_pairs={{0,6},{1,7},{2,4},{3,5},{4,2},{5,3},{6,0},{7,1},{8,14},{9,15},{10,... | collective-permute-start | bytes 393224 | tf_op jit(solution)/shard_map/ppermute | solution.py:162
  6.9 21.8 %collective-permute-start.10 = (bf16[128,512]{1,0:T(8,128)(2,1)S(1)}, bf16[128,512]{1,0:T(8,128)(2,1)S(1)}, u32[]{:S(2)}, u32[]{:S(2)}) collective-permute-start(bf16[128,512]{1,0:T(8,128)(2,1)S(1)} %get-tuple-element.50.own), channel_id=1, source_target_pairs={{0,2},{1,3},{2,0},{3,1},{4,6},{5,7},{6,4},{7,5},{8,10},{9,11},{10,... | collective-permute-start | bytes 393224 | tf_op jit(solution)/shard_map/ppermute | solution.py:162
  7.5 21.9 %collective-permute-start.11 = (bf16[128,512]{1,0:T(8,128)(2,1)S(1)}, bf16[128,512]{1,0:T(8,128)(2,1)S(1)}, u32[]{:S(2)}, u32[]{:S(2)}) collective-permute-start(bf16[128,512]{1,0:T(8,128)(2,1)S(1)} %get-tuple-element.50.own), channel_id=1, source_target_pairs={{0,4},{1,5},{2,6},{3,7},{4,0},{5,1},{6,2},{7,3},{8,12},{9,13},{10,... | collective-permute-start | bytes 393224 | tf_op jit(solution)/shard_map/ppermute | solution.py:162
  18.1 11.2 %collective-permute-start.12 = (bf16[128,512]{1,0:T(8,128)(2,1)S(1)}, bf16[128,512]{1,0:T(8,128)(2,1)S(1)}, u32[]{:S(2)}, u32[]{:S(2)}) collective-permute-start(bf16[128,512]{1,0:T(8,128)(2,1)S(1)} %get-tuple-element.50.own), channel_id=1, source_target_pairs={{0,6},{1,7},{2,4},{3,5},{4,2},{5,3},{6,0},{7,1},{8,14},{9,15},{10,... | collective-permute-start | bytes 393224 | tf_op jit(solution)/shard_map/ppermute | solution.py:162
  25.1 21.4 %collective-permute-start = (bf16[1024,128]{1,0:T(8,128)(2,1)S(1)}, bf16[1024,128]{1,0:T(8,128)(2,1)S(1)}, u32[]{:S(2)}, u32[]{:S(2)}) collective-permute-start(bf16[1024,128]{1,0:T(8,128)(2,1)S(1)} %get-tuple-element.22.refs_2_.p1_ref), channel_id=1, source_target_pairs={{0,8},{8,16},{16,24},{24,32},{32,40},{40,48},{48,56},{56,64},{64,7... | collective-permute-start | bytes 786440 | tf_op jit(solution)/shard_map/ppermute | solution.py:165
  28.6 32.4 %collective-permute-start.5 = (bf16[4,128,512]{2,1,0:T(8,128)(2,1)S(1)}, bf16[4,128,512]{2,1,0:T(8,128)(2,1)S(1)}, u32[]{:S(2)}, u32[]{:S(2)}) collective-permute-start(bf16[4,128,512]{2,1,0:T(8,128)(2,1)S(1)} %get-tuple-element.28), channel_id=1, source_target_pairs={{0,1},{1,0},{2,3},{3,2},{4,5},{5,4},{6,7},{7,6},{8,9},{9,8},{10,11... | collective-permute-start | bytes 1572872 | tf_op jit(solution)/shard_map/ppermute | solution.py:162
  28.7 20.9 %collective-permute-start.18 = (bf16[3,128,512]{2,1,0:T(8,128)(2,1)S(1)}, bf16[3,128,512]{2,1,0:T(8,128)(2,1)S(1)}, u32[]{:S(2)}, u32[]{:S(2)}) collective-permute-start(bf16[3,128,512]{2,1,0:T(8,128)(2,1)S(1)} %pad_maximum_fusion.1), channel_id=1, source_target_pairs={{0,1},{1,0},{2,3},{3,2},{4,5},{5,4},{6,7},{7,6},{8,9},{9,8},{10,11... | collective-permute-start | bytes 1179656 | tf_op jit(solution)/shard_map/ppermute | solution.py:162
  29.4 23.5 %collective-permute-start.13 = (bf16[3,128,512]{2,1,0:T(8,128)(2,1)S(1)}, bf16[3,128,512]{2,1,0:T(8,128)(2,1)S(1)}, u32[]{:S(2)}, u32[]{:S(2)}) collective-permute-start(bf16[3,128,512]{2,1,0:T(8,128)(2,1)S(1)} %pad_maximum_fusion), channel_id=1, source_target_pairs={{0,1},{1,0},{2,3},{3,2},{4,5},{5,4},{6,7},{7,6},{8,9},{9,8},{10,11... | collective-permute-start | bytes 1179656 | tf_op jit(solution)/shard_map/ppermute | solution.py:162
  29.5 19.4 %collective-permute-start.14 = (bf16[128,512]{1,0:T(8,128)(2,1)S(1)}, bf16[128,512]{1,0:T(8,128)(2,1)S(1)}, u32[]{:S(2)}, u32[]{:S(2)}) collective-permute-start(bf16[128,512]{1,0:T(8,128)(2,1)S(1)} %get-tuple-element.49.own), channel_id=1, source_target_pairs={{0,1},{1,0},{2,3},{3,2},{4,5},{5,4},{6,7},{7,6},{8,9},{9,8},{10,11... | collective-permute-start | bytes 393224 | tf_op jit(solution)/shard_map/ppermute | solution.py:162
  46.5 6.4 %collective-permute-start.9 = (bf16[128,512]{1,0:T(8,128)(2,1)S(1)}, bf16[128,512]{1,0:T(8,128)(2,1)S(1)}, u32[]{:S(2)}, u32[]{:S(2)}) collective-permute-start(bf16[128,512]{1,0:T(8,128)(2,1)S(1)} %get-tuple-element.50.own), channel_id=1, source_target_pairs={{0,1},{1,0},{2,3},{3,2},{4,5},{5,4},{6,7},{7,6},{8,9},{9,8},{10,11... | collective-permute-start | bytes 393224 | tf_op jit(solution)/shard_map/ppermute | solution.py:162
  48.9 48.8 %collective-permute-start.1 = (bf16[4,128,512]{2,1,0:T(8,128)(2,1)S(1)}, bf16[4,128,512]{2,1,0:T(8,128)(2,1)S(1)}, u32[]{:S(2)}, u32[]{:S(2)}) collective-permute-start(bf16[4,128,512]{2,1,0:T(8,128)(2,1)S(1)} %get-tuple-element.26), channel_id=1, source_target_pairs={{0,1},{1,0},{2,3},{3,2},{4,5},{5,4},{6,7},{7,6},{8,9},{9,8},{10,11... | collective-permute-start | bytes 1572872 | tf_op jit(solution)/shard_map/ppermute | solution.py:162
  61.0 4.7 %collective-permute-start.20 = (f32[64,128]{1,0:T(8,128)S(1)}, f32[64,128]{1,0:T(8,128)S(1)}, u32[]{:S(2)}, u32[]{:S(2)}) collective-permute-start(f32[64,128]{1,0:T(8,128)S(1)} %get-tuple-element.38), channel_id=1, source_target_pairs={{0,8},{8,0},{16,24},{24,16},{32,40},{40,32},{48,56},{56,48},{64,72... | collective-permute-start | bytes 98312 | tf_op jit(solution)/shard_map/ppermute | solution.py:224
  61.2 28.8 %collective-permute-start.6 = (bf16[128,512]{1,0:T(8,128)(2,1)S(1)}, bf16[128,512]{1,0:T(8,128)(2,1)S(1)}, u32[]{:S(2)}, u32[]{:S(2)}) collective-permute-start(bf16[128,512]{1,0:T(8,128)(2,1)S(1)} %get-tuple-element.46), channel_id=1, source_target_pairs={{0,2},{1,3},{2,0},{3,1},{4,6},{5,7},{6,4},{7,5},{8,10},{9,11},{10,... | collective-permute-start | bytes 393224 | tf_op jit(solution)/shard_map/ppermute | solution.py:162
  61.3 30.0 %collective-permute-start.7 = (bf16[128,512]{1,0:T(8,128)(2,1)S(1)}, bf16[128,512]{1,0:T(8,128)(2,1)S(1)}, u32[]{:S(2)}, u32[]{:S(2)}) collective-permute-start(bf16[128,512]{1,0:T(8,128)(2,1)S(1)} %get-tuple-element.48), channel_id=1, source_target_pairs={{0,4},{1,5},{2,6},{3,7},{4,0},{5,1},{6,2},{7,3},{8,12},{9,13},{10,... | collective-permute-start | bytes 393224 | tf_op jit(solution)/shard_map/ppermute | solution.py:162
  65.1 26.3 %collective-permute-start.8 = (bf16[128,512]{1,0:T(8,128)(2,1)S(1)}, bf16[128,512]{1,0:T(8,128)(2,1)S(1)}, u32[]{:S(2)}, u32[]{:S(2)}) collective-permute-start(bf16[128,512]{1,0:T(8,128)(2,1)S(1)} %get-tuple-element.47), channel_id=1, source_target_pairs={{0,6},{1,7},{2,4},{3,5},{4,2},{5,3},{6,0},{7,1},{8,14},{9,15},{10,... | collective-permute-start | bytes 393224 | tf_op jit(solution)/shard_map/ppermute | solution.py:162
  65.7 5.5 %collective-permute-start.21 = (f32[64,128]{1,0:T(8,128)S(1)}, f32[64,128]{1,0:T(8,128)S(1)}, u32[]{:S(2)}, u32[]{:S(2)}) collective-permute-start(f32[64,128]{1,0:T(8,128)S(1)} %add.53), channel_id=1, source_target_pairs={{0,16},{8,24},{16,0},{24,8},{32,48},{40,56},{48,32},{56,40},{64,80... | collective-permute-start | bytes 98312 | tf_op jit(solution)/shard_map/ppermute | solution.py:224
  71.2 7.9 %collective-permute-start.22 = (f32[64,128]{1,0:T(8,128)S(1)}, f32[64,128]{1,0:T(8,128)S(1)}, u32[]{:S(2)}, u32[]{:S(2)}) collective-permute-start(f32[64,128]{1,0:T(8,128)S(1)} %add.54), channel_id=1, source_target_pairs={{0,32},{8,40},{16,48},{24,56},{32,0},{40,8},{48,16},{56,24},{64,96... | collective-permute-start | bytes 98312 | tf_op jit(solution)/shard_map/ppermute | solution.py:224
  83.1 20.7 %collective-permute-start.19 = (bf16[1024,128]{1,0:T(8,128)(2,1)S(1)}, bf16[1024,128]{1,0:T(8,128)(2,1)S(1)}, u32[]{:S(2)}, u32[]{:S(2)}) collective-permute-start(bf16[1024,128]{1,0:T(8,128)(2,1)S(1)} %get-tuple-element.30.fg0_ref), channel_id=1, source_target_pairs={{8,0},{16,8},{24,16},{32,24},{40,32},{48,40},{56,48},{64,56},{72,6... | collective-permute-start | bytes 786440 | tf_op jit(solution)/shard_map/ppermute | solution.py:209
  90.1 5.5 %collective-permute-start.24 = (f32[64,128]{1,0:T(8,128)S(1)}, f32[64,128]{1,0:T(8,128)S(1)}, u32[]{:S(2)}, u32[]{:S(2)}) collective-permute-start(f32[64,128]{1,0:T(8,128)S(1)} %add.56), channel_id=1, source_target_pairs={{0,128},{8,136},{16,144},{24,152},{32,160},{40,168},{48,176},{56,1... | collective-permute-start | bytes 98312 | tf_op jit(solution)/shard_map/ppermute | solution.py:224
  97.9 9.8 %collective-permute-start.2 = (bf16[128,512]{1,0:T(8,128)(2,1)S(1)}, bf16[128,512]{1,0:T(8,128)(2,1)S(1)}, u32[]{:S(2)}, u32[]{:S(2)}) collective-permute-start(bf16[128,512]{1,0:T(8,128)(2,1)S(1)} %get-tuple-element.43), channel_id=1, source_target_pairs={{0,2},{1,3},{2,0},{3,1},{4,6},{5,7},{6,4},{7,5},{8,10},{9,11},{10,... | collective-permute-start | bytes 393224 | tf_op jit(solution)/shard_map/ppermute | solution.py:162
  98.0 11.2 %collective-permute-start.3 = (bf16[128,512]{1,0:T(8,128)(2,1)S(1)}, bf16[128,512]{1,0:T(8,128)(2,1)S(1)}, u32[]{:S(2)}, u32[]{:S(2)}) collective-permute-start(bf16[128,512]{1,0:T(8,128)(2,1)S(1)} %get-tuple-element.45), channel_id=1, source_target_pairs={{0,4},{1,5},{2,6},{3,7},{4,0},{5,1},{6,2},{7,3},{8,12},{9,13},{10,... | collective-permute-start | bytes 393224 | tf_op jit(solution)/shard_map/ppermute | solution.py:162
  100.1 9.0 %collective-permute-start.4 = (bf16[128,512]{1,0:T(8,128)(2,1)S(1)}, bf16[128,512]{1,0:T(8,128)(2,1)S(1)}, u32[]{:S(2)}, u32[]{:S(2)}) collective-permute-start(bf16[128,512]{1,0:T(8,128)(2,1)S(1)} %get-tuple-element.44), channel_id=1, source_target_pairs={{0,6},{1,7},{2,4},{3,5},{4,2},{5,3},{6,0},{7,1},{8,14},{9,15},{10,... | collective-permute-start | bytes 393224 | tf_op jit(solution)/shard_map/ppermute | solution.py:162
  (11 other events, 124.6 us)

commit v2 on v1

v2 whole, which is shorter than its diff:
```python
import math

import jax
import jax.numpy as jnp
from jax import lax
from jax.experimental import pallas as pl
from jax.experimental.pallas import tpu as pltpu
from jax.sharding import PartitionSpec as P

D = 8192
GROUPS = 512
FL = 128
GS = D // GROUPS
F32 = jnp.float32
BF = jnp.bfloat16
VM = pl.BlockSpec(memory_space=pltpu.VMEM)
SM = pl.BlockSpec(memory_space=pltpu.SMEM)
PARAMS = pltpu.CompilerParams(vmem_limit_bytes=16 << 20)


def call(kernel, outs, args, specs=None, out_specs=None, scratch=(), name=None):
    return pl.pallas_call(
        kernel,
        out_shape=outs,
        in_specs=[VM] * len(args) if specs is None else specs,
        out_specs=[VM] * len(outs) if out_specs is None else out_specs,
        scratch_shapes=list(scratch),
        compiler_params=PARAMS,
        cost_estimate=pl.CostEstimate(flops=1, bytes_accessed=1, transcendentals=0),
        name=name,
    )(*args)


def shape(*dims, dt=BF):
    return jax.ShapeDtypeStruct(dims, dt)


def shear(row):
    return pltpu.roll(jnp.broadcast_to(row, (FL, 2 * FL)), 0, 1, stride=1, stride_axis=0)


def flip(array):
    row = lax.broadcasted_iota(jnp.int32, (FL, FL), 0)
    col = lax.broadcasted_iota(jnp.int32, (FL, FL), 1)
    return jnp.dot(array, (row + col == FL - 1).astype(BF), preferred_element_type=F32).astype(BF)


def half_cols(half):
    return slice(half * FL, (half + 1) * FL)


def filter_kernel(prev_ref, cur_ref, band, fil_ref, *flips):
    for ref, flipped in zip((prev_ref, cur_ref), flips):
        flipped[...] = flip(ref[...])
    for g in range(band.shape[0]):
        rows = slice(g * GS, (g + 1) * GS)
        window = jnp.concatenate([prev_ref[rows, :], cur_ref[rows, :]], axis=1)
        fil_ref[rows, :] = jnp.dot(window, band[g], preferred_element_type=F32).astype(BF)


def project_kernel(place_ref, prev_ref, cur_ref, q_ref, fil1_ref, band, w_ref, fil0_ref, mine_ref, other_ref, flip_ref, gated_t):
    filter_kernel(prev_ref, cur_ref, band, fil0_ref, flip_ref)
    for half, fil_ref in enumerate((fil0_ref, fil1_ref)):
        cols = half_cols(half)
        gated_t[cols, :] = (q_ref[:, cols].astype(F32) * fil_ref[...].astype(F32)).astype(BF).T
    z, core = place_ref[0], place_ref[1]
    chips, _, width = mine_ref.shape
    for k in range(chips):
        for ref, side in ((other_ref, 1 - core), (mine_ref, core)):
            start = pl.multiple_of((2 * (z ^ k) + side) * width, width)
            ref[k] = jnp.dot(
                gated_t[...], w_ref[:, pl.ds(start, width)], preferred_element_type=F32
            ).astype(BF)


def bands_kernel(taps_ref, fwd_ref, bwd_ref):
    taps = taps_ref[...].astype(F32)
    ahead = jnp.concatenate([taps, jnp.zeros_like(taps)], axis=1)
    row = lax.broadcasted_iota(jnp.int32, (FL, 2 * FL), 0)
    col = lax.broadcasted_iota(jnp.int32, (FL, 2 * FL), 1)
    wrap = ((row + col) % (2 * FL) == 0).astype(BF)
    back = jnp.dot(taps_ref[...], wrap, preferred_element_type=F32)
    for g in range(taps_ref.shape[0]):
        fwd = shear(ahead[g : g + 1]).astype(BF)
        bwd = shear(back[g : g + 1]).astype(BF)
        fwd_ref[g, :FL, :] = fwd[:, FL:]
        fwd_ref[g, FL:, :] = fwd[:, :FL]
        bwd_ref[g, :FL, :] = bwd[:, :FL]
        bwd_ref[g, FL:, :] = bwd[:, FL:]


def grad_kernel(place_ref, own_ref, g1, g2, g3, mate_ref, w_ref, q_ref, gg_ref, fg0_ref, fg1_ref, cot_t):
    z, core = place_ref[0], place_ref[1]
    width = own_ref.shape[1]
    for k, got in enumerate((own_ref, g1, g2, g3)):
        for piece, side in ((got[...], core), (mate_ref[k], 1 - core)):
            start = pl.multiple_of((2 * (z ^ k) + side) * width, width)
            cot_t[pl.ds(start, width), :] = piece.T
    gg_ref[...] = jnp.dot(w_ref[...], cot_t[...], preferred_element_type=F32)
    for half, fg_ref in enumerate((fg0_ref, fg1_ref)):
        cols = half_cols(half)
        fg_ref[...] = (gg_ref[:, cols] * q_ref[:, cols].astype(F32)).astype(BF)


def taps_kernel(scale, fg0_ref, fg_ref, fliph, flip0, flip1, taps_ref):
    for g in range(taps_ref.shape[0]):
        rows = slice(g * GS, (g + 1) * GS)
        mid = flip0[rows, :]
        grads = jnp.concatenate([fg0_ref[rows, :], fg_ref[rows, :]], axis=0)
        window = jnp.concatenate(
            [
                jnp.concatenate([mid, fliph[rows, :]], axis=1),
                jnp.concatenate([flip1[rows, :], mid], axis=1),
            ],
            axis=0,
        )
        moments = lax.dot_general(
            grads, window, (((0,), (0,)), ((), ())), preferred_element_type=F32
        )
        sheared = pltpu.roll(moments, 1, 1, stride=1, stride_axis=0)
        taps_ref[g : g + 1, :] = jnp.sum(sheared[:, FL:], axis=0, keepdims=True) * scale


def backward_kernel(
    fg0_ref, fg1_ref, next_ref, band_ref, k_ref, v_ref, gg_ref, fil0_ref, fil1_ref, kg_ref, vg_ref, qg_ref
):
    qg_ref[:, :FL] = (gg_ref[:, :FL] * fil0_ref[...].astype(F32)).astype(BF)
    qg_ref[:, FL:] = (gg_ref[:, FL:] * fil1_ref[...].astype(F32)).astype(BF)
    for g in range(band_ref.shape[0]):
        rows = slice(g * GS, (g + 1) * GS)
        fg1 = fg1_ref[rows, :]
        window = jnp.concatenate(
            [
                jnp.concatenate([fg0_ref[rows, :], fg1], axis=1),
                jnp.concatenate([fg1, next_ref[rows, :]], axis=1),
            ],
            axis=0,
        )
        both = jnp.dot(window, band_ref[g], preferred_element_type=F32).astype(BF).astype(F32)
        pg = jnp.concatenate([both[:GS], both[GS:]], axis=1)
        kg_ref[rows, :] = (pg * v_ref[rows, :].astype(F32)).astype(BF)
        vg_ref[rows, :] = (pg * k_ref[rows, :].astype(F32)).astype(BF)


def wave(*values):
    return lax.optimization_barrier(values)


def shift_pairs(n_ctx, n_ten, by):
    ys, halves = 4, 2
    zs = n_ten // 2
    at = lambda x, z, y, core: ((x * halves + z // zs) * ys + y) * n_ten + (z % zs) * 2 + core
    direct, first, second = [], [], []
    for i in range(n_ctx):
        j = i + by
        if not 0 <= j < n_ctx:
            continue
        for t in range(n_ten):
            source, target = i * n_ten + t, j * n_ten + t
            direct.append((source, target))
            if i // ys == j // ys:
                first.append((source, target))
            else:
                z, z_half = (i // ys % halves) * zs + t // 2, zs // 2
                relay = at(i // (ys * halves), (z - z_half) % (halves * zs), j % ys, t % 2)
                first.append((source, relay))
                second.append((relay, target))
    return direct, first, second


def body(q_proj, k_proj, v_proj, filter_taps, out_weight, cotangent):
    chans, toks = q_proj.shape
    groups = filter_taps.shape[0]
    feats = out_weight.shape[1]
    width = cotangent.shape[1]
    n_ctx, n_ten = lax.axis_size("context"), lax.axis_size("tensor")
    scale = 1.0 / math.sqrt(GS * toks * n_ctx)
    zs = n_ten // 2
    me = lax.axis_index("tensor")
    place = jnp.stack([me // 2, me % 2]).astype(jnp.int32)
    half_shape = shape(chans, FL)
    gg_shape = shape(chans, toks, dt=F32)

    def move(name, array, axis, pairs):
        with jax.named_scope(name):
            return lax.ppermute(array, axis, pairs)

    def swap(name, array):
        return move(name, array, "tensor", [(j, j ^ 1) for j in range(n_ten)])

    def shift_first(name, array, by):
        direct, first, _ = shift_pairs(n_ctx, n_ten, by)
        cut = chans * 3 // 8
        axes = ("context", "tensor")
        return move(f"{name}_direct", array[:cut], axes, direct), move(f"{name}_relay", array[cut:], axes, first)

    def shift_second(name, relayed, by):
        _, _, second = shift_pairs(n_ctx, n_ten, by)
        return move(f"{name}_end", relayed, ("context", "tensor"), second)

    def shift_join(direct, relayed, end, by):
        ys = 4
        at_end = lax.axis_index("context") % ys == (0 if by > 0 else ys - 1)
        return jnp.concatenate([direct, jnp.where(at_end, end, relayed)], axis=0)

    def exchange(name, array, k):
        return move(f"{name}{k}", array, "tensor", [(j, j ^ (2 * k)) for j in range(n_ten)])

    def taps_phase(part, steps):
        got = [move(f"taps_{s}", part, "context", [(i, i ^ s) for i in range(n_ctx)]) for s in steps]
        if len(got) == 1:
            return part + got[0]
        return (part + got[0]) + (got[1] + got[2])

    got = [exchange("cot", cotangent, k) for k in range(1, zs)]
    p1, p0 = [
        (k_proj[:, c].astype(F32) * v_proj[:, c].astype(F32)).astype(BF) for c in map(half_cols, (1, 0))
    ]
    band_f, band_b = call(bands_kernel, [shape(groups, 2 * FL, FL)] * 2, (filter_taps,), name="bands")
    fil1, flip0, flip1 = call(filter_kernel, [half_shape] * 3, (p0, p1, band_f), name="filter1")
    halo = move("halo", p1, "context", [(i, i + 1) for i in range(n_ctx - 1)])
    fil0, mine, other, fliph = call(
        project_kernel,
        [half_shape, shape(zs, toks, width), shape(zs, toks, width), half_shape],
        (place, halo, p0, q_proj, fil1, band_f, out_weight),
        specs=[SM] + [VM] * 6,
        scratch=[pltpu.VMEM((toks, chans), BF)],
        name="project",
    )
    there = swap("out_swap", other)

    *got, fil0 = wave(*got, fil0)
    mate = swap("cot_swap", jnp.stack([cotangent, *got]))
    gg, fg0, fg1 = call(
        grad_kernel,
        [gg_shape, half_shape, half_shape],
        (place, cotangent, *got, mate, out_weight, q_proj),
        specs=[SM] + [VM] * (zs + 3),
        scratch=[pltpu.VMEM((feats, toks), BF)],
        name="grad",
    )
    after = move("after", fg0, "context", [(i + 1, i) for i in range(n_ctx - 1)])

    (taps_part,) = call(
        lambda *refs: taps_kernel(scale, *refs),
        [shape(groups, FL, dt=F32)],
        (fg0, fg1, fliph, flip0, flip1),
        name="taps",
    )
    there, taps_done = wave(there, taps_part)
    total = mine.astype(F32) + there.astype(F32)
    rest = [exchange("out", total[k].astype(BF), k) for k in range(1, zs)]
    for s in (8, 16, 1):
        taps_part = taps_phase(taps_part, [s])
    after, taps_part = wave(after, taps_part)
    k_grad, v_grad, q_grad = call(
        backward_kernel,
        [shape(chans, toks)] * 3,
        (fg0, fg1, after, band_b, k_proj, v_proj, gg, fil0, fil1),
        name="backward",
    )
    for s in (2, 4):
        taps_part = taps_phase(taps_part, [s])
    block_output = total[0]
    for r in rest:
        block_output = block_output + r.astype(F32)
    return (block_output.astype(BF), q_grad, k_grad, v_grad, taps_part)


def solution(mesh):
    placed = (
        P("tensor", "context"),
        P("tensor", "context"),
        P("tensor", "context"),
        P("tensor", None),
        P("tensor", None),
        P("context", "tensor"),
    )
    return jax.shard_map(
        body,
        mesh=mesh,
        in_specs=placed,
        out_specs=(
            P("context", "tensor"),
            P("tensor", "context"),
            P("tensor", "context"),
            P("tensor", "context"),
            P("tensor", None),
        ),
        check_vma=False,
    )
```

time: 111 us -> 98 us (0.88)
  the two profiles are of different devices: /device:TPU:6 before, /device:TPU:39 now
where the time goes in v2:
time: 98 us; the launch traced here: 97.7 us
  starting transfers between devices  35.6 us (36%)
  waiting for transfers between devices  33.9 us (35%)
  Pallas kernels  14.5 us (15%)
  local copies, waits for them, and re-layouts  9.54 us (10%)
  other arithmetic  3.42 us (3%)
    ppermute x15, starting transfers between devices, move(): return lax.ppermute(array, axis, pairs)  35.6 us
    ppermute x15, waiting for transfers between devices, move(): return lax.ppermute(array, axis, pairs)  33.9 us
    pallas_call x6, Pallas kernels, call(): pl.pallas_call(kernel, out_shape=outs, in_specs=[VM] * len(args) if specs...  14.5 us
    unnamed x22, local copies, waits for them, and re-layouts  9.49 us
  transfers between devices with their start and end apart: 15, of which 8 were waited for; matrix products, arithmetic and copies ran while one was open for 1% of the time, Pallas kernels for 15%

profile of v2, /device:TPU:39, one launch (start us, length us, event | category | flops | bytes accessed | tf_op | source)
XLA Modules:
  0.0 97.7 jit_solution(241092385085327171)
XLA Ops:
  0.6 1.3 %multiply_convert_fusion = (bf16[1024,128]{1,0:T(8,128)(2,1)S(1)}, bf16[1024,128]{1,0:T(8,128)(2,1)S(1)}) fusion(bf16[1024,256]{1,0:T(8,128)(2,1)} %v_ref.1, bf16[1024,256]{1,0:T(8,128)(2,1)} %k_ref.1), kind=kLoop, calls=%fused_computation.7 | loop fusion | flops 1048576 | bytes 1572864 | tf_op jit(solution)/shard_map/convert_element_type | solution.py:217
  2.0 3.2 %collective-permute-start = (bf16[1024,128]{1,0:T(8,128)(2,1)S(1)}, bf16[1024,128]{1,0:T(8,128)(2,1)S(1)}, u32[]{:S(2)}, u32[]{:S(2)}) collective-permute-start(bf16[1024,128]{1,0:T(8,128)(2,1)S(1)} %get-tuple-element.55.cur_ref), channel_id=1, source_target_pairs={{0,8},{8,16},{16,24},{24,32},{32,40},{40,48},{48,56},{56,64},{64,7... | collective-permute-start | bytes 786440 | tf_op jit(solution)/shard_map/halo/ppermute | solution.py:186
  5.3 3.1 %collective-permute-start.3 = (bf16[256,512]{1,0:T(8,128)(2,1)}, bf16[256,512]{1,0:T(8,128)(2,1)S(1)}, u32[]{:S(2)}, u32[]{:S(2)}) collective-permute-start(bf16[256,512]{1,0:T(8,128)(2,1)} %own_ref.1), channel_id=1, source_target_pairs={{0,4},{1,5},{2,6},{3,7},{4,0},{5,1},{6,2},{7,3},{8,12},{9,13},{10,... | collective-permute-start | bytes 786440 | tf_op jit(solution)/shard_map/cot2/ppermute | solution.py:186
  9.3 1.9 %bands.1 = (bf16[64,256,128]{2,1,0:T(8,128)(2,1)S(1)}, bf16[64,256,128]{2,1,0:T(8,128)(2,1)S(1)}) custom-call(bf16[64,128]{1,0:T(8,128)(2,1)S(1)} %copy-done.10), custom_call_target="tpu_custom_call" | custom-call | flops 1 | bytes 1 | tf_op jit(solution)/shard_map/bands/pallas_call | solution.py:22
  11.1 1.9 %copy-done.4 = bf16[64,256,128]{2,1,0:T(8,128)(2,1)} copy-done((bf16[64,256,128]{2,1,0:T(8,128)(2,1)}, bf16[64,256,128]{2,1,0:T(8,128)(2,1)S(1)}, u32[]{:S(2)}) %copy-start.4) | copy-done | bytes 4194328
  13.9 1.2 %copy-done.2 = bf16[64,256,128]{2,1,0:T(8,128)(2,1)} copy-done((bf16[64,256,128]{2,1,0:T(8,128)(2,1)}, bf16[64,256,128]{2,1,0:T(8,128)(2,1)S(1)}, u32[]{:S(2)}) %copy-start.2) | copy-done | bytes 4194328
  15.2 5.9 %collective-permute-done.prev_ref = bf16[1024,128]{1,0:T(8,128)(2,1)S(1)} collective-permute-done((bf16[1024,128]{1,0:T(8,128)(2,1)S(1)}, bf16[1024,128]{1,0:T(8,128)(2,1)S(1)}, u32[]{:S(2)}, u32[]{:S(2)}) %collective-permute-start) | collective-permute-done | bytes 262176 | tf_op jit(solution)/shard_map/halo/ppermute | solution.py:186
  21.1 3.4 %copy-done = bf16[1024,4096]{1,0:T(8,128)(2,1)S(1)} copy-done((bf16[1024,4096]{1,0:T(8,128)(2,1)S(1)}, bf16[1024,4096]{1,0:T(8,128)(2,1)}, u32[]{:S(2)}) %copy-start) | copy-done | bytes 8388632
  24.5 2.2 %copy-done.3 = bf16[64,256,128]{2,1,0:T(8,128)(2,1)S(1)} copy-done((bf16[64,256,128]{2,1,0:T(8,128)(2,1)S(1)}, bf16[64,256,128]{2,1,0:T(8,128)(2,1)}, u32[]{:S(2)}) %copy-start.3) | copy-done | bytes 4194328
  26.7 3.6 %project.1 = (bf16[1024,128]{1,0:T(8,128)(2,1)S(1)}, bf16[4,256,512]{2,1,0:T(8,128)(2,1)S(1)}, bf16[4,256,512]{2,1,0:T(8,128)(2,1)S(1)}, bf16[1024,128]{1,0:T(8,128)(2,1)S(1)}) custom-call(s32[2]{0:T(128)S(1)} %pad_add_fusion.place_ref, bf16[1024,128]{1,0:T(8,128)(2,1)S(1)} %collective-permute-done.prev_ref, ...), custom_call_target="tpu_custom_call" | custom-call | flops 1 | bytes 1 | tf_op jit(solution)/shard_map/project/pallas_call | solution.py:22
  31.3 3.9 %collective-permute-start.5 = (bf16[4,256,512]{2,1,0:T(8,128)(2,1)S(1)}, bf16[4,256,512]{2,1,0:T(8,128)(2,1)S(1)}, u32[]{:S(2)}, u32[]{:S(2)}) collective-permute-start(bf16[4,256,512]{2,1,0:T(8,128)(2,1)S(1)} %pad_maximum_fusion), channel_id=1, source_target_pairs={{0,1},{1,0},{2,3},{3,2},{4,5},{5,4},{6,7},{7,6},{8,9},{9,8},{10,11... | collective-permute-start | bytes 3145736 | tf_op jit(solution)/shard_map/cot_swap/ppermute | solution.py:186
  35.2 2.2 %collective-permute-done.5.mate_ref = bf16[4,256,512]{2,1,0:T(8,128)(2,1)S(1)} collective-permute-done((bf16[4,256,512]{2,1,0:T(8,128)(2,1)S(1)}, bf16[4,256,512]{2,1,0:T(8,128)(2,1)S(1)}, u32[]{:S(2)}, u32[]{:S(2)}) %collective-permute-start.5) | collective-permute-done | bytes 1048608 | tf_op jit(solution)/shard_map/cot_swap/ppermute | solution.py:186
  37.4 3.5 %grad.1 = (f32[1024,256]{1,0:T(8,128)S(1)}, bf16[1024,128]{1,0:T(8,128)(2,1)S(1)}, bf16[1024,128]{1,0:T(8,128)(2,1)S(1)}) custom-call(s32[2]{0:T(128)S(1)} %pad_add_fusion.place_ref, bf16[256,512]{1,0:T(8,128)(2,1)S(1)} %copy-done.9, bf16[256,512]{1,0:T(8,128)(2,1)S(1)} %collective-permute-done.2.g1, bf16[256,512]{1,0:T(8,128)(2,1)S(1)} %collective-permute-done.3.g2, ...), custom_call_target="tpu_custom_call" | custom-call | flops 1 | bytes 1 | tf_op jit(solution)/shard_map/grad/pallas_call | solution.py:22
  40.9 17.8 %collective-permute-start.9 = (bf16[1024,128]{1,0:T(8,128)(2,1)S(1)}, bf16[1024,128]{1,0:T(8,128)(2,1)S(1)}, u32[]{:S(2)}, u32[]{:S(2)}) collective-permute-start(bf16[1024,128]{1,0:T(8,128)(2,1)S(1)} %get-tuple-element.35.refs_0_.fg0_ref), channel_id=1, source_target_pairs={{8,0},{16,8},{24,16},{32,24},{40,32},{48,40},{56,48},{64,56},{72,6... | collective-permute-start | bytes 786440 | tf_op jit(solution)/shard_map/after/ppermute | solution.py:186
  58.8 2.8 %taps.1 = f32[64,128]{1,0:T(8,128)S(1)} custom-call(bf16[1024,128]{1,0:T(8,128)(2,1)S(1)} %get-tuple-element.35.refs_0_.fg0_ref, bf16[1024,128]{1,0:T(8,128)(2,1)S(1)} %get-tuple-element.36.refs_1_.fg1_ref, bf16[1024,128]{1,0:T(8,128)(2,1)S(1)} %get-tuple-element.37.refs_2_, bf16[1024,128]{1,0:T(8,128)(2,1)S(1)} %get-tuple-element.38.refs_3_, ...), custom_call_target="tpu_custom_call" | custom-call | flops 1 | bytes 1 | tf_op jit(solution)/shard_map/taps/pallas_call | solution.py:22
  62.7 2.1 %collective-permute-start.8 = (bf16[256,512]{1,0:T(8,128)(2,1)S(1)}, bf16[256,512]{1,0:T(8,128)(2,1)S(1)}, u32[]{:S(2)}, u32[]{:S(2)}) collective-permute-start(bf16[256,512]{1,0:T(8,128)(2,1)S(1)} %get-tuple-element.52), channel_id=1, source_target_pairs={{0,6},{1,7},{2,4},{3,5},{4,2},{5,3},{6,0},{7,1},{8,14},{9,15},{10,... | collective-permute-start | bytes 786440 | tf_op jit(solution)/shard_map/out3/ppermute | solution.py:186
  65.4 2.5 %collective-permute-done.10 = f32[64,128]{1,0:T(8,128)S(1)} collective-permute-done((f32[64,128]{1,0:T(8,128)S(1)}, f32[64,128]{1,0:T(8,128)S(1)}, u32[]{:S(2)}, u32[]{:S(2)}) %collective-permute-start.10) | collective-permute-done | bytes 32800 | tf_op jit(solution)/shard_map/taps_8/ppermute | solution.py:186
  68.7 3.4 %collective-permute-done.11 = f32[64,128]{1,0:T(8,128)S(1)} collective-permute-done((f32[64,128]{1,0:T(8,128)S(1)}, f32[64,128]{1,0:T(8,128)S(1)}, u32[]{:S(2)}, u32[]{:S(2)}) %collective-permute-start.11) | collective-permute-done | bytes 32800 | tf_op jit(solution)/shard_map/taps_16/ppermute | solution.py:186
  72.2 3.1 %collective-permute-done.12 = f32[64,128]{1,0:T(8,128)S(1)} collective-permute-done((f32[64,128]{1,0:T(8,128)S(1)}, f32[64,128]{1,0:T(8,128)S(1)}, u32[]{:S(2)}, u32[]{:S(2)}) %collective-permute-start.12) | collective-permute-done | bytes 32800 | tf_op jit(solution)/shard_map/taps_1/ppermute | solution.py:186
  75.4 4.3 %collective-permute-done.13 = f32[64,128]{1,0:T(8,128)S(1)} collective-permute-done((f32[64,128]{1,0:T(8,128)S(1)}, f32[64,128]{1,0:T(8,128)S(1)}, u32[]{:S(2)}, u32[]{:S(2)}) %collective-permute-start.13) | collective-permute-done | bytes 32800 | tf_op jit(solution)/shard_map/taps_2/ppermute | solution.py:186
  79.6 3.0 %collective-permute-start.14 = (f32[64,128]{1,0:T(8,128)S(1)}, f32[64,128]{1,0:T(8,128)S(1)}, u32[]{:S(2)}, u32[]{:S(2)}) collective-permute-start(f32[64,128]{1,0:T(8,128)S(1)} %add.40), channel_id=1, source_target_pairs={{0,32},{8,40},{16,48},{24,56},{32,0},{40,8},{48,16},{56,24},{64,96... | collective-permute-start | bytes 98312 | tf_op jit(solution)/shard_map/taps_4/ppermute | solution.py:186
  82.6 11.7 %collective-permute-done.8 = bf16[256,512]{1,0:T(8,128)(2,1)S(1)} collective-permute-done((bf16[256,512]{1,0:T(8,128)(2,1)S(1)}, bf16[256,512]{1,0:T(8,128)(2,1)S(1)}, u32[]{:S(2)}, u32[]{:S(2)}) %collective-permute-start.8) | collective-permute-done | bytes 262176 | tf_op jit(solution)/shard_map/out3/ppermute | solution.py:186
  94.3 0.8 fusion.3
  95.1 2.0 %backward.1 = (bf16[1024,256]{1,0:T(8,128)(2,1)}, bf16[1024,256]{1,0:T(8,128)(2,1)}, bf16[1024,256]{1,0:T(8,128)(2,1)}) custom-call(bf16[1024,128]{1,0:T(8,128)(2,1)S(1)} %get-tuple-element.35.refs_0_.fg0_ref, bf16[1024,128]{1,0:T(8,128)(2,1)S(1)} %get-tuple-element.36.refs_1_.fg1_ref, bf16[1024,128]{1,0:T(8,128)(2,1)S(1)} %collective-permute-done.9.next_ref, ...), custom_call_target="tpu_custom_call" | custom-call | flops 1 | bytes 1 | tf_op jit(solution)/shard_map/backward/pallas_call | solution.py:22
  (45 shorter events, 6.1 us)
Async XLA Ops:
  2.0 19.2 %collective-permute-start = (bf16[1024,128]{1,0:T(8,128)(2,1)S(1)}, bf16[1024,128]{1,0:T(8,128)(2,1)S(1)}, u32[]{:S(2)}, u32[]{:S(2)}) collective-permute-start(bf16[1024,128]{1,0:T(8,128)(2,1)S(1)} %get-tuple-element.55.cur_ref), channel_id=1, source_target_pairs={{0,8},{8,16},{16,24},{24,32},{32,40},{40,48},{48,56},{56,64},{64,7... | collective-permute-start | bytes 786440 | tf_op jit(solution)/shard_map/halo/ppermute | solution.py:186
  5.2 25.1 %collective-permute-start.2 = (bf16[256,512]{1,0:T(8,128)(2,1)}, bf16[256,512]{1,0:T(8,128)(2,1)S(1)}, u32[]{:S(2)}, u32[]{:S(2)}) collective-permute-start(bf16[256,512]{1,0:T(8,128)(2,1)} %own_ref.1), channel_id=1, source_target_pairs={{0,2},{1,3},{2,0},{3,1},{4,6},{5,7},{6,4},{7,5},{8,10},{9,11},{10,... | collective-permute-start | bytes 786440 | tf_op jit(solution)/shard_map/cot1/ppermute | solution.py:186
  5.3 25.0 %collective-permute-start.3 = (bf16[256,512]{1,0:T(8,128)(2,1)}, bf16[256,512]{1,0:T(8,128)(2,1)S(1)}, u32[]{:S(2)}, u32[]{:S(2)}) collective-permute-start(bf16[256,512]{1,0:T(8,128)(2,1)} %own_ref.1), channel_id=1, source_target_pairs={{0,4},{1,5},{2,6},{3,7},{4,0},{5,1},{6,2},{7,3},{8,12},{9,13},{10,... | collective-permute-start | bytes 786440 | tf_op jit(solution)/shard_map/cot2/ppermute | solution.py:186
  8.4 22.8 %collective-permute-start.4 = (bf16[256,512]{1,0:T(8,128)(2,1)}, bf16[256,512]{1,0:T(8,128)(2,1)S(1)}, u32[]{:S(2)}, u32[]{:S(2)}) collective-permute-start(bf16[256,512]{1,0:T(8,128)(2,1)} %own_ref.1), channel_id=1, source_target_pairs={{0,6},{1,7},{2,4},{3,5},{4,2},{5,3},{6,0},{7,1},{8,14},{9,15},{10,... | collective-permute-start | bytes 786440 | tf_op jit(solution)/shard_map/cot3/ppermute | solution.py:186
  13.1 2.0 %copy-start.2 = (bf16[64,256,128]{2,1,0:T(8,128)(2,1)}, bf16[64,256,128]{2,1,0:T(8,128)(2,1)S(1)}, u32[]{:S(2)}) copy-start(bf16[64,256,128]{2,1,0:T(8,128)(2,1)S(1)} %get-tuple-element.27.band) | copy-start | bytes 12582916
  13.1 8.0 %copy-start.6 = (bf16[1024,256]{1,0:T(8,128)(2,1)S(1)}, bf16[1024,256]{1,0:T(8,128)(2,1)}, u32[]{:S(2)}) copy-start(bf16[1024,256]{1,0:T(8,128)(2,1)} %q_ref.3) | copy-start | bytes 1572868
  21.1 3.4 %copy-start = (bf16[1024,4096]{1,0:T(8,128)(2,1)S(1)}, bf16[1024,4096]{1,0:T(8,128)(2,1)}, u32[]{:S(2)}) copy-start(bf16[1024,4096]{1,0:T(8,128)(2,1)} %w_ref.3) | copy-start | bytes 25165828
  24.5 2.2 %copy-start.3 = (bf16[64,256,128]{2,1,0:T(8,128)(2,1)S(1)}, bf16[64,256,128]{2,1,0:T(8,128)(2,1)}, u32[]{:S(2)}) copy-start(bf16[64,256,128]{2,1,0:T(8,128)(2,1)} %copy-done.2) | copy-start | bytes 12582916
  26.7 4.4 %copy-start.9 = (bf16[256,512]{1,0:T(8,128)(2,1)S(1)}, bf16[256,512]{1,0:T(8,128)(2,1)}, u32[]{:S(2)}) copy-start(bf16[256,512]{1,0:T(8,128)(2,1)} %own_ref.1) | copy-start | bytes 786436
  26.7 10.7 %copy-start.1 = (bf16[1024,4096]{1,0:T(8,128)(2,1)S(1)}, bf16[1024,4096]{1,0:T(8,128)(2,1)}, u32[]{:S(2)}) copy-start(bf16[1024,4096]{1,0:T(8,128)(2,1)} %w_ref.3) | copy-start | bytes 25165828
  31.3 6.2 %collective-permute-start.5 = (bf16[4,256,512]{2,1,0:T(8,128)(2,1)S(1)}, bf16[4,256,512]{2,1,0:T(8,128)(2,1)S(1)}, u32[]{:S(2)}, u32[]{:S(2)}) collective-permute-start(bf16[4,256,512]{2,1,0:T(8,128)(2,1)S(1)} %pad_maximum_fusion), channel_id=1, source_target_pairs={{0,1},{1,0},{2,3},{3,2},{4,5},{5,4},{6,7},{7,6},{8,9},{9,8},{10,11... | collective-permute-start | bytes 3145736 | tf_op jit(solution)/shard_map/cot_swap/ppermute | solution.py:186
  35.1 26.5 %collective-permute-start.1 = (bf16[4,256,512]{2,1,0:T(8,128)(2,1)S(1)}, bf16[4,256,512]{2,1,0:T(8,128)(2,1)S(1)}, u32[]{:S(2)}, u32[]{:S(2)}) collective-permute-start(bf16[4,256,512]{2,1,0:T(8,128)(2,1)S(1)} %get-tuple-element.30), channel_id=1, source_target_pairs={{0,1},{1,0},{2,3},{3,2},{4,5},{5,4},{6,7},{7,6},{8,9},{9,8},{10,11... | collective-permute-start | bytes 3145736 | tf_op jit(solution)/shard_map/out_swap/ppermute | solution.py:186
  40.9 34.3 %collective-permute-start.9 = (bf16[1024,128]{1,0:T(8,128)(2,1)S(1)}, bf16[1024,128]{1,0:T(8,128)(2,1)S(1)}, u32[]{:S(2)}, u32[]{:S(2)}) collective-permute-start(bf16[1024,128]{1,0:T(8,128)(2,1)S(1)} %get-tuple-element.35.refs_0_.fg0_ref), channel_id=1, source_target_pairs={{8,0},{16,8},{24,16},{32,24},{40,32},{48,40},{56,48},{64,56},{72,6... | collective-permute-start | bytes 786440 | tf_op jit(solution)/shard_map/after/ppermute | solution.py:186
  61.6 33.5 %copy-start.5 = (bf16[64,256,128]{2,1,0:T(8,128)(2,1)S(1)}, bf16[64,256,128]{2,1,0:T(8,128)(2,1)}, u32[]{:S(2)}) copy-start(bf16[64,256,128]{2,1,0:T(8,128)(2,1)} %copy-done.4) | copy-start | bytes 12582916
  62.0 33.1 %copy-start.7 = (bf16[1024,256]{1,0:T(8,128)(2,1)S(1)}, bf16[1024,256]{1,0:T(8,128)(2,1)}, u32[]{:S(2)}) copy-start(bf16[1024,256]{1,0:T(8,128)(2,1)} %v_ref.1) | copy-start | bytes 1572868
  62.0 33.1 %copy-start.8 = (bf16[1024,256]{1,0:T(8,128)(2,1)S(1)}, bf16[1024,256]{1,0:T(8,128)(2,1)}, u32[]{:S(2)}) copy-start(bf16[1024,256]{1,0:T(8,128)(2,1)} %k_ref.1) | copy-start | bytes 1572868
  62.1 20.5 %collective-permute-start.6 = (bf16[256,512]{1,0:T(8,128)(2,1)S(1)}, bf16[256,512]{1,0:T(8,128)(2,1)S(1)}, u32[]{:S(2)}, u32[]{:S(2)}) collective-permute-start(bf16[256,512]{1,0:T(8,128)(2,1)S(1)} %get-tuple-element.51), channel_id=1, source_target_pairs={{0,2},{1,3},{2,0},{3,1},{4,6},{5,7},{6,4},{7,5},{8,10},{9,11},{10,... | collective-permute-start | bytes 786440 | tf_op jit(solution)/shard_map/out1/ppermute | solution.py:186
  62.2 20.4 %collective-permute-start.7 = (bf16[256,512]{1,0:T(8,128)(2,1)S(1)}, bf16[256,512]{1,0:T(8,128)(2,1)S(1)}, u32[]{:S(2)}, u32[]{:S(2)}) collective-permute-start(bf16[256,512]{1,0:T(8,128)(2,1)S(1)} %get-tuple-element.53), channel_id=1, source_target_pairs={{0,4},{1,5},{2,6},{3,7},{4,0},{5,1},{6,2},{7,3},{8,12},{9,13},{10,... | collective-permute-start | bytes 786440 | tf_op jit(solution)/shard_map/out2/ppermute | solution.py:186
  62.7 31.5 %collective-permute-start.8 = (bf16[256,512]{1,0:T(8,128)(2,1)S(1)}, bf16[256,512]{1,0:T(8,128)(2,1)S(1)}, u32[]{:S(2)}, u32[]{:S(2)}) collective-permute-start(bf16[256,512]{1,0:T(8,128)(2,1)S(1)} %get-tuple-element.52), channel_id=1, source_target_pairs={{0,6},{1,7},{2,4},{3,5},{4,2},{5,3},{6,0},{7,1},{8,14},{9,15},{10,... | collective-permute-start | bytes 786440 | tf_op jit(solution)/shard_map/out3/ppermute | solution.py:186
  64.8 3.1 %collective-permute-start.10 = (f32[64,128]{1,0:T(8,128)S(1)}, f32[64,128]{1,0:T(8,128)S(1)}, u32[]{:S(2)}, u32[]{:S(2)}) collective-permute-start(f32[64,128]{1,0:T(8,128)S(1)} %taps.1), channel_id=1, source_target_pairs={{0,64},{8,72},{16,80},{24,88},{32,96},{40,104},{48,112},{56,120},{... | collective-permute-start | bytes 98312 | tf_op jit(solution)/shard_map/taps_8/ppermute | solution.py:186
  67.9 4.3 %collective-permute-start.11 = (f32[64,128]{1,0:T(8,128)S(1)}, f32[64,128]{1,0:T(8,128)S(1)}, u32[]{:S(2)}, u32[]{:S(2)}) collective-permute-start(f32[64,128]{1,0:T(8,128)S(1)} %add.37), channel_id=1, source_target_pairs={{0,128},{8,136},{16,144},{24,152},{32,160},{40,168},{48,176},{56,1... | collective-permute-start | bytes 98312 | tf_op jit(solution)/shard_map/taps_16/ppermute | solution.py:186
  72.2 3.1 %collective-permute-start.12 = (f32[64,128]{1,0:T(8,128)S(1)}, f32[64,128]{1,0:T(8,128)S(1)}, u32[]{:S(2)}, u32[]{:S(2)}) collective-permute-start(f32[64,128]{1,0:T(8,128)S(1)} %add.38), channel_id=1, source_target_pairs={{0,8},{8,0},{16,24},{24,16},{32,40},{40,32},{48,56},{56,48},{64,72... | collective-permute-start | bytes 98312 | tf_op jit(solution)/shard_map/taps_1/ppermute | solution.py:186
  75.2 4.4 %collective-permute-start.13 = (f32[64,128]{1,0:T(8,128)S(1)}, f32[64,128]{1,0:T(8,128)S(1)}, u32[]{:S(2)}, u32[]{:S(2)}) collective-permute-start(f32[64,128]{1,0:T(8,128)S(1)} %add.39), channel_id=1, source_target_pairs={{0,16},{8,24},{16,0},{24,8},{32,48},{40,56},{48,32},{56,40},{64,80... | collective-permute-start | bytes 98312 | tf_op jit(solution)/shard_map/taps_2/ppermute | solution.py:186
  79.6 17.5 %collective-permute-start.14 = (f32[64,128]{1,0:T(8,128)S(1)}, f32[64,128]{1,0:T(8,128)S(1)}, u32[]{:S(2)}, u32[]{:S(2)}) collective-permute-start(f32[64,128]{1,0:T(8,128)S(1)} %add.40), channel_id=1, source_target_pairs={{0,32},{8,40},{16,48},{24,56},{32,0},{40,8},{48,16},{56,24},{64,96... | collective-permute-start | bytes 98312 | tf_op jit(solution)/shard_map/taps_4/ppermute | solution.py:186
  (2 other events, 2.7 us)

commit v3 on v2

--- a/solution.py
+++ b/solution.py
@@ -49,20 +49,32 @@
     return slice(half * FL, (half + 1) * FL)
 
 
-def filter_kernel(prev_ref, cur_ref, band, fil_ref, *flips):
-    for ref, flipped in zip((prev_ref, cur_ref), flips):
-        flipped[...] = flip(ref[...])
+def forward_bands(taps_ref, band):
+    taps = taps_ref[...].astype(F32)
+    ahead = jnp.concatenate([taps, jnp.zeros_like(taps)], axis=1)
+    for g in range(taps.shape[0]):
+        fwd = shear(ahead[g : g + 1]).astype(BF)
+        band[g, :FL, :] = fwd[:, FL:]
+        band[g, FL:, :] = fwd[:, :FL]
+
+
+def run_filter(prev_ref, cur_ref, band, fil_ref):
     for g in range(band.shape[0]):
         rows = slice(g * GS, (g + 1) * GS)
         window = jnp.concatenate([prev_ref[rows, :], cur_ref[rows, :]], axis=1)
         fil_ref[rows, :] = jnp.dot(window, band[g], preferred_element_type=F32).astype(BF)
 
 
-def project_kernel(place_ref, prev_ref, cur_ref, q_ref, fil1_ref, band, w_ref, fil0_ref, mine_ref, other_ref, flip_ref, gated_t):
-    filter_kernel(prev_ref, cur_ref, band, fil0_ref, flip_ref)
-    for half, fil_ref in enumerate((fil0_ref, fil1_ref)):
-        cols = half_cols(half)
-        gated_t[cols, :] = (q_ref[:, cols].astype(F32) * fil_ref[...].astype(F32)).astype(BF).T
+def filter_kernel(place_ref, p0_ref, p1_ref, taps_ref, q_ref, w_ref, fil_ref, mine_ref, other_ref, flip0_ref, flip1_ref, gated_t, band):
+    forward_bands(taps_ref, band)
+    flip0_ref[...] = flip(p0_ref[...])
+    flip1_ref[...] = flip(p1_ref[...])
+    run_filter(p0_ref, p1_ref, band, fil_ref)
+    project(1, place_ref, q_ref, fil_ref, w_ref, mine_ref, other_ref, gated_t)
+
+
+def project(half, place_ref, q_ref, fil_ref, w_ref, mine_ref, other_ref, gated_t):
+    gated_t[...] = (q_ref[:, half_cols(half)].astype(F32) * fil_ref[...].astype(F32)).astype(BF).T
     z, core = place_ref[0], place_ref[1]
     chips, _, width = mine_ref.shape
     for k in range(chips):
@@ -73,20 +85,17 @@
             ).astype(BF)
 
 
-def bands_kernel(taps_ref, fwd_ref, bwd_ref):
-    taps = taps_ref[...].astype(F32)
-    ahead = jnp.concatenate([taps, jnp.zeros_like(taps)], axis=1)
-    row = lax.broadcasted_iota(jnp.int32, (FL, 2 * FL), 0)
-    col = lax.broadcasted_iota(jnp.int32, (FL, 2 * FL), 1)
-    wrap = ((row + col) % (2 * FL) == 0).astype(BF)
-    back = jnp.dot(taps_ref[...], wrap, preferred_element_type=F32)
-    for g in range(taps_ref.shape[0]):
-        fwd = shear(ahead[g : g + 1]).astype(BF)
-        bwd = shear(back[g : g + 1]).astype(BF)
-        fwd_ref[g, :FL, :] = fwd[:, FL:]
-        fwd_ref[g, FL:, :] = fwd[:, :FL]
-        bwd_ref[g, :FL, :] = bwd[:, :FL]
-        bwd_ref[g, FL:, :] = bwd[:, FL:]
+def filter_first_kernel(
+    place_ref, near_ref, far_ref, direct_ref, p0_ref, taps_ref, q_ref, w_ref,
+    fil_ref, mine_ref, other_ref, flip_ref, gated_t, band, halo,
+):
+    cut = near_ref.shape[0]
+    halo[:cut, :] = jnp.where(place_ref[2] == 1, far_ref[...], near_ref[...])
+    halo[cut:, :] = direct_ref[...]
+    forward_bands(taps_ref, band)
+    flip_ref[...] = flip(halo[...])
+    run_filter(halo, p0_ref, band, fil_ref)
+    project(0, place_ref, q_ref, fil_ref, w_ref, mine_ref, other_ref, gated_t)
 
 
 def grad_kernel(place_ref, own_ref, g1, g2, g3, mate_ref, w_ref, q_ref, gg_ref, fg0_ref, fg1_ref, cot_t):
@@ -122,12 +131,18 @@
 
 
 def backward_kernel(
-    fg0_ref, fg1_ref, next_ref, band_ref, k_ref, v_ref, gg_ref, fil0_ref, fil1_ref, kg_ref, vg_ref, qg_ref
+    fg0_ref, fg1_ref, next_ref, taps_ref, k_ref, v_ref, gg_ref, fil0_ref, fil1_ref, kg_ref, vg_ref, qg_ref
 ):
+    row = lax.broadcasted_iota(jnp.int32, (FL, 2 * FL), 0)
+    col = lax.broadcasted_iota(jnp.int32, (FL, 2 * FL), 1)
+    wrap = ((row + col) % (2 * FL) == 0).astype(BF)
+    back = jnp.dot(taps_ref[...], wrap, preferred_element_type=F32)
     qg_ref[:, :FL] = (gg_ref[:, :FL] * fil0_ref[...].astype(F32)).astype(BF)
     qg_ref[:, FL:] = (gg_ref[:, FL:] * fil1_ref[...].astype(F32)).astype(BF)
-    for g in range(band_ref.shape[0]):
+    for g in range(taps_ref.shape[0]):
         rows = slice(g * GS, (g + 1) * GS)
+        bwd = shear(back[g : g + 1]).astype(BF)
+        band = jnp.concatenate([bwd[:, :FL], bwd[:, FL:]], axis=0)
         fg1 = fg1_ref[rows, :]
         window = jnp.concatenate(
             [
@@ -136,7 +151,7 @@
             ],
             axis=0,
         )
-        both = jnp.dot(window, band_ref[g], preferred_element_type=F32).astype(BF).astype(F32)
+        both = jnp.dot(window, band, preferred_element_type=F32).astype(BF).astype(F32)
         pg = jnp.concatenate([both[:GS], both[GS:]], axis=1)
         kg_ref[rows, :] = (pg * v_ref[rows, :].astype(F32)).astype(BF)
         vg_ref[rows, :] = (pg * k_ref[rows, :].astype(F32)).astype(BF)
@@ -161,8 +176,7 @@
             if i // ys == j // ys:
                 first.append((source, target))
             else:
-                z, z_half = (i // ys % halves) * zs + t // 2, zs // 2
-                relay = at(i // (ys * halves), (z - z_half) % (halves * zs), j % ys, t % 2)
+                relay = at(i // (ys * halves), (i // ys % halves) * zs + t // 2, j % ys, t % 2)
                 first.append((source, relay))
                 second.append((relay, target))
     return direct, first, second
@@ -177,7 +191,7 @@
     scale = 1.0 / math.sqrt(GS * toks * n_ctx)
     zs = n_ten // 2
     me = lax.axis_index("tensor")
-    place = jnp.stack([me // 2, me % 2]).astype(jnp.int32)
+    place = jnp.stack([me // 2, me % 2, (lax.axis_index("context") % 4 == 0)]).astype(jnp.int32)
     half_shape = shape(chans, FL)
     gg_shape = shape(chans, toks, dt=F32)
 
@@ -187,21 +201,6 @@
 
     def swap(name, array):
         return move(name, array, "tensor", [(j, j ^ 1) for j in range(n_ten)])
-
-    def shift_first(name, array, by):
-        direct, first, _ = shift_pairs(n_ctx, n_ten, by)
-        cut = chans * 3 // 8
-        axes = ("context", "tensor")
-        return move(f"{name}_direct", array[:cut], axes, direct), move(f"{name}_relay", array[cut:], axes, first)
-
-    def shift_second(name, relayed, by):
-        _, _, second = shift_pairs(n_ctx, n_ten, by)
-        return move(f"{name}_end", relayed, ("context", "tensor"), second)
-
-    def shift_join(direct, relayed, end, by):
-        ys = 4
-        at_end = lax.axis_index("context") % ys == (0 if by > 0 else ys - 1)
-        return jnp.concatenate([direct, jnp.where(at_end, end, relayed)], axis=0)
 
     def exchange(name, array, k):
         return move(f"{name}{k}", array, "tensor", [(j, j ^ (2 * k)) for j in range(n_ten)])
@@ -216,21 +215,36 @@
     p1, p0 = [
         (k_proj[:, c].astype(F32) * v_proj[:, c].astype(F32)).astype(BF) for c in map(half_cols, (1, 0))
     ]
-    band_f, band_b = call(bands_kernel, [shape(groups, 2 * FL, FL)] * 2, (filter_taps,), name="bands")
-    fil1, flip0, flip1 = call(filter_kernel, [half_shape] * 3, (p0, p1, band_f), name="filter1")
-    halo = move("halo", p1, "context", [(i, i + 1) for i in range(n_ctx - 1)])
-    fil0, mine, other, fliph = call(
-        project_kernel,
-        [half_shape, shape(zs, toks, width), shape(zs, toks, width), half_shape],
-        (place, halo, p0, q_proj, fil1, band_f, out_weight),
-        specs=[SM] + [VM] * 6,
-        scratch=[pltpu.VMEM((toks, chans), BF)],
-        name="project",
-    )
-    there = swap("out_swap", other)
-
-    *got, fil0 = wave(*got, fil0)
+    axes = ("context", "tensor")
+    direct_pairs, first, second = shift_pairs(n_ctx, n_ten, 1)
+    cut = chans // 2
+    near = move("halo_near", p1[:cut], axes, first)
+    out_half = shape(zs, FL, width)
+    scratch = [pltpu.VMEM((FL, chans), BF), pltpu.VMEM((groups, 2 * FL, FL), BF)]
+    fil1, mine1, other1, flip0, flip1 = call(
+        filter_kernel,
+        [half_shape, out_half, out_half, half_shape, half_shape],
+        (place, p0, p1, filter_taps, q_proj, out_weight),
+        specs=[SM] + [VM] * 5,
+        scratch=scratch,
+        name="forward1",
+    )
+    direct = move("halo_direct", p1[cut:], axes, direct_pairs)
+    far = move("halo_far", near, axes, second)
+    *got, direct, far, other1 = wave(*got, direct, far, other1)
+
     mate = swap("cot_swap", jnp.stack([cotangent, *got]))
+    there1 = swap("out1_swap", other1)
+    fil0, mine0, other0, fliph = call(
+        filter_first_kernel,
+        [half_shape, out_half, out_half, half_shape],
+        (place, near, far, direct, p0, filter_taps, q_proj, out_weight),
+        specs=[SM] + [VM] * 7,
+        scratch=scratch + [pltpu.VMEM((chans, FL), BF)],
+        name="forward0",
+    )
+    there0 = swap("out0_swap", other0)
+    mate, fil0 = wave(mate, fil0)
     gg, fg0, fg1 = call(
         grad_kernel,
         [gg_shape, half_shape, half_shape],
@@ -240,31 +254,35 @@
         name="grad",
     )
     after = move("after", fg0, "context", [(i + 1, i) for i in range(n_ctx - 1)])
-
+    near, fg1 = wave(near, fg1)
     (taps_part,) = call(
         lambda *refs: taps_kernel(scale, *refs),
         [shape(groups, FL, dt=F32)],
         (fg0, fg1, fliph, flip0, flip1),
         name="taps",
     )
-    there, taps_done = wave(there, taps_part)
-    total = mine.astype(F32) + there.astype(F32)
+    total = jnp.concatenate(
+        [m.astype(F32) + t.astype(F32) for m, t in ((mine0, there0), (mine1, there1))], axis=1
+    )
     rest = [exchange("out", total[k].astype(BF), k) for k in range(1, zs)]
-    for s in (8, 16, 1):
-        taps_part = taps_phase(taps_part, [s])
+    taps_part = taps_phase(taps_part, [8])
+    taps_part = taps_phase(taps_part, [16])
+    taps_part = taps_phase(taps_part, [1])
     after, taps_part = wave(after, taps_part)
     k_grad, v_grad, q_grad = call(
         backward_kernel,
         [shape(chans, toks)] * 3,
-        (fg0, fg1, after, band_b, k_proj, v_proj, gg, fil0, fil1),
+        (fg0, fg1, after, filter_taps, k_proj, v_proj, gg, fil0, fil1),
         name="backward",
     )
-    for s in (2, 4):
-        taps_part = taps_phase(taps_part, [s])
+    taps_part = taps_phase(taps_part, [2])
+    taps_part, k_grad = wave(taps_part, k_grad)
+    taps_part = taps_phase(taps_part, [4])
     block_output = total[0]
-    for r in rest:
-        block_output = block_output + r.astype(F32)
-    return (block_output.astype(BF), q_grad, k_grad, v_grad, taps_part)
+    for part in rest:
+        block_output = block_output + part.astype(F32)
+    block_output = block_output.astype(BF)
+    return (block_output, q_grad, k_grad, v_grad, taps_part)
 
 
 def solution(mesh):

time: 98 us -> 91.5 us (0.934)
  the two profiles are of different devices: /device:TPU:39 before, /device:TPU:6 now
where the time goes in v3:
time: 91.5 us; the launch traced here: 91 us
  starting transfers between devices  34.4 us (38%)
  waiting for transfers between devices  33.6 us (37%)
  Pallas kernels  15.1 us (17%)
  local copies, waits for them, and re-layouts  3.48 us (4%)
  other arithmetic  3.45 us (4%)
  between operations  0.93 us (1%)
    ppermute x18, starting transfers between devices, move(): return lax.ppermute(array, axis, pairs)  34.4 us
    ppermute x18, waiting for transfers between devices, move(): return lax.ppermute(array, axis, pairs)  33.6 us
    pallas_call x5, Pallas kernels, call(): pl.pallas_call(kernel, out_shape=outs, in_specs=[VM] * len(args) if specs...  15.1 us
    unnamed x14, local copies, waits for them, and re-layouts  3.41 us
  transfers between devices with their start and end apart: 18, of which 9 were waited for; matrix products, arithmetic and copies ran while one was open for 3% of the time, Pallas kernels for 9%

profile of v3, /device:TPU:6, one launch (start us, length us, event | category | flops | bytes accessed | tf_op | source)
XLA Modules:
  0.0 91.0 jit_solution(18357087016801151318)
XLA Ops:
  0.7 2.0 %collective-permute-start.1 = (bf16[256,512]{1,0:T(8,128)(2,1)}, bf16[256,512]{1,0:T(8,128)(2,1)S(1)}, u32[]{:S(2)}, u32[]{:S(2)}) collective-permute-start(bf16[256,512]{1,0:T(8,128)(2,1)} %own_ref.1), channel_id=1, source_target_pairs={{0,2},{1,3},{2,0},{3,1},{4,6},{5,7},{6,4},{7,5},{8,10},{9,11},{10,... | collective-permute-start | bytes 786440 | tf_op jit(solution)/shard_map/cot1/ppermute | solution.py:200
  2.7 3.3 %collective-permute-start.2 = (bf16[256,512]{1,0:T(8,128)(2,1)}, bf16[256,512]{1,0:T(8,128)(2,1)S(1)}, u32[]{:S(2)}, u32[]{:S(2)}) collective-permute-start(bf16[256,512]{1,0:T(8,128)(2,1)} %own_ref.1), channel_id=1, source_target_pairs={{0,4},{1,5},{2,6},{3,7},{4,0},{5,1},{6,2},{7,3},{8,12},{9,13},{10,... | collective-permute-start | bytes 786440 | tf_op jit(solution)/shard_map/cot2/ppermute | solution.py:200
  5.9 1.3 %multiply_convert_fusion = (bf16[1024,128]{1,0:T(8,128)(2,1)S(1)}, bf16[1024,128]{1,0:T(8,128)(2,1)S(1)}) fusion(bf16[1024,256]{1,0:T(8,128)(2,1)} %v_ref.1, bf16[1024,256]{1,0:T(8,128)(2,1)} %k_ref.1), kind=kLoop, calls=%fused_computation.13 | loop fusion | flops 1048576 | bytes 1572864 | tf_op jit(solution)/shard_map/convert_element_type | solution.py:216
  7.3 3.5 %collective-permute-start = (bf16[512,128]{1,0:T(8,128)(2,1)S(1)}, bf16[512,128]{1,0:T(8,128)(2,1)S(1)}, u32[]{:S(2)}, u32[]{:S(2)}) collective-permute-start(bf16[512,128]{1,0:T(8,128)(2,1)S(1)} %get-tuple-element.67), channel_id=1, source_target_pairs={{0,8},{1,9},{2,10},{3,11},{4,12},{5,13},{6,14},{7,15},{8,16},{9,17... | collective-permute-start | bytes 393224 | tf_op jit(solution)/shard_map/halo_near/ppermute | solution.py:200
  10.9 3.5 %collective-permute-start.4 = (bf16[512,128]{1,0:T(8,128)(2,1)S(1)}, bf16[512,128]{1,0:T(8,128)(2,1)S(1)}, u32[]{:S(2)}, u32[]{:S(2)}) collective-permute-start(bf16[512,128]{1,0:T(8,128)(2,1)S(1)} %get-tuple-element.66), channel_id=1, source_target_pairs={{0,8},{1,9},{2,10},{3,11},{4,12},{5,13},{6,14},{7,15},{8,16},{9,17... | collective-permute-start | bytes 393224 | tf_op jit(solution)/shard_map/halo_direct/ppermute | solution.py:200
  14.4 1.0 %collective-permute-done.near_ref = bf16[512,128]{1,0:T(8,128)(2,1)S(1)} collective-permute-done((bf16[512,128]{1,0:T(8,128)(2,1)S(1)}, bf16[512,128]{1,0:T(8,128)(2,1)S(1)}, u32[]{:S(2)}, u32[]{:S(2)}) %collective-permute-start) | collective-permute-done | bytes 131104 | tf_op jit(solution)/shard_map/halo_near/ppermute | solution.py:200
  15.4 7.3 %collective-permute-start.5 = (bf16[512,128]{1,0:T(8,128)(2,1)S(1)}, bf16[512,128]{1,0:T(8,128)(2,1)S(1)}, u32[]{:S(2)}, u32[]{:S(2)}) collective-permute-start(bf16[512,128]{1,0:T(8,128)(2,1)S(1)} %collective-permute-done.near_ref), channel_id=1, source_target_pairs={{0,32},{1,33},{2,34},{3,35},{4,36},{5,37},{6,38},{7,39},{32,64},{3... | collective-permute-start | bytes 393224 | tf_op jit(solution)/shard_map/halo_far/ppermute | solution.py:200
  22.8 3.4 %copy-done = bf16[1024,4096]{1,0:T(8,128)(2,1)S(1)} copy-done((bf16[1024,4096]{1,0:T(8,128)(2,1)S(1)}, bf16[1024,4096]{1,0:T(8,128)(2,1)}, u32[]{:S(2)}) %copy-start) | copy-done | bytes 8388632
  26.2 3.1 %forward1.1 = (bf16[1024,128]{1,0:T(8,128)(2,1)S(1)}, bf16[4,128,512]{2,1,0:T(8,128)(2,1)S(1)}, bf16[4,128,512]{2,1,0:T(8,128)(2,1)S(1)}, bf16[1024,128]{1,0:T(8,128)(2,1)S(1)}, bf16[1024,128]{1,0:T(8,128)(2,1)S(1)}) custom-call(s32[3]{0:T(128)S(1)} %pad_add_fusion.place_ref, bf16[1024,128]{1,0:T(8,128)(2,1)S(1)} %get-tuple-element.64.p0_ref, ...), custom_call_target="tpu_custom_call" | custom-call | flops 1 | bytes 1 | tf_op jit(solution)/shard_map/forward1/pallas_call | solution.py:22
  29.2 5.6 %collective-permute-done.4.direct_ref = bf16[512,128]{1,0:T(8,128)(2,1)S(1)} collective-permute-done((bf16[512,128]{1,0:T(8,128)(2,1)S(1)}, bf16[512,128]{1,0:T(8,128)(2,1)S(1)}, u32[]{:S(2)}, u32[]{:S(2)}) %collective-permute-start.4) | collective-permute-done | bytes 131104 | tf_op jit(solution)/shard_map/halo_direct/ppermute | solution.py:200
  34.9 3.0 %forward0.1 = (bf16[1024,128]{1,0:T(8,128)(2,1)S(1)}, bf16[4,128,512]{2,1,0:T(8,128)(2,1)S(1)}, bf16[4,128,512]{2,1,0:T(8,128)(2,1)S(1)}, bf16[1024,128]{1,0:T(8,128)(2,1)S(1)}) custom-call(s32[3]{0:T(128)S(1)} %pad_add_fusion.place_ref, bf16[512,128]{1,0:T(8,128)(2,1)S(1)} %collective-permute-done.near_ref, ...), custom_call_target="tpu_custom_call" | custom-call | flops 1 | bytes 1 | tf_op jit(solution)/shard_map/forward0/pallas_call | solution.py:22
  38.9 1.1 %collective-permute-done.6 = bf16[4,128,512]{2,1,0:T(8,128)(2,1)S(1)} collective-permute-done((bf16[4,128,512]{2,1,0:T(8,128)(2,1)S(1)}, bf16[4,128,512]{2,1,0:T(8,128)(2,1)S(1)}, u32[]{:S(2)}, u32[]{:S(2)}) %collective-permute-start.6) | collective-permute-done | bytes 524320 | tf_op jit(solution)/shard_map/out0_swap/ppermute | solution.py:200
  40.1 2.1 %collective-permute-done.7 = bf16[4,128,512]{2,1,0:T(8,128)(2,1)S(1)} collective-permute-done((bf16[4,128,512]{2,1,0:T(8,128)(2,1)S(1)}, bf16[4,128,512]{2,1,0:T(8,128)(2,1)S(1)}, u32[]{:S(2)}, u32[]{:S(2)}) %collective-permute-start.7) | collective-permute-done | bytes 524320 | tf_op jit(solution)/shard_map/out1_swap/ppermute | solution.py:200
  42.5 3.5 %grad.1 = (f32[1024,256]{1,0:T(8,128)S(1)}, bf16[1024,128]{1,0:T(8,128)(2,1)S(1)}, bf16[1024,128]{1,0:T(8,128)(2,1)S(1)}) custom-call(s32[3]{0:T(128)S(1)} %pad_add_fusion.place_ref, bf16[256,512]{1,0:T(8,128)(2,1)S(1)} %copy-done.5, bf16[256,512]{1,0:T(8,128)(2,1)S(1)} %collective-permute-done.1.g1, bf16[256,512]{1,0:T(8,128)(2,1)S(1)} %collective-permute-done.2.g2, ...), custom_call_target="tpu_custom_call" | custom-call | flops 1 | bytes 1 | tf_op jit(solution)/shard_map/grad/pallas_call | solution.py:22
  46.0 6.0 %collective-permute-start.12 = (bf16[1024,128]{1,0:T(8,128)(2,1)S(1)}, bf16[1024,128]{1,0:T(8,128)(2,1)S(1)}, u32[]{:S(2)}, u32[]{:S(2)}) collective-permute-start(bf16[1024,128]{1,0:T(8,128)(2,1)S(1)} %get-tuple-element.45.refs_0_.fg0_ref), channel_id=1, source_target_pairs={{8,0},{16,8},{24,16},{32,24},{40,32},{48,40},{56,48},{64,56},{72,6... | collective-permute-start | bytes 786440 | tf_op jit(solution)/shard_map/after/ppermute | solution.py:200
  52.1 2.0 %collective-permute-start.10 = (bf16[256,512]{1,0:T(8,128)(2,1)S(1)}, bf16[256,512]{1,0:T(8,128)(2,1)S(1)}, u32[]{:S(2)}, u32[]{:S(2)}) collective-permute-start(bf16[256,512]{1,0:T(8,128)(2,1)S(1)} %get-tuple-element.62), channel_id=1, source_target_pairs={{0,6},{1,7},{2,4},{3,5},{4,2},{5,3},{6,0},{7,1},{8,14},{9,15},{10,... | collective-permute-start | bytes 786440 | tf_op jit(solution)/shard_map/out3/ppermute | solution.py:200
  54.1 4.3 %collective-permute-start.9 = (bf16[256,512]{1,0:T(8,128)(2,1)S(1)}, bf16[256,512]{1,0:T(8,128)(2,1)S(1)}, u32[]{:S(2)}, u32[]{:S(2)}) collective-permute-start(bf16[256,512]{1,0:T(8,128)(2,1)S(1)} %get-tuple-element.63), channel_id=1, source_target_pairs={{0,4},{1,5},{2,6},{3,7},{4,0},{5,1},{6,2},{7,3},{8,12},{9,13},{10,... | collective-permute-start | bytes 786440 | tf_op jit(solution)/shard_map/out2/ppermute | solution.py:200
  58.4 2.8 %taps.1 = f32[64,128]{1,0:T(8,128)S(1)} custom-call(bf16[1024,128]{1,0:T(8,128)(2,1)S(1)} %get-tuple-element.45.refs_0_.fg0_ref, bf16[1024,128]{1,0:T(8,128)(2,1)S(1)} %get-tuple-element.47.refs_1_.fg1_ref, bf16[1024,128]{1,0:T(8,128)(2,1)S(1)} %get-tuple-element.48.refs_2_, bf16[1024,128]{1,0:T(8,128)(2,1)S(1)} %get-tuple-element.49.refs_3_, ...), custom_call_target="tpu_custom_call" | custom-call | flops 1 | bytes 1 | tf_op jit(solution)/shard_map/taps/pallas_call | solution.py:22
  61.9 3.5 %collective-permute-done.13 = f32[64,128]{1,0:T(8,128)S(1)} collective-permute-done((f32[64,128]{1,0:T(8,128)S(1)}, f32[64,128]{1,0:T(8,128)S(1)}, u32[]{:S(2)}, u32[]{:S(2)}) %collective-permute-start.13) | collective-permute-done | bytes 32800 | tf_op jit(solution)/shard_map/taps_8/ppermute | solution.py:200
  66.4 4.4 %collective-permute-done.14 = f32[64,128]{1,0:T(8,128)S(1)} collective-permute-done((f32[64,128]{1,0:T(8,128)S(1)}, f32[64,128]{1,0:T(8,128)S(1)}, u32[]{:S(2)}, u32[]{:S(2)}) %collective-permute-start.14) | collective-permute-done | bytes 32800 | tf_op jit(solution)/shard_map/taps_16/ppermute | solution.py:200
  70.8 3.9 %collective-permute-done.15 = f32[64,128]{1,0:T(8,128)S(1)} collective-permute-done((f32[64,128]{1,0:T(8,128)S(1)}, f32[64,128]{1,0:T(8,128)S(1)}, u32[]{:S(2)}, u32[]{:S(2)}) %collective-permute-start.15) | collective-permute-done | bytes 32800 | tf_op jit(solution)/shard_map/taps_1/ppermute | solution.py:200
  74.9 2.7 %backward.1 = (bf16[1024,256]{1,0:T(8,128)(2,1)}, bf16[1024,256]{1,0:T(8,128)(2,1)}, bf16[1024,256]{1,0:T(8,128)(2,1)}) custom-call(bf16[1024,128]{1,0:T(8,128)(2,1)S(1)} %get-tuple-element.45.refs_0_.fg0_ref, bf16[1024,128]{1,0:T(8,128)(2,1)S(1)} %get-tuple-element.47.refs_1_.fg1_ref, bf16[1024,128]{1,0:T(8,128)(2,1)S(1)} %collective-permute-done.12.next_ref, ...), custom_call_target="tpu_custom_call" | custom-call | flops 1 | bytes 1 | tf_op jit(solution)/shard_map/backward/pallas_call | solution.py:22
  77.5 2.7 %collective-permute-done.16 = f32[64,128]{1,0:T(8,128)S(1)} collective-permute-done((f32[64,128]{1,0:T(8,128)S(1)}, f32[64,128]{1,0:T(8,128)S(1)}, u32[]{:S(2)}, u32[]{:S(2)}) %collective-permute-start.16) | collective-permute-done | bytes 32800 | tf_op jit(solution)/shard_map/taps_2/ppermute | solution.py:200
  80.3 9.3 %collective-permute-done.9 = bf16[256,512]{1,0:T(8,128)(2,1)S(1)} collective-permute-done((bf16[256,512]{1,0:T(8,128)(2,1)S(1)}, bf16[256,512]{1,0:T(8,128)(2,1)S(1)}, u32[]{:S(2)}, u32[]{:S(2)}) %collective-permute-start.9) | collective-permute-done | bytes 262176 | tf_op jit(solution)/shard_map/out2/ppermute | solution.py:200
  (45 shorter events, 4.8 us)
Async XLA Ops:
  0.6 10.2 %copy-start.5 = (bf16[256,512]{1,0:T(8,128)(2,1)S(1)}, bf16[256,512]{1,0:T(8,128)(2,1)}, u32[]{:S(2)}) copy-start(bf16[256,512]{1,0:T(8,128)(2,1)} %own_ref.1) | copy-start | bytes 786436
  0.6 22.1 %copy-start.6 = (bf16[64,128]{1,0:T(8,128)(2,1)S(1)}, bf16[64,128]{1,0:T(8,128)(2,1)}, u32[]{:S(2)}) copy-start(bf16[64,128]{1,0:T(8,128)(2,1)} %taps_ref.5) | copy-start | bytes 49156
  0.7 22.1 %copy-start.2 = (bf16[1024,256]{1,0:T(8,128)(2,1)S(1)}, bf16[1024,256]{1,0:T(8,128)(2,1)}, u32[]{:S(2)}) copy-start(bf16[1024,256]{1,0:T(8,128)(2,1)} %q_ref.5) | copy-start | bytes 1572868
  0.7 34.2 %collective-permute-start.1 = (bf16[256,512]{1,0:T(8,128)(2,1)}, bf16[256,512]{1,0:T(8,128)(2,1)S(1)}, u32[]{:S(2)}, u32[]{:S(2)}) collective-permute-start(bf16[256,512]{1,0:T(8,128)(2,1)} %own_ref.1), channel_id=1, source_target_pairs={{0,2},{1,3},{2,0},{3,1},{4,6},{5,7},{6,4},{7,5},{8,10},{9,11},{10,... | collective-permute-start | bytes 786440 | tf_op jit(solution)/shard_map/cot1/ppermute | solution.py:200
  2.7 32.2 %collective-permute-start.2 = (bf16[256,512]{1,0:T(8,128)(2,1)}, bf16[256,512]{1,0:T(8,128)(2,1)S(1)}, u32[]{:S(2)}, u32[]{:S(2)}) collective-permute-start(bf16[256,512]{1,0:T(8,128)(2,1)} %own_ref.1), channel_id=1, source_target_pairs={{0,4},{1,5},{2,6},{3,7},{4,0},{5,1},{6,2},{7,3},{8,12},{9,13},{10,... | collective-permute-start | bytes 786440 | tf_op jit(solution)/shard_map/cot2/ppermute | solution.py:200
  7.3 8.1 %collective-permute-start = (bf16[512,128]{1,0:T(8,128)(2,1)S(1)}, bf16[512,128]{1,0:T(8,128)(2,1)S(1)}, u32[]{:S(2)}, u32[]{:S(2)}) collective-permute-start(bf16[512,128]{1,0:T(8,128)(2,1)S(1)} %get-tuple-element.67), channel_id=1, source_target_pairs={{0,8},{1,9},{2,10},{3,11},{4,12},{5,13},{6,14},{7,15},{8,16},{9,17... | collective-permute-start | bytes 393224 | tf_op jit(solution)/shard_map/halo_near/ppermute | solution.py:200
  10.8 24.1 %collective-permute-start.3 = (bf16[256,512]{1,0:T(8,128)(2,1)S(1)}, bf16[256,512]{1,0:T(8,128)(2,1)S(1)}, u32[]{:S(2)}, u32[]{:S(2)}) collective-permute-start(bf16[256,512]{1,0:T(8,128)(2,1)S(1)} %copy-done.5), channel_id=1, source_target_pairs={{0,6},{1,7},{2,4},{3,5},{4,2},{5,3},{6,0},{7,1},{8,14},{9,15},{10,... | collective-permute-start | bytes 786440 | tf_op jit(solution)/shard_map/cot3/ppermute | solution.py:200
  10.9 24.0 %collective-permute-start.4 = (bf16[512,128]{1,0:T(8,128)(2,1)S(1)}, bf16[512,128]{1,0:T(8,128)(2,1)S(1)}, u32[]{:S(2)}, u32[]{:S(2)}) collective-permute-start(bf16[512,128]{1,0:T(8,128)(2,1)S(1)} %get-tuple-element.66), channel_id=1, source_target_pairs={{0,8},{1,9},{2,10},{3,11},{4,12},{5,13},{6,14},{7,15},{8,16},{9,17... | collective-permute-start | bytes 393224 | tf_op jit(solution)/shard_map/halo_direct/ppermute | solution.py:200
  15.4 19.5 %collective-permute-start.5 = (bf16[512,128]{1,0:T(8,128)(2,1)S(1)}, bf16[512,128]{1,0:T(8,128)(2,1)S(1)}, u32[]{:S(2)}, u32[]{:S(2)}) collective-permute-start(bf16[512,128]{1,0:T(8,128)(2,1)S(1)} %collective-permute-done.near_ref), channel_id=1, source_target_pairs={{0,32},{1,33},{2,34},{3,35},{4,36},{5,37},{6,38},{7,39},{32,64},{3... | collective-permute-start | bytes 393224 | tf_op jit(solution)/shard_map/halo_far/ppermute | solution.py:200
  26.2 8.7 %copy-start.1 = (bf16[1024,4096]{1,0:T(8,128)(2,1)S(1)}, bf16[1024,4096]{1,0:T(8,128)(2,1)}, u32[]{:S(2)}) copy-start(bf16[1024,4096]{1,0:T(8,128)(2,1)} %w_ref.5) | copy-start | bytes 25165828
  37.9 2.0 %collective-permute-start.6 = (bf16[4,128,512]{2,1,0:T(8,128)(2,1)S(1)}, bf16[4,128,512]{2,1,0:T(8,128)(2,1)S(1)}, u32[]{:S(2)}, u32[]{:S(2)}) collective-permute-start(bf16[4,128,512]{2,1,0:T(8,128)(2,1)S(1)} %get-tuple-element.37), channel_id=1, source_target_pairs={{0,1},{1,0},{2,3},{3,2},{4,5},{5,4},{6,7},{7,6},{8,9},{9,8},{10,11... | collective-permute-start | bytes 1572872 | tf_op jit(solution)/shard_map/out0_swap/ppermute | solution.py:200
  38.2 4.3 %collective-permute-start.11 = (bf16[4,256,512]{2,1,0:T(8,128)(2,1)S(1)}, bf16[4,256,512]{2,1,0:T(8,128)(2,1)S(1)}, u32[]{:S(2)}, u32[]{:S(2)}) collective-permute-start(bf16[4,256,512]{2,1,0:T(8,128)(2,1)S(1)} %pad_maximum_fusion.1), channel_id=1, source_target_pairs={{0,1},{1,0},{2,3},{3,2},{4,5},{5,4},{6,7},{7,6},{8,9},{9,8},{10,11... | collective-permute-start | bytes 3145736 | tf_op jit(solution)/shard_map/cot_swap/ppermute | solution.py:200
  38.8 3.4 %collective-permute-start.7 = (bf16[4,128,512]{2,1,0:T(8,128)(2,1)S(1)}, bf16[4,128,512]{2,1,0:T(8,128)(2,1)S(1)}, u32[]{:S(2)}, u32[]{:S(2)}) collective-permute-start(bf16[4,128,512]{2,1,0:T(8,128)(2,1)S(1)} %get-tuple-element.39), channel_id=1, source_target_pairs={{0,1},{1,0},{2,3},{3,2},{4,5},{5,4},{6,7},{7,6},{8,9},{9,8},{10,11... | collective-permute-start | bytes 1572872 | tf_op jit(solution)/shard_map/out1_swap/ppermute | solution.py:200
  46.0 28.9 %copy-start.3 = (bf16[1024,256]{1,0:T(8,128)(2,1)S(1)}, bf16[1024,256]{1,0:T(8,128)(2,1)}, u32[]{:S(2)}) copy-start(bf16[1024,256]{1,0:T(8,128)(2,1)} %v_ref.1) | copy-start | bytes 1572868
  46.0 28.9 %copy-start.4 = (bf16[1024,256]{1,0:T(8,128)(2,1)S(1)}, bf16[1024,256]{1,0:T(8,128)(2,1)}, u32[]{:S(2)}) copy-start(bf16[1024,256]{1,0:T(8,128)(2,1)} %k_ref.1) | copy-start | bytes 1572868
  46.0 28.7 %collective-permute-start.12 = (bf16[1024,128]{1,0:T(8,128)(2,1)S(1)}, bf16[1024,128]{1,0:T(8,128)(2,1)S(1)}, u32[]{:S(2)}, u32[]{:S(2)}) collective-permute-start(bf16[1024,128]{1,0:T(8,128)(2,1)S(1)} %get-tuple-element.45.refs_0_.fg0_ref), channel_id=1, source_target_pairs={{8,0},{16,8},{24,16},{32,24},{40,32},{48,40},{56,48},{64,56},{72,6... | collective-permute-start | bytes 786440 | tf_op jit(solution)/shard_map/after/ppermute | solution.py:200
  52.1 28.2 %collective-permute-start.10 = (bf16[256,512]{1,0:T(8,128)(2,1)S(1)}, bf16[256,512]{1,0:T(8,128)(2,1)S(1)}, u32[]{:S(2)}, u32[]{:S(2)}) collective-permute-start(bf16[256,512]{1,0:T(8,128)(2,1)S(1)} %get-tuple-element.62), channel_id=1, source_target_pairs={{0,6},{1,7},{2,4},{3,5},{4,2},{5,3},{6,0},{7,1},{8,14},{9,15},{10,... | collective-permute-start | bytes 786440 | tf_op jit(solution)/shard_map/out3/ppermute | solution.py:200
  54.1 35.4 %collective-permute-start.9 = (bf16[256,512]{1,0:T(8,128)(2,1)S(1)}, bf16[256,512]{1,0:T(8,128)(2,1)S(1)}, u32[]{:S(2)}, u32[]{:S(2)}) collective-permute-start(bf16[256,512]{1,0:T(8,128)(2,1)S(1)} %get-tuple-element.63), channel_id=1, source_target_pairs={{0,4},{1,5},{2,6},{3,7},{4,0},{5,1},{6,2},{7,3},{8,12},{9,13},{10,... | collective-permute-start | bytes 786440 | tf_op jit(solution)/shard_map/out2/ppermute | solution.py:200
  58.4 31.1 %collective-permute-start.8 = (bf16[256,512]{1,0:T(8,128)(2,1)S(1)}, bf16[256,512]{1,0:T(8,128)(2,1)S(1)}, u32[]{:S(2)}, u32[]{:S(2)}) collective-permute-start(bf16[256,512]{1,0:T(8,128)(2,1)S(1)} %get-tuple-element.61), channel_id=1, source_target_pairs={{0,2},{1,3},{2,0},{3,1},{4,6},{5,7},{6,4},{7,5},{8,10},{9,11},{10,... | collective-permute-start | bytes 786440 | tf_op jit(solution)/shard_map/out1/ppermute | solution.py:200
  61.2 4.2 %collective-permute-start.13 = (f32[64,128]{1,0:T(8,128)S(1)}, f32[64,128]{1,0:T(8,128)S(1)}, u32[]{:S(2)}, u32[]{:S(2)}) collective-permute-start(f32[64,128]{1,0:T(8,128)S(1)} %taps.1), channel_id=1, source_target_pairs={{0,64},{8,72},{16,80},{24,88},{32,96},{40,104},{48,112},{56,120},{... | collective-permute-start | bytes 98312 | tf_op jit(solution)/shard_map/taps_8/ppermute | solution.py:200
  65.4 5.4 %collective-permute-start.14 = (f32[64,128]{1,0:T(8,128)S(1)}, f32[64,128]{1,0:T(8,128)S(1)}, u32[]{:S(2)}, u32[]{:S(2)}) collective-permute-start(f32[64,128]{1,0:T(8,128)S(1)} %add.45), channel_id=1, source_target_pairs={{0,128},{8,136},{16,144},{24,152},{32,160},{40,168},{48,176},{56,1... | collective-permute-start | bytes 98312 | tf_op jit(solution)/shard_map/taps_16/ppermute | solution.py:200
  70.8 3.9 %collective-permute-start.15 = (f32[64,128]{1,0:T(8,128)S(1)}, f32[64,128]{1,0:T(8,128)S(1)}, u32[]{:S(2)}, u32[]{:S(2)}) collective-permute-start(f32[64,128]{1,0:T(8,128)S(1)} %add.46), channel_id=1, source_target_pairs={{0,8},{8,0},{16,24},{24,16},{32,40},{40,32},{48,56},{56,48},{64,72... | collective-permute-start | bytes 98312 | tf_op jit(solution)/shard_map/taps_1/ppermute | solution.py:200
  74.8 5.5 %collective-permute-start.16 = (f32[64,128]{1,0:T(8,128)S(1)}, f32[64,128]{1,0:T(8,128)S(1)}, u32[]{:S(2)}, u32[]{:S(2)}) collective-permute-start(f32[64,128]{1,0:T(8,128)S(1)} %add.47), channel_id=1, source_target_pairs={{0,16},{8,24},{16,0},{24,8},{32,48},{40,56},{48,32},{56,40},{64,80... | collective-permute-start | bytes 98312 | tf_op jit(solution)/shard_map/taps_2/ppermute | solution.py:200
  80.3 10.1 %collective-permute-start.17 = (f32[64,128]{1,0:T(8,128)S(1)}, f32[64,128]{1,0:T(8,128)S(1)}, u32[]{:S(2)}, u32[]{:S(2)}) collective-permute-start(f32[64,128]{1,0:T(8,128)S(1)} %add.48), channel_id=1, source_target_pairs={{0,32},{8,40},{16,48},{24,56},{32,0},{40,8},{48,16},{56,24},{64,96... | collective-permute-start | bytes 98312 | tf_op jit(solution)/shard_map/taps_4/ppermute | solution.py:200
  (1 other events, 3.4 us)

commit v4 on v3

--- a/solution.py
+++ b/solution.py
@@ -111,7 +111,20 @@
         fg_ref[...] = (gg_ref[:, cols] * q_ref[:, cols].astype(F32)).astype(BF)
 
 
-def taps_kernel(scale, fg0_ref, fg_ref, fliph, flip0, flip1, taps_ref):
+def taps_kernel(scale, turn, place_ref, fg0_ref, fg_ref, fliph, flip0, flip1, *rest):
+    *before_ref, taps_ref = rest
+    mine = place_ref[3] == turn
+
+    @pl.when(mine)
+    def _():
+        sum_taps(scale, fg0_ref, fg_ref, fliph, flip0, flip1, taps_ref)
+
+    @pl.when(jnp.logical_not(mine))
+    def _():
+        taps_ref[...] = before_ref[0][...] if before_ref else jnp.zeros_like(taps_ref)
+
+
+def sum_taps(scale, fg0_ref, fg_ref, fliph, flip0, flip1, taps_ref):
     for g in range(taps_ref.shape[0]):
         rows = slice(g * GS, (g + 1) * GS)
         mid = flip0[rows, :]
@@ -191,7 +204,7 @@
     scale = 1.0 / math.sqrt(GS * toks * n_ctx)
     zs = n_ten // 2
     me = lax.axis_index("tensor")
-    place = jnp.stack([me // 2, me % 2, (lax.axis_index("context") % 4 == 0)]).astype(jnp.int32)
+    place = jnp.stack([me // 2, me % 2, lax.axis_index("context") % 4 == 0, lax.axis_index("context") % 4 == 3]).astype(jnp.int32)
     half_shape = shape(chans, FL)
     gg_shape = shape(chans, toks, dt=F32)
 
@@ -253,14 +266,20 @@
         scratch=[pltpu.VMEM((feats, toks), BF)],
         name="grad",
     )
-    after = move("after", fg0, "context", [(i + 1, i) for i in range(n_ctx - 1)])
     near, fg1 = wave(near, fg1)
-    (taps_part,) = call(
-        lambda *refs: taps_kernel(scale, *refs),
-        [shape(groups, FL, dt=F32)],
-        (fg0, fg1, fliph, flip0, flip1),
-        name="taps",
-    )
+    def taps(turn, *before):
+        return call(
+            lambda *refs: taps_kernel(scale, turn, *refs),
+            [shape(groups, FL, dt=F32)],
+            (place, fg0, fg1, fliph, flip0, flip1, *before),
+            specs=[SM] + [VM] * (5 + len(before)),
+            name=f"taps{turn}",
+        )[0]
+
+    taps_part = taps(0)
+    fg0_sent, taps_part = wave(fg0, taps_part)
+    after = move("after", fg0_sent, "context", [(i + 1, i) for i in range(n_ctx - 1)])
+    taps_part = taps(1, taps_part)
     total = jnp.concatenate(
         [m.astype(F32) + t.astype(F32) for m, t in ((mine0, there0), (mine1, there1))], axis=1
     )
@@ -268,20 +287,21 @@
     taps_part = taps_phase(taps_part, [8])
     taps_part = taps_phase(taps_part, [16])
     taps_part = taps_phase(taps_part, [1])
-    after, taps_part = wave(after, taps_part)
+    taps_part = taps_phase(taps_part, [2])
+    after, *rest = wave(after, *rest)
     k_grad, v_grad, q_grad = call(
         backward_kernel,
         [shape(chans, toks)] * 3,
         (fg0, fg1, after, filter_taps, k_proj, v_proj, gg, fil0, fil1),
         name="backward",
     )
-    taps_part = taps_phase(taps_part, [2])
-    taps_part, k_grad = wave(taps_part, k_grad)
-    taps_part = taps_phase(taps_part, [4])
+    last = move("taps_4", taps_part, "context", [(i, i ^ 4) for i in range(n_ctx)])
     block_output = total[0]
     for part in rest:
         block_output = block_output + part.astype(F32)
     block_output = block_output.astype(BF)
+    last, k_grad, block_output = wave(last, k_grad, block_output)
+    taps_part = taps_part + last
     return (block_output, q_grad, k_grad, v_grad, taps_part)
 
 

time: 91.5 us -> 85.8 us (0.938)
  waiting for transfers between devices: 33.6 us -> 29 us
  starting transfers between devices: 34.4 us -> 32.5 us
  Pallas kernels: 15.1 us -> 16.2 us
    ppermute x18, waiting for transfers between devices: 33.6 us -> 29 us  [move(): return lax.ppermute(array, axis, pairs)]
    ppermute x18, starting transfers between devices: 34.4 us -> 32.5 us  [move(): return lax.ppermute(array, axis, pairs)]
    pallas_call x5 -> x6, Pallas kernels: 15.1 us -> 16.2 us  [call(): pl.pallas_call(kernel, out_shape=outs, in_specs=[VM] * len(args) if specs...]
  transfers between devices with their start and end apart: 18 -> 18, of which waited for: 9 -> 8; matrix products, arithmetic and copies ran while one was open for 3% -> 3% of each run, Pallas kernels for 9% -> 19%
where the time goes in v4:
time: 85.8 us; the launch traced here: 85.5 us
  starting transfers between devices  32.5 us (38%)
  waiting for transfers between devices  29 us (34%)
  Pallas kernels  16.2 us (19%)
  local copies, waits for them, and re-layouts  3.48 us (4%)
  other arithmetic  3.44 us (4%)
  between operations  0.94 us (1%)
    ppermute x18, starting transfers between devices, move(): return lax.ppermute(array, axis, pairs)  32.5 us
    ppermute x18, waiting for transfers between devices, move(): return lax.ppermute(array, axis, pairs)  29 us
    pallas_call x6, Pallas kernels, call(): pl.pallas_call(kernel, out_shape=outs, in_specs=[VM] * len(args) if specs...  16.2 us
    unnamed x14, local copies, waits for them, and re-layouts  3.41 us
  transfers between devices with their start and end apart: 18, of which 8 were waited for; matrix products, arithmetic and copies ran while one was open for 3% of the time, Pallas kernels for 19%

profile of v4, /device:TPU:6, one launch (start us, length us, event | category | flops | bytes accessed | tf_op | source)
XLA Modules:
  0.0 85.5 jit_solution(8633394680241827553)
XLA Ops:
  0.7 2.0 %collective-permute-start = (bf16[256,512]{1,0:T(8,128)(2,1)}, bf16[256,512]{1,0:T(8,128)(2,1)S(1)}, u32[]{:S(2)}, u32[]{:S(2)}) collective-permute-start(bf16[256,512]{1,0:T(8,128)(2,1)} %own_ref.1), channel_id=1, source_target_pairs={{0,2},{1,3},{2,0},{3,1},{4,6},{5,7},{6,4},{7,5},{8,10},{9,11},{10,... | collective-permute-start | bytes 786440 | tf_op jit(solution)/shard_map/cot1/ppermute | solution.py:213
  2.7 3.3 %collective-permute-start.1 = (bf16[256,512]{1,0:T(8,128)(2,1)}, bf16[256,512]{1,0:T(8,128)(2,1)S(1)}, u32[]{:S(2)}, u32[]{:S(2)}) collective-permute-start(bf16[256,512]{1,0:T(8,128)(2,1)} %own_ref.1), channel_id=1, source_target_pairs={{0,4},{1,5},{2,6},{3,7},{4,0},{5,1},{6,2},{7,3},{8,12},{9,13},{10,... | collective-permute-start | bytes 786440 | tf_op jit(solution)/shard_map/cot2/ppermute | solution.py:213
  5.9 1.3 %multiply_convert_fusion = (bf16[1024,128]{1,0:T(8,128)(2,1)S(1)}, bf16[1024,128]{1,0:T(8,128)(2,1)S(1)}) fusion(bf16[1024,256]{1,0:T(8,128)(2,1)} %v_ref.1, bf16[1024,256]{1,0:T(8,128)(2,1)} %k_ref.1), kind=kLoop, calls=%fused_computation.13 | loop fusion | flops 1048576 | bytes 1572864 | tf_op jit(solution)/shard_map/convert_element_type | solution.py:229
  7.3 3.5 %collective-permute-start.4 = (bf16[512,128]{1,0:T(8,128)(2,1)S(1)}, bf16[512,128]{1,0:T(8,128)(2,1)S(1)}, u32[]{:S(2)}, u32[]{:S(2)}) collective-permute-start(bf16[512,128]{1,0:T(8,128)(2,1)S(1)} %get-tuple-element.76), channel_id=1, source_target_pairs={{0,8},{1,9},{2,10},{3,11},{4,12},{5,13},{6,14},{7,15},{8,16},{9,17... | collective-permute-start | bytes 393224 | tf_op jit(solution)/shard_map/halo_near/ppermute | solution.py:213
  10.9 3.5 %collective-permute-start.3 = (bf16[512,128]{1,0:T(8,128)(2,1)S(1)}, bf16[512,128]{1,0:T(8,128)(2,1)S(1)}, u32[]{:S(2)}, u32[]{:S(2)}) collective-permute-start(bf16[512,128]{1,0:T(8,128)(2,1)S(1)} %get-tuple-element.77), channel_id=1, source_target_pairs={{0,8},{1,9},{2,10},{3,11},{4,12},{5,13},{6,14},{7,15},{8,16},{9,17... | collective-permute-start | bytes 393224 | tf_op jit(solution)/shard_map/halo_direct/ppermute | solution.py:213
  14.4 1.0 %collective-permute-done.4.near_ref = bf16[512,128]{1,0:T(8,128)(2,1)S(1)} collective-permute-done((bf16[512,128]{1,0:T(8,128)(2,1)S(1)}, bf16[512,128]{1,0:T(8,128)(2,1)S(1)}, u32[]{:S(2)}, u32[]{:S(2)}) %collective-permute-start.4) | collective-permute-done | bytes 131104 | tf_op jit(solution)/shard_map/halo_near/ppermute | solution.py:213
  15.4 7.3 %collective-permute-start.5 = (bf16[512,128]{1,0:T(8,128)(2,1)S(1)}, bf16[512,128]{1,0:T(8,128)(2,1)S(1)}, u32[]{:S(2)}, u32[]{:S(2)}) collective-permute-start(bf16[512,128]{1,0:T(8,128)(2,1)S(1)} %collective-permute-done.4.near_ref), channel_id=1, source_target_pairs={{0,32},{1,33},{2,34},{3,35},{4,36},{5,37},{6,38},{7,39},{32,64},{3... | collective-permute-start | bytes 393224 | tf_op jit(solution)/shard_map/halo_far/ppermute | solution.py:213
  22.8 3.4 %copy-done = bf16[1024,4096]{1,0:T(8,128)(2,1)S(1)} copy-done((bf16[1024,4096]{1,0:T(8,128)(2,1)S(1)}, bf16[1024,4096]{1,0:T(8,128)(2,1)}, u32[]{:S(2)}) %copy-start) | copy-done | bytes 8388632
  26.2 3.1 %forward1.1 = (bf16[1024,128]{1,0:T(8,128)(2,1)S(1)}, bf16[4,128,512]{2,1,0:T(8,128)(2,1)S(1)}, bf16[4,128,512]{2,1,0:T(8,128)(2,1)S(1)}, bf16[1024,128]{1,0:T(8,128)(2,1)S(1)}, bf16[1024,128]{1,0:T(8,128)(2,1)S(1)}) custom-call(s32[4]{0:T(128)S(1)} %pad_add_fusion.place_ref.refs_0_, bf16[1024,128]{1,0:T(8,128)(2,1)S(1)} %get-tuple-element.74.p0_ref, ...), custom_call_target="tpu_custom_call" | custom-call | flops 1 | bytes 1 | tf_op jit(solution)/shard_map/forward1/pallas_call | solution.py:22
  29.2 5.6 %collective-permute-done.3.direct_ref = bf16[512,128]{1,0:T(8,128)(2,1)S(1)} collective-permute-done((bf16[512,128]{1,0:T(8,128)(2,1)S(1)}, bf16[512,128]{1,0:T(8,128)(2,1)S(1)}, u32[]{:S(2)}, u32[]{:S(2)}) %collective-permute-start.3) | collective-permute-done | bytes 131104 | tf_op jit(solution)/shard_map/halo_direct/ppermute | solution.py:213
  35.0 3.0 %forward0.1 = (bf16[1024,128]{1,0:T(8,128)(2,1)S(1)}, bf16[4,128,512]{2,1,0:T(8,128)(2,1)S(1)}, bf16[4,128,512]{2,1,0:T(8,128)(2,1)S(1)}, bf16[1024,128]{1,0:T(8,128)(2,1)S(1)}) custom-call(s32[4]{0:T(128)S(1)} %pad_add_fusion.place_ref.refs_0_, bf16[512,128]{1,0:T(8,128)(2,1)S(1)} %collective-permute-done.4.near_ref, ...), custom_call_target="tpu_custom_call" | custom-call | flops 1 | bytes 1 | tf_op jit(solution)/shard_map/forward0/pallas_call | solution.py:22
  39.0 1.1 %collective-permute-done.13 = bf16[4,128,512]{2,1,0:T(8,128)(2,1)S(1)} collective-permute-done((bf16[4,128,512]{2,1,0:T(8,128)(2,1)S(1)}, bf16[4,128,512]{2,1,0:T(8,128)(2,1)S(1)}, u32[]{:S(2)}, u32[]{:S(2)}) %collective-permute-start.13) | collective-permute-done | bytes 524320 | tf_op jit(solution)/shard_map/out0_swap/ppermute | solution.py:213
  40.6 2.5 %collective-permute-start.16 = (bf16[256,512]{1,0:T(8,128)(2,1)S(1)}, bf16[256,512]{1,0:T(8,128)(2,1)S(1)}, u32[]{:S(2)}, u32[]{:S(2)}) collective-permute-start(bf16[256,512]{1,0:T(8,128)(2,1)S(1)} %get-tuple-element.72), channel_id=1, source_target_pairs={{0,4},{1,5},{2,6},{3,7},{4,0},{5,1},{6,2},{7,3},{8,12},{9,13},{10,... | collective-permute-start | bytes 786440 | tf_op jit(solution)/shard_map/out2/ppermute | solution.py:213
  43.1 1.9 %collective-permute-start.17 = (bf16[256,512]{1,0:T(8,128)(2,1)S(1)}, bf16[256,512]{1,0:T(8,128)(2,1)S(1)}, u32[]{:S(2)}, u32[]{:S(2)}) collective-permute-start(bf16[256,512]{1,0:T(8,128)(2,1)S(1)} %get-tuple-element.71), channel_id=1, source_target_pairs={{0,6},{1,7},{2,4},{3,5},{4,2},{5,3},{6,0},{7,1},{8,14},{9,15},{10,... | collective-permute-start | bytes 786440 | tf_op jit(solution)/shard_map/out3/ppermute | solution.py:213
  45.0 3.5 %grad.1 = (f32[1024,256]{1,0:T(8,128)S(1)}, bf16[1024,128]{1,0:T(8,128)(2,1)S(1)}, bf16[1024,128]{1,0:T(8,128)(2,1)S(1)}) custom-call(s32[4]{0:T(128)S(1)} %pad_add_fusion.place_ref.refs_0_, bf16[256,512]{1,0:T(8,128)(2,1)S(1)} %copy-done.5, bf16[256,512]{1,0:T(8,128)(2,1)S(1)} %collective-permute-done.g1, bf16[256,512]{1,0:T(8,128)(2,1)S(1)} %collective-permute-done.1.g2, ...), custom_call_target="tpu_custom_call" | custom-call | flops 1 | bytes 1 | tf_op jit(solution)/shard_map/grad/pallas_call | solution.py:22
  48.5 3.4 %taps0.1.refs_6_ = f32[64,128]{1,0:T(8,128)S(1)} custom-call(s32[4]{0:T(128)S(1)} %pad_add_fusion.place_ref.refs_0_, bf16[1024,128]{1,0:T(8,128)(2,1)S(1)} %get-tuple-element.53.refs_1_.fg0_ref, bf16[1024,128]{1,0:T(8,128)(2,1)S(1)} %get-tuple-element.48.refs_2_.fg1_ref, bf16[1024,128]{1,0:T(8,128)(2,1)S(1)} %get-tuple-element.49.refs_3_, ...), custom_call_target="tpu_custom_call" | custom-call | flops 1 | bytes 1 | tf_op jit(solution)/shard_map/taps0/pallas_call | solution.py:22
  51.9 5.8 %collective-permute-start.12 = (bf16[1024,128]{1,0:T(8,128)(2,1)S(1)}, bf16[1024,128]{1,0:T(8,128)(2,1)S(1)}, u32[]{:S(2)}, u32[]{:S(2)}) collective-permute-start(bf16[1024,128]{1,0:T(8,128)(2,1)S(1)} %get-tuple-element.53.refs_1_.fg0_ref), channel_id=1, source_target_pairs={{8,0},{16,8},{24,16},{32,24},{40,32},{48,40},{56,48},{64,56},{72,6... | collective-permute-start | bytes 786440 | tf_op jit(solution)/shard_map/after/ppermute | solution.py:213
  58.9 3.4 %collective-permute-done.7 = f32[64,128]{1,0:T(8,128)S(1)} collective-permute-done((f32[64,128]{1,0:T(8,128)S(1)}, f32[64,128]{1,0:T(8,128)S(1)}, u32[]{:S(2)}, u32[]{:S(2)}) %collective-permute-start.7) | collective-permute-done | bytes 32800 | tf_op jit(solution)/shard_map/taps_8/ppermute | solution.py:213
  62.3 1.1 %collective-permute-start.8 = (f32[64,128]{1,0:T(8,128)S(1)}, f32[64,128]{1,0:T(8,128)S(1)}, u32[]{:S(2)}, u32[]{:S(2)}) collective-permute-start(f32[64,128]{1,0:T(8,128)S(1)} %add.41), channel_id=1, source_target_pairs={{0,128},{8,136},{16,144},{24,152},{32,160},{40,168},{48,176},{56,1... | collective-permute-start | bytes 98312 | tf_op jit(solution)/shard_map/taps_16/ppermute | solution.py:213
  63.4 4.3 %collective-permute-done.8 = f32[64,128]{1,0:T(8,128)S(1)} collective-permute-done((f32[64,128]{1,0:T(8,128)S(1)}, f32[64,128]{1,0:T(8,128)S(1)}, u32[]{:S(2)}, u32[]{:S(2)}) %collective-permute-start.8) | collective-permute-done | bytes 32800 | tf_op jit(solution)/shard_map/taps_16/ppermute | solution.py:213
  67.7 3.9 %collective-permute-done.9 = f32[64,128]{1,0:T(8,128)S(1)} collective-permute-done((f32[64,128]{1,0:T(8,128)S(1)}, f32[64,128]{1,0:T(8,128)S(1)}, u32[]{:S(2)}, u32[]{:S(2)}) %collective-permute-start.9) | collective-permute-done | bytes 32800 | tf_op jit(solution)/shard_map/taps_1/ppermute | solution.py:213
  71.6 5.4 %collective-permute-done.10 = f32[64,128]{1,0:T(8,128)S(1)} collective-permute-done((f32[64,128]{1,0:T(8,128)S(1)}, f32[64,128]{1,0:T(8,128)S(1)}, u32[]{:S(2)}, u32[]{:S(2)}) %collective-permute-start.10) | collective-permute-done | bytes 32800 | tf_op jit(solution)/shard_map/taps_2/ppermute | solution.py:213
  78.0 2.7 %backward.1 = (bf16[1024,256]{1,0:T(8,128)(2,1)}, bf16[1024,256]{1,0:T(8,128)(2,1)}, bf16[1024,256]{1,0:T(8,128)(2,1)}) custom-call(bf16[1024,128]{1,0:T(8,128)(2,1)S(1)} %get-tuple-element.53.refs_1_.fg0_ref, bf16[1024,128]{1,0:T(8,128)(2,1)S(1)} %get-tuple-element.48.refs_2_.fg1_ref, bf16[1024,128]{1,0:T(8,128)(2,1)S(1)} %collective-permute-done.12.next_ref, ...), custom_call_target="tpu_custom_call" | custom-call | flops 1 | bytes 1 | tf_op jit(solution)/shard_map/backward/pallas_call | solution.py:22
  80.6 4.3 %collective-permute-done.11 = f32[64,128]{1,0:T(8,128)S(1)} collective-permute-done((f32[64,128]{1,0:T(8,128)S(1)}, f32[64,128]{1,0:T(8,128)S(1)}, u32[]{:S(2)}, u32[]{:S(2)}) %collective-permute-start.11) | collective-permute-done | bytes 32800 | tf_op jit(solution)/shard_map/taps_4/ppermute | solution.py:213
  (46 shorter events, 4.4 us)
Async XLA Ops:
  0.6 10.2 %copy-start.5 = (bf16[256,512]{1,0:T(8,128)(2,1)S(1)}, bf16[256,512]{1,0:T(8,128)(2,1)}, u32[]{:S(2)}) copy-start(bf16[256,512]{1,0:T(8,128)(2,1)} %own_ref.1) | copy-start | bytes 786436
  0.6 22.1 %copy-start.6 = (bf16[64,128]{1,0:T(8,128)(2,1)S(1)}, bf16[64,128]{1,0:T(8,128)(2,1)}, u32[]{:S(2)}) copy-start(bf16[64,128]{1,0:T(8,128)(2,1)} %taps_ref.5) | copy-start | bytes 49156
  0.7 22.1 %copy-start.2 = (bf16[1024,256]{1,0:T(8,128)(2,1)S(1)}, bf16[1024,256]{1,0:T(8,128)(2,1)}, u32[]{:S(2)}) copy-start(bf16[1024,256]{1,0:T(8,128)(2,1)} %q_ref.5) | copy-start | bytes 1572868
  0.7 34.2 %collective-permute-start = (bf16[256,512]{1,0:T(8,128)(2,1)}, bf16[256,512]{1,0:T(8,128)(2,1)S(1)}, u32[]{:S(2)}, u32[]{:S(2)}) collective-permute-start(bf16[256,512]{1,0:T(8,128)(2,1)} %own_ref.1), channel_id=1, source_target_pairs={{0,2},{1,3},{2,0},{3,1},{4,6},{5,7},{6,4},{7,5},{8,10},{9,11},{10,... | collective-permute-start | bytes 786440 | tf_op jit(solution)/shard_map/cot1/ppermute | solution.py:213
  2.7 32.2 %collective-permute-start.1 = (bf16[256,512]{1,0:T(8,128)(2,1)}, bf16[256,512]{1,0:T(8,128)(2,1)S(1)}, u32[]{:S(2)}, u32[]{:S(2)}) collective-permute-start(bf16[256,512]{1,0:T(8,128)(2,1)} %own_ref.1), channel_id=1, source_target_pairs={{0,4},{1,5},{2,6},{3,7},{4,0},{5,1},{6,2},{7,3},{8,12},{9,13},{10,... | collective-permute-start | bytes 786440 | tf_op jit(solution)/shard_map/cot2/ppermute | solution.py:213
  7.3 8.1 %collective-permute-start.4 = (bf16[512,128]{1,0:T(8,128)(2,1)S(1)}, bf16[512,128]{1,0:T(8,128)(2,1)S(1)}, u32[]{:S(2)}, u32[]{:S(2)}) collective-permute-start(bf16[512,128]{1,0:T(8,128)(2,1)S(1)} %get-tuple-element.76), channel_id=1, source_target_pairs={{0,8},{1,9},{2,10},{3,11},{4,12},{5,13},{6,14},{7,15},{8,16},{9,17... | collective-permute-start | bytes 393224 | tf_op jit(solution)/shard_map/halo_near/ppermute | solution.py:213
  10.8 24.1 %collective-permute-start.2 = (bf16[256,512]{1,0:T(8,128)(2,1)S(1)}, bf16[256,512]{1,0:T(8,128)(2,1)S(1)}, u32[]{:S(2)}, u32[]{:S(2)}) collective-permute-start(bf16[256,512]{1,0:T(8,128)(2,1)S(1)} %copy-done.5), channel_id=1, source_target_pairs={{0,6},{1,7},{2,4},{3,5},{4,2},{5,3},{6,0},{7,1},{8,14},{9,15},{10,... | collective-permute-start | bytes 786440 | tf_op jit(solution)/shard_map/cot3/ppermute | solution.py:213
  10.9 24.0 %collective-permute-start.3 = (bf16[512,128]{1,0:T(8,128)(2,1)S(1)}, bf16[512,128]{1,0:T(8,128)(2,1)S(1)}, u32[]{:S(2)}, u32[]{:S(2)}) collective-permute-start(bf16[512,128]{1,0:T(8,128)(2,1)S(1)} %get-tuple-element.77), channel_id=1, source_target_pairs={{0,8},{1,9},{2,10},{3,11},{4,12},{5,13},{6,14},{7,15},{8,16},{9,17... | collective-permute-start | bytes 393224 | tf_op jit(solution)/shard_map/halo_direct/ppermute | solution.py:213
  15.4 19.5 %collective-permute-start.5 = (bf16[512,128]{1,0:T(8,128)(2,1)S(1)}, bf16[512,128]{1,0:T(8,128)(2,1)S(1)}, u32[]{:S(2)}, u32[]{:S(2)}) collective-permute-start(bf16[512,128]{1,0:T(8,128)(2,1)S(1)} %collective-permute-done.4.near_ref), channel_id=1, source_target_pairs={{0,32},{1,33},{2,34},{3,35},{4,36},{5,37},{6,38},{7,39},{32,64},{3... | collective-permute-start | bytes 393224 | tf_op jit(solution)/shard_map/halo_far/ppermute | solution.py:213
  26.2 8.8 %copy-start.1 = (bf16[1024,4096]{1,0:T(8,128)(2,1)S(1)}, bf16[1024,4096]{1,0:T(8,128)(2,1)}, u32[]{:S(2)}) copy-start(bf16[1024,4096]{1,0:T(8,128)(2,1)} %w_ref.5) | copy-start | bytes 25165828
  34.9 4.0 %collective-permute-start.14 = (bf16[4,128,512]{2,1,0:T(8,128)(2,1)S(1)}, bf16[4,128,512]{2,1,0:T(8,128)(2,1)S(1)}, u32[]{:S(2)}, u32[]{:S(2)}) collective-permute-start(bf16[4,128,512]{2,1,0:T(8,128)(2,1)S(1)} %get-tuple-element.57), channel_id=1, source_target_pairs={{0,1},{1,0},{2,3},{3,2},{4,5},{5,4},{6,7},{7,6},{8,9},{9,8},{10,11... | collective-permute-start | bytes 1572872 | tf_op jit(solution)/shard_map/out1_swap/ppermute | solution.py:213
  38.0 2.1 %collective-permute-start.13 = (bf16[4,128,512]{2,1,0:T(8,128)(2,1)S(1)}, bf16[4,128,512]{2,1,0:T(8,128)(2,1)S(1)}, u32[]{:S(2)}, u32[]{:S(2)}) collective-permute-start(bf16[4,128,512]{2,1,0:T(8,128)(2,1)S(1)} %get-tuple-element.55), channel_id=1, source_target_pairs={{0,1},{1,0},{2,3},{3,2},{4,5},{5,4},{6,7},{7,6},{8,9},{9,8},{10,11... | collective-permute-start | bytes 1572872 | tf_op jit(solution)/shard_map/out0_swap/ppermute | solution.py:213
  38.7 6.2 %collective-permute-start.6 = (bf16[4,256,512]{2,1,0:T(8,128)(2,1)S(1)}, bf16[4,256,512]{2,1,0:T(8,128)(2,1)S(1)}, u32[]{:S(2)}, u32[]{:S(2)}) collective-permute-start(bf16[4,256,512]{2,1,0:T(8,128)(2,1)S(1)} %pad_maximum_fusion.1), channel_id=1, source_target_pairs={{0,1},{1,0},{2,3},{3,2},{4,5},{5,4},{6,7},{7,6},{8,9},{9,8},{10,11... | collective-permute-start | bytes 3145736 | tf_op jit(solution)/shard_map/cot_swap/ppermute | solution.py:213
  40.5 36.6 %collective-permute-start.15 = (bf16[256,512]{1,0:T(8,128)(2,1)S(1)}, bf16[256,512]{1,0:T(8,128)(2,1)S(1)}, u32[]{:S(2)}, u32[]{:S(2)}) collective-permute-start(bf16[256,512]{1,0:T(8,128)(2,1)S(1)} %get-tuple-element.73), channel_id=1, source_target_pairs={{0,2},{1,3},{2,0},{3,1},{4,6},{5,7},{6,4},{7,5},{8,10},{9,11},{10,... | collective-permute-start | bytes 786440 | tf_op jit(solution)/shard_map/out1/ppermute | solution.py:213
  40.6 36.5 %collective-permute-start.16 = (bf16[256,512]{1,0:T(8,128)(2,1)S(1)}, bf16[256,512]{1,0:T(8,128)(2,1)S(1)}, u32[]{:S(2)}, u32[]{:S(2)}) collective-permute-start(bf16[256,512]{1,0:T(8,128)(2,1)S(1)} %get-tuple-element.72), channel_id=1, source_target_pairs={{0,4},{1,5},{2,6},{3,7},{4,0},{5,1},{6,2},{7,3},{8,12},{9,13},{10,... | collective-permute-start | bytes 786440 | tf_op jit(solution)/shard_map/out2/ppermute | solution.py:213
  43.1 34.0 %collective-permute-start.17 = (bf16[256,512]{1,0:T(8,128)(2,1)S(1)}, bf16[256,512]{1,0:T(8,128)(2,1)S(1)}, u32[]{:S(2)}, u32[]{:S(2)}) collective-permute-start(bf16[256,512]{1,0:T(8,128)(2,1)S(1)} %get-tuple-element.71), channel_id=1, source_target_pairs={{0,6},{1,7},{2,4},{3,5},{4,2},{5,3},{6,0},{7,1},{8,14},{9,15},{10,... | collective-permute-start | bytes 786440 | tf_op jit(solution)/shard_map/out3/ppermute | solution.py:213
  51.9 25.2 %collective-permute-start.12 = (bf16[1024,128]{1,0:T(8,128)(2,1)S(1)}, bf16[1024,128]{1,0:T(8,128)(2,1)S(1)}, u32[]{:S(2)}, u32[]{:S(2)}) collective-permute-start(bf16[1024,128]{1,0:T(8,128)(2,1)S(1)} %get-tuple-element.53.refs_1_.fg0_ref), channel_id=1, source_target_pairs={{8,0},{16,8},{24,16},{32,24},{40,32},{48,40},{56,48},{64,56},{72,6... | collective-permute-start | bytes 786440 | tf_op jit(solution)/shard_map/after/ppermute | solution.py:213
  58.3 19.7 %copy-start.3 = (bf16[1024,256]{1,0:T(8,128)(2,1)S(1)}, bf16[1024,256]{1,0:T(8,128)(2,1)}, u32[]{:S(2)}) copy-start(bf16[1024,256]{1,0:T(8,128)(2,1)} %v_ref.1) | copy-start | bytes 1572868
  58.3 19.7 %copy-start.4 = (bf16[1024,256]{1,0:T(8,128)(2,1)S(1)}, bf16[1024,256]{1,0:T(8,128)(2,1)}, u32[]{:S(2)}) copy-start(bf16[1024,256]{1,0:T(8,128)(2,1)} %k_ref.1) | copy-start | bytes 1572868
  58.3 4.0 %collective-permute-start.7 = (f32[64,128]{1,0:T(8,128)S(1)}, f32[64,128]{1,0:T(8,128)S(1)}, u32[]{:S(2)}, u32[]{:S(2)}) collective-permute-start(f32[64,128]{1,0:T(8,128)S(1)} %taps1.1), channel_id=1, source_target_pairs={{0,64},{8,72},{16,80},{24,88},{32,96},{40,104},{48,112},{56,120},{... | collective-permute-start | bytes 98312 | tf_op jit(solution)/shard_map/taps_8/ppermute | solution.py:213
  62.3 5.4 %collective-permute-start.8 = (f32[64,128]{1,0:T(8,128)S(1)}, f32[64,128]{1,0:T(8,128)S(1)}, u32[]{:S(2)}, u32[]{:S(2)}) collective-permute-start(f32[64,128]{1,0:T(8,128)S(1)} %add.41), channel_id=1, source_target_pairs={{0,128},{8,136},{16,144},{24,152},{32,160},{40,168},{48,176},{56,1... | collective-permute-start | bytes 98312 | tf_op jit(solution)/shard_map/taps_16/ppermute | solution.py:213
  67.7 3.9 %collective-permute-start.9 = (f32[64,128]{1,0:T(8,128)S(1)}, f32[64,128]{1,0:T(8,128)S(1)}, u32[]{:S(2)}, u32[]{:S(2)}) collective-permute-start(f32[64,128]{1,0:T(8,128)S(1)} %add.42), channel_id=1, source_target_pairs={{0,8},{8,0},{16,24},{24,16},{32,40},{40,32},{48,56},{56,48},{64,72... | collective-permute-start | bytes 98312 | tf_op jit(solution)/shard_map/taps_1/ppermute | solution.py:213
  71.6 5.4 %collective-permute-start.10 = (f32[64,128]{1,0:T(8,128)S(1)}, f32[64,128]{1,0:T(8,128)S(1)}, u32[]{:S(2)}, u32[]{:S(2)}) collective-permute-start(f32[64,128]{1,0:T(8,128)S(1)} %add.43), channel_id=1, source_target_pairs={{0,16},{8,24},{16,0},{24,8},{32,48},{40,56},{48,32},{56,40},{64,80... | collective-permute-start | bytes 98312 | tf_op jit(solution)/shard_map/taps_2/ppermute | solution.py:213
  77.1 7.8 %collective-permute-start.11 = (f32[64,128]{1,0:T(8,128)S(1)}, f32[64,128]{1,0:T(8,128)S(1)}, u32[]{:S(2)}, u32[]{:S(2)}) collective-permute-start(f32[64,128]{1,0:T(8,128)S(1)} %add.44), channel_id=1, source_target_pairs={{0,32},{8,40},{16,48},{24,56},{32,0},{40,8},{48,16},{56,24},{64,96... | collective-permute-start | bytes 98312 | tf_op jit(solution)/shard_map/taps_4/ppermute | solution.py:213
  (1 other events, 3.4 us)

commit v5 on v4

--- a/solution.py
+++ b/solution.py
@@ -18,7 +18,7 @@
 PARAMS = pltpu.CompilerParams(vmem_limit_bytes=16 << 20)
 
 
-def call(kernel, outs, args, specs=None, out_specs=None, scratch=(), name=None):
+def call(kernel, outs, args, specs=None, out_specs=None, scratch=(), name=None, aliases=None):
     return pl.pallas_call(
         kernel,
         out_shape=outs,
@@ -26,6 +26,7 @@
         out_specs=[VM] * len(outs) if out_specs is None else out_specs,
         scratch_shapes=list(scratch),
         compiler_params=PARAMS,
+        input_output_aliases=aliases or {},
         cost_estimate=pl.CostEstimate(flops=1, bytes_accessed=1, transcendentals=0),
         name=name,
     )(*args)
@@ -119,9 +120,11 @@
     def _():
         sum_taps(scale, fg0_ref, fg_ref, fliph, flip0, flip1, taps_ref)
 
-    @pl.when(jnp.logical_not(mine))
-    def _():
-        taps_ref[...] = before_ref[0][...] if before_ref else jnp.zeros_like(taps_ref)
+    if not before_ref:
+
+        @pl.when(jnp.logical_not(mine))
+        def _():
+            taps_ref[...] = jnp.zeros_like(taps_ref)
 
 
 def sum_taps(scale, fg0_ref, fg_ref, fliph, flip0, flip1, taps_ref):
@@ -274,10 +277,11 @@
             (place, fg0, fg1, fliph, flip0, flip1, *before),
             specs=[SM] + [VM] * (5 + len(before)),
             name=f"taps{turn}",
+            aliases={6: 0} if before else None,
         )[0]
 
     taps_part = taps(0)
-    fg0_sent, taps_part = wave(fg0, taps_part)
+    fg0_sent, _ = wave(fg0, taps_part)
     after = move("after", fg0_sent, "context", [(i + 1, i) for i in range(n_ctx - 1)])
     taps_part = taps(1, taps_part)
     total = jnp.concatenate(

time: 85.8 us -> 85.8 us (level)
  no operation moved by 1% of the time
where the time goes in v5:
time: 85.8 us; the launch traced here: 85.5 us
  starting transfers between devices  32.5 us (38%)
  waiting for transfers between devices  29 us (34%)
  Pallas kernels  16.2 us (19%)
  local copies, waits for them, and re-layouts  3.48 us (4%)
  other arithmetic  3.44 us (4%)
  between operations  0.94 us (1%)
    ppermute x18, starting transfers between devices, move(): return lax.ppermute(array, axis, pairs)  32.5 us
    ppermute x18, waiting for transfers between devices, move(): return lax.ppermute(array, axis, pairs)  29 us
    pallas_call x6, Pallas kernels, call(): pl.pallas_call(kernel, out_shape=outs, in_specs=[VM] * len(args) if specs...  16.2 us
    unnamed x14, local copies, waits for them, and re-layouts  3.41 us
  transfers between devices with their start and end apart: 18, of which 8 were waited for; matrix products, arithmetic and copies ran while one was open for 3% of the time, Pallas kernels for 19%

profile of v5, /device:TPU:6, one launch (start us, length us, event | category | flops | bytes accessed | tf_op | source)
XLA Modules:
  0.0 85.5 jit_solution(14570206037298484009)
XLA Ops:
  0.7 2.0 %collective-permute-start = (bf16[256,512]{1,0:T(8,128)(2,1)}, bf16[256,512]{1,0:T(8,128)(2,1)S(1)}, u32[]{:S(2)}, u32[]{:S(2)}) collective-permute-start(bf16[256,512]{1,0:T(8,128)(2,1)} %own_ref.1), channel_id=1, source_target_pairs={{0,2},{1,3},{2,0},{3,1},{4,6},{5,7},{6,4},{7,5},{8,10},{9,11},{10,... | collective-permute-start | bytes 786440 | tf_op jit(solution)/shard_map/cot1/ppermute | solution.py:216
  2.7 3.3 %collective-permute-start.1 = (bf16[256,512]{1,0:T(8,128)(2,1)}, bf16[256,512]{1,0:T(8,128)(2,1)S(1)}, u32[]{:S(2)}, u32[]{:S(2)}) collective-permute-start(bf16[256,512]{1,0:T(8,128)(2,1)} %own_ref.1), channel_id=1, source_target_pairs={{0,4},{1,5},{2,6},{3,7},{4,0},{5,1},{6,2},{7,3},{8,12},{9,13},{10,... | collective-permute-start | bytes 786440 | tf_op jit(solution)/shard_map/cot2/ppermute | solution.py:216
  5.9 1.3 %multiply_convert_fusion = (bf16[1024,128]{1,0:T(8,128)(2,1)S(1)}, bf16[1024,128]{1,0:T(8,128)(2,1)S(1)}) fusion(bf16[1024,256]{1,0:T(8,128)(2,1)} %v_ref.1, bf16[1024,256]{1,0:T(8,128)(2,1)} %k_ref.1), kind=kLoop, calls=%fused_computation.13 | loop fusion | flops 1048576 | bytes 1572864 | tf_op jit(solution)/shard_map/convert_element_type | solution.py:232
  7.3 3.5 %collective-permute-start.4 = (bf16[512,128]{1,0:T(8,128)(2,1)S(1)}, bf16[512,128]{1,0:T(8,128)(2,1)S(1)}, u32[]{:S(2)}, u32[]{:S(2)}) collective-permute-start(bf16[512,128]{1,0:T(8,128)(2,1)S(1)} %get-tuple-element.74), channel_id=1, source_target_pairs={{0,8},{1,9},{2,10},{3,11},{4,12},{5,13},{6,14},{7,15},{8,16},{9,17... | collective-permute-start | bytes 393224 | tf_op jit(solution)/shard_map/halo_near/ppermute | solution.py:216
  10.9 3.5 %collective-permute-start.3 = (bf16[512,128]{1,0:T(8,128)(2,1)S(1)}, bf16[512,128]{1,0:T(8,128)(2,1)S(1)}, u32[]{:S(2)}, u32[]{:S(2)}) collective-permute-start(bf16[512,128]{1,0:T(8,128)(2,1)S(1)} %get-tuple-element.75), channel_id=1, source_target_pairs={{0,8},{1,9},{2,10},{3,11},{4,12},{5,13},{6,14},{7,15},{8,16},{9,17... | collective-permute-start | bytes 393224 | tf_op jit(solution)/shard_map/halo_direct/ppermute | solution.py:216
  14.4 1.0 %collective-permute-done.4.near_ref = bf16[512,128]{1,0:T(8,128)(2,1)S(1)} collective-permute-done((bf16[512,128]{1,0:T(8,128)(2,1)S(1)}, bf16[512,128]{1,0:T(8,128)(2,1)S(1)}, u32[]{:S(2)}, u32[]{:S(2)}) %collective-permute-start.4) | collective-permute-done | bytes 131104 | tf_op jit(solution)/shard_map/halo_near/ppermute | solution.py:216
  15.4 7.3 %collective-permute-start.5 = (bf16[512,128]{1,0:T(8,128)(2,1)S(1)}, bf16[512,128]{1,0:T(8,128)(2,1)S(1)}, u32[]{:S(2)}, u32[]{:S(2)}) collective-permute-start(bf16[512,128]{1,0:T(8,128)(2,1)S(1)} %collective-permute-done.4.near_ref), channel_id=1, source_target_pairs={{0,32},{1,33},{2,34},{3,35},{4,36},{5,37},{6,38},{7,39},{32,64},{3... | collective-permute-start | bytes 393224 | tf_op jit(solution)/shard_map/halo_far/ppermute | solution.py:216
  22.8 3.4 %copy-done = bf16[1024,4096]{1,0:T(8,128)(2,1)S(1)} copy-done((bf16[1024,4096]{1,0:T(8,128)(2,1)S(1)}, bf16[1024,4096]{1,0:T(8,128)(2,1)}, u32[]{:S(2)}) %copy-start) | copy-done | bytes 8388632
  26.2 3.1 %forward1.1 = (bf16[1024,128]{1,0:T(8,128)(2,1)S(1)}, bf16[4,128,512]{2,1,0:T(8,128)(2,1)S(1)}, bf16[4,128,512]{2,1,0:T(8,128)(2,1)S(1)}, bf16[1024,128]{1,0:T(8,128)(2,1)S(1)}, bf16[1024,128]{1,0:T(8,128)(2,1)S(1)}) custom-call(s32[4]{0:T(128)S(1)} %pad_add_fusion.place_ref.refs_0_, bf16[1024,128]{1,0:T(8,128)(2,1)S(1)} %get-tuple-element.72.p0_ref, ...), custom_call_target="tpu_custom_call" | custom-call | flops 1 | bytes 1 | tf_op jit(solution)/shard_map/forward1/pallas_call | solution.py:22
  29.2 5.6 %collective-permute-done.3.direct_ref = bf16[512,128]{1,0:T(8,128)(2,1)S(1)} collective-permute-done((bf16[512,128]{1,0:T(8,128)(2,1)S(1)}, bf16[512,128]{1,0:T(8,128)(2,1)S(1)}, u32[]{:S(2)}, u32[]{:S(2)}) %collective-permute-start.3) | collective-permute-done | bytes 131104 | tf_op jit(solution)/shard_map/halo_direct/ppermute | solution.py:216
  35.0 3.0 %forward0.1 = (bf16[1024,128]{1,0:T(8,128)(2,1)S(1)}, bf16[4,128,512]{2,1,0:T(8,128)(2,1)S(1)}, bf16[4,128,512]{2,1,0:T(8,128)(2,1)S(1)}, bf16[1024,128]{1,0:T(8,128)(2,1)S(1)}) custom-call(s32[4]{0:T(128)S(1)} %pad_add_fusion.place_ref.refs_0_, bf16[512,128]{1,0:T(8,128)(2,1)S(1)} %collective-permute-done.4.near_ref, ...), custom_call_target="tpu_custom_call" | custom-call | flops 1 | bytes 1 | tf_op jit(solution)/shard_map/forward0/pallas_call | solution.py:22
  39.0 1.1 %collective-permute-done.13 = bf16[4,128,512]{2,1,0:T(8,128)(2,1)S(1)} collective-permute-done((bf16[4,128,512]{2,1,0:T(8,128)(2,1)S(1)}, bf16[4,128,512]{2,1,0:T(8,128)(2,1)S(1)}, u32[]{:S(2)}, u32[]{:S(2)}) %collective-permute-start.13) | collective-permute-done | bytes 524320 | tf_op jit(solution)/shard_map/out0_swap/ppermute | solution.py:216
  40.6 2.5 %collective-permute-start.16 = (bf16[256,512]{1,0:T(8,128)(2,1)S(1)}, bf16[256,512]{1,0:T(8,128)(2,1)S(1)}, u32[]{:S(2)}, u32[]{:S(2)}) collective-permute-start(bf16[256,512]{1,0:T(8,128)(2,1)S(1)} %get-tuple-element.70), channel_id=1, source_target_pairs={{0,4},{1,5},{2,6},{3,7},{4,0},{5,1},{6,2},{7,3},{8,12},{9,13},{10,... | collective-permute-start | bytes 786440 | tf_op jit(solution)/shard_map/out2/ppermute | solution.py:216
  43.1 1.9 %collective-permute-start.17 = (bf16[256,512]{1,0:T(8,128)(2,1)S(1)}, bf16[256,512]{1,0:T(8,128)(2,1)S(1)}, u32[]{:S(2)}, u32[]{:S(2)}) collective-permute-start(bf16[256,512]{1,0:T(8,128)(2,1)S(1)} %get-tuple-element.69), channel_id=1, source_target_pairs={{0,6},{1,7},{2,4},{3,5},{4,2},{5,3},{6,0},{7,1},{8,14},{9,15},{10,... | collective-permute-start | bytes 786440 | tf_op jit(solution)/shard_map/out3/ppermute | solution.py:216
  45.0 3.5 %grad.1 = (f32[1024,256]{1,0:T(8,128)S(1)}, bf16[1024,128]{1,0:T(8,128)(2,1)S(1)}, bf16[1024,128]{1,0:T(8,128)(2,1)S(1)}) custom-call(s32[4]{0:T(128)S(1)} %pad_add_fusion.place_ref.refs_0_, bf16[256,512]{1,0:T(8,128)(2,1)S(1)} %copy-done.5, bf16[256,512]{1,0:T(8,128)(2,1)S(1)} %collective-permute-done.g1, bf16[256,512]{1,0:T(8,128)(2,1)S(1)} %collective-permute-done.1.g2, ...), custom_call_target="tpu_custom_call" | custom-call | flops 1 | bytes 1 | tf_op jit(solution)/shard_map/grad/pallas_call | solution.py:22
  48.5 3.4 %taps0.1.refs_6_ = f32[64,128]{1,0:T(8,128)S(1)} custom-call(s32[4]{0:T(128)S(1)} %pad_add_fusion.place_ref.refs_0_, bf16[1024,128]{1,0:T(8,128)(2,1)S(1)} %get-tuple-element.51.refs_1_.fg0_ref, bf16[1024,128]{1,0:T(8,128)(2,1)S(1)} %get-tuple-element.47.refs_2_.fg1_ref, bf16[1024,128]{1,0:T(8,128)(2,1)S(1)} %get-tuple-element.48.refs_3_, ...), custom_call_target="tpu_custom_call" | custom-call | flops 1 | bytes 1 | tf_op jit(solution)/shard_map/taps0/pallas_call | solution.py:22
  51.9 5.8 %collective-permute-start.12 = (bf16[1024,128]{1,0:T(8,128)(2,1)S(1)}, bf16[1024,128]{1,0:T(8,128)(2,1)S(1)}, u32[]{:S(2)}, u32[]{:S(2)}) collective-permute-start(bf16[1024,128]{1,0:T(8,128)(2,1)S(1)} %get-tuple-element.51.refs_1_.fg0_ref), channel_id=1, source_target_pairs={{8,0},{16,8},{24,16},{32,24},{40,32},{48,40},{56,48},{64,56},{72,6... | collective-permute-start | bytes 786440 | tf_op jit(solution)/shard_map/after/ppermute | solution.py:216
  58.9 3.4 %collective-permute-done.7 = f32[64,128]{1,0:T(8,128)S(1)} collective-permute-done((f32[64,128]{1,0:T(8,128)S(1)}, f32[64,128]{1,0:T(8,128)S(1)}, u32[]{:S(2)}, u32[]{:S(2)}) %collective-permute-start.7) | collective-permute-done | bytes 32800 | tf_op jit(solution)/shard_map/taps_8/ppermute | solution.py:216
  62.3 1.1 %collective-permute-start.8 = (f32[64,128]{1,0:T(8,128)S(1)}, f32[64,128]{1,0:T(8,128)S(1)}, u32[]{:S(2)}, u32[]{:S(2)}) collective-permute-start(f32[64,128]{1,0:T(8,128)S(1)} %add.41), channel_id=1, source_target_pairs={{0,128},{8,136},{16,144},{24,152},{32,160},{40,168},{48,176},{56,1... | collective-permute-start | bytes 98312 | tf_op jit(solution)/shard_map/taps_16/ppermute | solution.py:216
  63.4 4.3 %collective-permute-done.8 = f32[64,128]{1,0:T(8,128)S(1)} collective-permute-done((f32[64,128]{1,0:T(8,128)S(1)}, f32[64,128]{1,0:T(8,128)S(1)}, u32[]{:S(2)}, u32[]{:S(2)}) %collective-permute-start.8) | collective-permute-done | bytes 32800 | tf_op jit(solution)/shard_map/taps_16/ppermute | solution.py:216
  67.7 3.9 %collective-permute-done.9 = f32[64,128]{1,0:T(8,128)S(1)} collective-permute-done((f32[64,128]{1,0:T(8,128)S(1)}, f32[64,128]{1,0:T(8,128)S(1)}, u32[]{:S(2)}, u32[]{:S(2)}) %collective-permute-start.9) | collective-permute-done | bytes 32800 | tf_op jit(solution)/shard_map/taps_1/ppermute | solution.py:216
  71.6 5.4 %collective-permute-done.10 = f32[64,128]{1,0:T(8,128)S(1)} collective-permute-done((f32[64,128]{1,0:T(8,128)S(1)}, f32[64,128]{1,0:T(8,128)S(1)}, u32[]{:S(2)}, u32[]{:S(2)}) %collective-permute-start.10) | collective-permute-done | bytes 32800 | tf_op jit(solution)/shard_map/taps_2/ppermute | solution.py:216
  78.0 2.7 %backward.1 = (bf16[1024,256]{1,0:T(8,128)(2,1)}, bf16[1024,256]{1,0:T(8,128)(2,1)}, bf16[1024,256]{1,0:T(8,128)(2,1)}) custom-call(bf16[1024,128]{1,0:T(8,128)(2,1)S(1)} %get-tuple-element.51.refs_1_.fg0_ref, bf16[1024,128]{1,0:T(8,128)(2,1)S(1)} %get-tuple-element.47.refs_2_.fg1_ref, bf16[1024,128]{1,0:T(8,128)(2,1)S(1)} %collective-permute-done.12.next_ref, ...), custom_call_target="tpu_custom_call" | custom-call | flops 1 | bytes 1 | tf_op jit(solution)/shard_map/backward/pallas_call | solution.py:22
  80.6 4.3 %collective-permute-done.11 = f32[64,128]{1,0:T(8,128)S(1)} collective-permute-done((f32[64,128]{1,0:T(8,128)S(1)}, f32[64,128]{1,0:T(8,128)S(1)}, u32[]{:S(2)}, u32[]{:S(2)}) %collective-permute-start.11) | collective-permute-done | bytes 32800 | tf_op jit(solution)/shard_map/taps_4/ppermute | solution.py:216
  (46 shorter events, 4.4 us)
Async XLA Ops:
  0.6 10.2 %copy-start.5 = (bf16[256,512]{1,0:T(8,128)(2,1)S(1)}, bf16[256,512]{1,0:T(8,128)(2,1)}, u32[]{:S(2)}) copy-start(bf16[256,512]{1,0:T(8,128)(2,1)} %own_ref.1) | copy-start | bytes 786436
  0.6 22.1 %copy-start.6 = (bf16[64,128]{1,0:T(8,128)(2,1)S(1)}, bf16[64,128]{1,0:T(8,128)(2,1)}, u32[]{:S(2)}) copy-start(bf16[64,128]{1,0:T(8,128)(2,1)} %taps_ref.5) | copy-start | bytes 49156
  0.7 22.1 %copy-start.2 = (bf16[1024,256]{1,0:T(8,128)(2,1)S(1)}, bf16[1024,256]{1,0:T(8,128)(2,1)}, u32[]{:S(2)}) copy-start(bf16[1024,256]{1,0:T(8,128)(2,1)} %q_ref.5) | copy-start | bytes 1572868
  0.7 34.2 %collective-permute-start = (bf16[256,512]{1,0:T(8,128)(2,1)}, bf16[256,512]{1,0:T(8,128)(2,1)S(1)}, u32[]{:S(2)}, u32[]{:S(2)}) collective-permute-start(bf16[256,512]{1,0:T(8,128)(2,1)} %own_ref.1), channel_id=1, source_target_pairs={{0,2},{1,3},{2,0},{3,1},{4,6},{5,7},{6,4},{7,5},{8,10},{9,11},{10,... | collective-permute-start | bytes 786440 | tf_op jit(solution)/shard_map/cot1/ppermute | solution.py:216
  2.7 32.2 %collective-permute-start.1 = (bf16[256,512]{1,0:T(8,128)(2,1)}, bf16[256,512]{1,0:T(8,128)(2,1)S(1)}, u32[]{:S(2)}, u32[]{:S(2)}) collective-permute-start(bf16[256,512]{1,0:T(8,128)(2,1)} %own_ref.1), channel_id=1, source_target_pairs={{0,4},{1,5},{2,6},{3,7},{4,0},{5,1},{6,2},{7,3},{8,12},{9,13},{10,... | collective-permute-start | bytes 786440 | tf_op jit(solution)/shard_map/cot2/ppermute | solution.py:216
  7.3 8.1 %collective-permute-start.4 = (bf16[512,128]{1,0:T(8,128)(2,1)S(1)}, bf16[512,128]{1,0:T(8,128)(2,1)S(1)}, u32[]{:S(2)}, u32[]{:S(2)}) collective-permute-start(bf16[512,128]{1,0:T(8,128)(2,1)S(1)} %get-tuple-element.74), channel_id=1, source_target_pairs={{0,8},{1,9},{2,10},{3,11},{4,12},{5,13},{6,14},{7,15},{8,16},{9,17... | collective-permute-start | bytes 393224 | tf_op jit(solution)/shard_map/halo_near/ppermute | solution.py:216
  10.8 24.1 %collective-permute-start.2 = (bf16[256,512]{1,0:T(8,128)(2,1)S(1)}, bf16[256,512]{1,0:T(8,128)(2,1)S(1)}, u32[]{:S(2)}, u32[]{:S(2)}) collective-permute-start(bf16[256,512]{1,0:T(8,128)(2,1)S(1)} %copy-done.5), channel_id=1, source_target_pairs={{0,6},{1,7},{2,4},{3,5},{4,2},{5,3},{6,0},{7,1},{8,14},{9,15},{10,... | collective-permute-start | bytes 786440 | tf_op jit(solution)/shard_map/cot3/ppermute | solution.py:216
  10.9 24.0 %collective-permute-start.3 = (bf16[512,128]{1,0:T(8,128)(2,1)S(1)}, bf16[512,128]{1,0:T(8,128)(2,1)S(1)}, u32[]{:S(2)}, u32[]{:S(2)}) collective-permute-start(bf16[512,128]{1,0:T(8,128)(2,1)S(1)} %get-tuple-element.75), channel_id=1, source_target_pairs={{0,8},{1,9},{2,10},{3,11},{4,12},{5,13},{6,14},{7,15},{8,16},{9,17... | collective-permute-start | bytes 393224 | tf_op jit(solution)/shard_map/halo_direct/ppermute | solution.py:216
  15.4 19.5 %collective-permute-start.5 = (bf16[512,128]{1,0:T(8,128)(2,1)S(1)}, bf16[512,128]{1,0:T(8,128)(2,1)S(1)}, u32[]{:S(2)}, u32[]{:S(2)}) collective-permute-start(bf16[512,128]{1,0:T(8,128)(2,1)S(1)} %collective-permute-done.4.near_ref), channel_id=1, source_target_pairs={{0,32},{1,33},{2,34},{3,35},{4,36},{5,37},{6,38},{7,39},{32,64},{3... | collective-permute-start | bytes 393224 | tf_op jit(solution)/shard_map/halo_far/ppermute | solution.py:216
  26.2 8.8 %copy-start.1 = (bf16[1024,4096]{1,0:T(8,128)(2,1)S(1)}, bf16[1024,4096]{1,0:T(8,128)(2,1)}, u32[]{:S(2)}) copy-start(bf16[1024,4096]{1,0:T(8,128)(2,1)} %w_ref.5) | copy-start | bytes 25165828
  34.9 4.0 %collective-permute-start.14 = (bf16[4,128,512]{2,1,0:T(8,128)(2,1)S(1)}, bf16[4,128,512]{2,1,0:T(8,128)(2,1)S(1)}, u32[]{:S(2)}, u32[]{:S(2)}) collective-permute-start(bf16[4,128,512]{2,1,0:T(8,128)(2,1)S(1)} %get-tuple-element.55), channel_id=1, source_target_pairs={{0,1},{1,0},{2,3},{3,2},{4,5},{5,4},{6,7},{7,6},{8,9},{9,8},{10,11... | collective-permute-start | bytes 1572872 | tf_op jit(solution)/shard_map/out1_swap/ppermute | solution.py:216
  38.0 2.1 %collective-permute-start.13 = (bf16[4,128,512]{2,1,0:T(8,128)(2,1)S(1)}, bf16[4,128,512]{2,1,0:T(8,128)(2,1)S(1)}, u32[]{:S(2)}, u32[]{:S(2)}) collective-permute-start(bf16[4,128,512]{2,1,0:T(8,128)(2,1)S(1)} %get-tuple-element.53), channel_id=1, source_target_pairs={{0,1},{1,0},{2,3},{3,2},{4,5},{5,4},{6,7},{7,6},{8,9},{9,8},{10,11... | collective-permute-start | bytes 1572872 | tf_op jit(solution)/shard_map/out0_swap/ppermute | solution.py:216
  38.7 6.2 %collective-permute-start.6 = (bf16[4,256,512]{2,1,0:T(8,128)(2,1)S(1)}, bf16[4,256,512]{2,1,0:T(8,128)(2,1)S(1)}, u32[]{:S(2)}, u32[]{:S(2)}) collective-permute-start(bf16[4,256,512]{2,1,0:T(8,128)(2,1)S(1)} %pad_maximum_fusion.1), channel_id=1, source_target_pairs={{0,1},{1,0},{2,3},{3,2},{4,5},{5,4},{6,7},{7,6},{8,9},{9,8},{10,11... | collective-permute-start | bytes 3145736 | tf_op jit(solution)/shard_map/cot_swap/ppermute | solution.py:216
  40.5 36.6 %collective-permute-start.15 = (bf16[256,512]{1,0:T(8,128)(2,1)S(1)}, bf16[256,512]{1,0:T(8,128)(2,1)S(1)}, u32[]{:S(2)}, u32[]{:S(2)}) collective-permute-start(bf16[256,512]{1,0:T(8,128)(2,1)S(1)} %get-tuple-element.71), channel_id=1, source_target_pairs={{0,2},{1,3},{2,0},{3,1},{4,6},{5,7},{6,4},{7,5},{8,10},{9,11},{10,... | collective-permute-start | bytes 786440 | tf_op jit(solution)/shard_map/out1/ppermute | solution.py:216
  40.6 36.5 %collective-permute-start.16 = (bf16[256,512]{1,0:T(8,128)(2,1)S(1)}, bf16[256,512]{1,0:T(8,128)(2,1)S(1)}, u32[]{:S(2)}, u32[]{:S(2)}) collective-permute-start(bf16[256,512]{1,0:T(8,128)(2,1)S(1)} %get-tuple-element.70), channel_id=1, source_target_pairs={{0,4},{1,5},{2,6},{3,7},{4,0},{5,1},{6,2},{7,3},{8,12},{9,13},{10,... | collective-permute-start | bytes 786440 | tf_op jit(solution)/shard_map/out2/ppermute | solution.py:216
  43.1 34.0 %collective-permute-start.17 = (bf16[256,512]{1,0:T(8,128)(2,1)S(1)}, bf16[256,512]{1,0:T(8,128)(2,1)S(1)}, u32[]{:S(2)}, u32[]{:S(2)}) collective-permute-start(bf16[256,512]{1,0:T(8,128)(2,1)S(1)} %get-tuple-element.69), channel_id=1, source_target_pairs={{0,6},{1,7},{2,4},{3,5},{4,2},{5,3},{6,0},{7,1},{8,14},{9,15},{10,... | collective-permute-start | bytes 786440 | tf_op jit(solution)/shard_map/out3/ppermute | solution.py:216
  51.9 25.2 %collective-permute-start.12 = (bf16[1024,128]{1,0:T(8,128)(2,1)S(1)}, bf16[1024,128]{1,0:T(8,128)(2,1)S(1)}, u32[]{:S(2)}, u32[]{:S(2)}) collective-permute-start(bf16[1024,128]{1,0:T(8,128)(2,1)S(1)} %get-tuple-element.51.refs_1_.fg0_ref), channel_id=1, source_target_pairs={{8,0},{16,8},{24,16},{32,24},{40,32},{48,40},{56,48},{64,56},{72,6... | collective-permute-start | bytes 786440 | tf_op jit(solution)/shard_map/after/ppermute | solution.py:216
  58.3 19.7 %copy-start.3 = (bf16[1024,256]{1,0:T(8,128)(2,1)S(1)}, bf16[1024,256]{1,0:T(8,128)(2,1)}, u32[]{:S(2)}) copy-start(bf16[1024,256]{1,0:T(8,128)(2,1)} %v_ref.1) | copy-start | bytes 1572868
  58.3 19.7 %copy-start.4 = (bf16[1024,256]{1,0:T(8,128)(2,1)S(1)}, bf16[1024,256]{1,0:T(8,128)(2,1)}, u32[]{:S(2)}) copy-start(bf16[1024,256]{1,0:T(8,128)(2,1)} %k_ref.1) | copy-start | bytes 1572868
  58.3 4.0 %collective-permute-start.7 = (f32[64,128]{1,0:T(8,128)S(1)}, f32[64,128]{1,0:T(8,128)S(1)}, u32[]{:S(2)}, u32[]{:S(2)}) collective-permute-start(f32[64,128]{1,0:T(8,128)S(1)} %taps1.1), channel_id=1, source_target_pairs={{0,64},{8,72},{16,80},{24,88},{32,96},{40,104},{48,112},{56,120},{... | collective-permute-start | bytes 98312 | tf_op jit(solution)/shard_map/taps_8/ppermute | solution.py:216
  62.3 5.4 %collective-permute-start.8 = (f32[64,128]{1,0:T(8,128)S(1)}, f32[64,128]{1,0:T(8,128)S(1)}, u32[]{:S(2)}, u32[]{:S(2)}) collective-permute-start(f32[64,128]{1,0:T(8,128)S(1)} %add.41), channel_id=1, source_target_pairs={{0,128},{8,136},{16,144},{24,152},{32,160},{40,168},{48,176},{56,1... | collective-permute-start | bytes 98312 | tf_op jit(solution)/shard_map/taps_16/ppermute | solution.py:216
  67.7 3.9 %collective-permute-start.9 = (f32[64,128]{1,0:T(8,128)S(1)}, f32[64,128]{1,0:T(8,128)S(1)}, u32[]{:S(2)}, u32[]{:S(2)}) collective-permute-start(f32[64,128]{1,0:T(8,128)S(1)} %add.42), channel_id=1, source_target_pairs={{0,8},{8,0},{16,24},{24,16},{32,40},{40,32},{48,56},{56,48},{64,72... | collective-permute-start | bytes 98312 | tf_op jit(solution)/shard_map/taps_1/ppermute | solution.py:216
  71.6 5.4 %collective-permute-start.10 = (f32[64,128]{1,0:T(8,128)S(1)}, f32[64,128]{1,0:T(8,128)S(1)}, u32[]{:S(2)}, u32[]{:S(2)}) collective-permute-start(f32[64,128]{1,0:T(8,128)S(1)} %add.43), channel_id=1, source_target_pairs={{0,16},{8,24},{16,0},{24,8},{32,48},{40,56},{48,32},{56,40},{64,80... | collective-permute-start | bytes 98312 | tf_op jit(solution)/shard_map/taps_2/ppermute | solution.py:216
  77.1 7.8 %collective-permute-start.11 = (f32[64,128]{1,0:T(8,128)S(1)}, f32[64,128]{1,0:T(8,128)S(1)}, u32[]{:S(2)}, u32[]{:S(2)}) collective-permute-start(f32[64,128]{1,0:T(8,128)S(1)} %add.44), channel_id=1, source_target_pairs={{0,32},{8,40},{16,48},{24,56},{32,0},{40,8},{48,16},{56,24},{64,96... | collective-permute-start | bytes 98312 | tf_op jit(solution)/shard_map/taps_4/ppermute | solution.py:216
  (1 other events, 3.4 us)

commit v6 on v5

--- a/solution.py
+++ b/solution.py
@@ -290,8 +290,8 @@
     rest = [exchange("out", total[k].astype(BF), k) for k in range(1, zs)]
     taps_part = taps_phase(taps_part, [8])
     taps_part = taps_phase(taps_part, [16])
+    taps_part = taps_phase(taps_part, [2])
     taps_part = taps_phase(taps_part, [1])
-    taps_part = taps_phase(taps_part, [2])
     after, *rest = wave(after, *rest)
     k_grad, v_grad, q_grad = call(
         backward_kernel,

time: 85.8 us -> 85.8 us (level)
  no operation moved by 1% of the time
where the time goes in v6:
time: 85.8 us; the launch traced here: 85.5 us
  starting transfers between devices  32.5 us (38%)
  waiting for transfers between devices  29 us (34%)
  Pallas kernels  16.2 us (19%)
  local copies, waits for them, and re-layouts  3.48 us (4%)
  other arithmetic  3.44 us (4%)
  between operations  0.94 us (1%)
    ppermute x18, starting transfers between devices, move(): return lax.ppermute(array, axis, pairs)  32.5 us
    ppermute x18, waiting for transfers between devices, move(): return lax.ppermute(array, axis, pairs)  29 us
    pallas_call x6, Pallas kernels, call(): pl.pallas_call(kernel, out_shape=outs, in_specs=[VM] * len(args) if specs...  16.2 us
    unnamed x14, local copies, waits for them, and re-layouts  3.41 us
  transfers between devices with their start and end apart: 18, of which 8 were waited for; matrix products, arithmetic and copies ran while one was open for 3% of the time, Pallas kernels for 19%

profile of v6, /device:TPU:6, one launch (start us, length us, event | category | flops | bytes accessed | tf_op | source)
XLA Modules:
  0.0 85.5 jit_solution(14352711501047642609)
XLA Ops:
  0.7 2.0 %collective-permute-start = (bf16[256,512]{1,0:T(8,128)(2,1)}, bf16[256,512]{1,0:T(8,128)(2,1)S(1)}, u32[]{:S(2)}, u32[]{:S(2)}) collective-permute-start(bf16[256,512]{1,0:T(8,128)(2,1)} %own_ref.1), channel_id=1, source_target_pairs={{0,2},{1,3},{2,0},{3,1},{4,6},{5,7},{6,4},{7,5},{8,10},{9,11},{10,... | collective-permute-start | bytes 786440 | tf_op jit(solution)/shard_map/cot1/ppermute | solution.py:216
  2.7 3.3 %collective-permute-start.1 = (bf16[256,512]{1,0:T(8,128)(2,1)}, bf16[256,512]{1,0:T(8,128)(2,1)S(1)}, u32[]{:S(2)}, u32[]{:S(2)}) collective-permute-start(bf16[256,512]{1,0:T(8,128)(2,1)} %own_ref.1), channel_id=1, source_target_pairs={{0,4},{1,5},{2,6},{3,7},{4,0},{5,1},{6,2},{7,3},{8,12},{9,13},{10,... | collective-permute-start | bytes 786440 | tf_op jit(solution)/shard_map/cot2/ppermute | solution.py:216
  5.9 1.3 %multiply_convert_fusion = (bf16[1024,128]{1,0:T(8,128)(2,1)S(1)}, bf16[1024,128]{1,0:T(8,128)(2,1)S(1)}) fusion(bf16[1024,256]{1,0:T(8,128)(2,1)} %v_ref.1, bf16[1024,256]{1,0:T(8,128)(2,1)} %k_ref.1), kind=kLoop, calls=%fused_computation.13 | loop fusion | flops 1048576 | bytes 1572864 | tf_op jit(solution)/shard_map/convert_element_type | solution.py:232
  7.3 3.5 %collective-permute-start.4 = (bf16[512,128]{1,0:T(8,128)(2,1)S(1)}, bf16[512,128]{1,0:T(8,128)(2,1)S(1)}, u32[]{:S(2)}, u32[]{:S(2)}) collective-permute-start(bf16[512,128]{1,0:T(8,128)(2,1)S(1)} %get-tuple-element.74), channel_id=1, source_target_pairs={{0,8},{1,9},{2,10},{3,11},{4,12},{5,13},{6,14},{7,15},{8,16},{9,17... | collective-permute-start | bytes 393224 | tf_op jit(solution)/shard_map/halo_near/ppermute | solution.py:216
  10.9 3.5 %collective-permute-start.3 = (bf16[512,128]{1,0:T(8,128)(2,1)S(1)}, bf16[512,128]{1,0:T(8,128)(2,1)S(1)}, u32[]{:S(2)}, u32[]{:S(2)}) collective-permute-start(bf16[512,128]{1,0:T(8,128)(2,1)S(1)} %get-tuple-element.75), channel_id=1, source_target_pairs={{0,8},{1,9},{2,10},{3,11},{4,12},{5,13},{6,14},{7,15},{8,16},{9,17... | collective-permute-start | bytes 393224 | tf_op jit(solution)/shard_map/halo_direct/ppermute | solution.py:216
  14.4 1.0 %collective-permute-done.4.near_ref = bf16[512,128]{1,0:T(8,128)(2,1)S(1)} collective-permute-done((bf16[512,128]{1,0:T(8,128)(2,1)S(1)}, bf16[512,128]{1,0:T(8,128)(2,1)S(1)}, u32[]{:S(2)}, u32[]{:S(2)}) %collective-permute-start.4) | collective-permute-done | bytes 131104 | tf_op jit(solution)/shard_map/halo_near/ppermute | solution.py:216
  15.4 7.3 %collective-permute-start.5 = (bf16[512,128]{1,0:T(8,128)(2,1)S(1)}, bf16[512,128]{1,0:T(8,128)(2,1)S(1)}, u32[]{:S(2)}, u32[]{:S(2)}) collective-permute-start(bf16[512,128]{1,0:T(8,128)(2,1)S(1)} %collective-permute-done.4.near_ref), channel_id=1, source_target_pairs={{0,32},{1,33},{2,34},{3,35},{4,36},{5,37},{6,38},{7,39},{32,64},{3... | collective-permute-start | bytes 393224 | tf_op jit(solution)/shard_map/halo_far/ppermute | solution.py:216
  22.8 3.4 %copy-done = bf16[1024,4096]{1,0:T(8,128)(2,1)S(1)} copy-done((bf16[1024,4096]{1,0:T(8,128)(2,1)S(1)}, bf16[1024,4096]{1,0:T(8,128)(2,1)}, u32[]{:S(2)}) %copy-start) | copy-done | bytes 8388632
  26.2 3.1 %forward1.1 = (bf16[1024,128]{1,0:T(8,128)(2,1)S(1)}, bf16[4,128,512]{2,1,0:T(8,128)(2,1)S(1)}, bf16[4,128,512]{2,1,0:T(8,128)(2,1)S(1)}, bf16[1024,128]{1,0:T(8,128)(2,1)S(1)}, bf16[1024,128]{1,0:T(8,128)(2,1)S(1)}) custom-call(s32[4]{0:T(128)S(1)} %pad_add_fusion.place_ref.refs_0_, bf16[1024,128]{1,0:T(8,128)(2,1)S(1)} %get-tuple-element.72.p0_ref, ...), custom_call_target="tpu_custom_call" | custom-call | flops 1 | bytes 1 | tf_op jit(solution)/shard_map/forward1/pallas_call | solution.py:22
  29.2 5.6 %collective-permute-done.3.direct_ref = bf16[512,128]{1,0:T(8,128)(2,1)S(1)} collective-permute-done((bf16[512,128]{1,0:T(8,128)(2,1)S(1)}, bf16[512,128]{1,0:T(8,128)(2,1)S(1)}, u32[]{:S(2)}, u32[]{:S(2)}) %collective-permute-start.3) | collective-permute-done | bytes 131104 | tf_op jit(solution)/shard_map/halo_direct/ppermute | solution.py:216
  35.0 3.0 %forward0.1 = (bf16[1024,128]{1,0:T(8,128)(2,1)S(1)}, bf16[4,128,512]{2,1,0:T(8,128)(2,1)S(1)}, bf16[4,128,512]{2,1,0:T(8,128)(2,1)S(1)}, bf16[1024,128]{1,0:T(8,128)(2,1)S(1)}) custom-call(s32[4]{0:T(128)S(1)} %pad_add_fusion.place_ref.refs_0_, bf16[512,128]{1,0:T(8,128)(2,1)S(1)} %collective-permute-done.4.near_ref, ...), custom_call_target="tpu_custom_call" | custom-call | flops 1 | bytes 1 | tf_op jit(solution)/shard_map/forward0/pallas_call | solution.py:22
  39.0 1.1 %collective-permute-done.13 = bf16[4,128,512]{2,1,0:T(8,128)(2,1)S(1)} collective-permute-done((bf16[4,128,512]{2,1,0:T(8,128)(2,1)S(1)}, bf16[4,128,512]{2,1,0:T(8,128)(2,1)S(1)}, u32[]{:S(2)}, u32[]{:S(2)}) %collective-permute-start.13) | collective-permute-done | bytes 524320 | tf_op jit(solution)/shard_map/out0_swap/ppermute | solution.py:216
  40.6 2.5 %collective-permute-start.16 = (bf16[256,512]{1,0:T(8,128)(2,1)S(1)}, bf16[256,512]{1,0:T(8,128)(2,1)S(1)}, u32[]{:S(2)}, u32[]{:S(2)}) collective-permute-start(bf16[256,512]{1,0:T(8,128)(2,1)S(1)} %get-tuple-element.70), channel_id=1, source_target_pairs={{0,4},{1,5},{2,6},{3,7},{4,0},{5,1},{6,2},{7,3},{8,12},{9,13},{10,... | collective-permute-start | bytes 786440 | tf_op jit(solution)/shard_map/out2/ppermute | solution.py:216
  43.1 1.9 %collective-permute-start.17 = (bf16[256,512]{1,0:T(8,128)(2,1)S(1)}, bf16[256,512]{1,0:T(8,128)(2,1)S(1)}, u32[]{:S(2)}, u32[]{:S(2)}) collective-permute-start(bf16[256,512]{1,0:T(8,128)(2,1)S(1)} %get-tuple-element.69), channel_id=1, source_target_pairs={{0,6},{1,7},{2,4},{3,5},{4,2},{5,3},{6,0},{7,1},{8,14},{9,15},{10,... | collective-permute-start | bytes 786440 | tf_op jit(solution)/shard_map/out3/ppermute | solution.py:216
  45.0 3.5 %grad.1 = (f32[1024,256]{1,0:T(8,128)S(1)}, bf16[1024,128]{1,0:T(8,128)(2,1)S(1)}, bf16[1024,128]{1,0:T(8,128)(2,1)S(1)}) custom-call(s32[4]{0:T(128)S(1)} %pad_add_fusion.place_ref.refs_0_, bf16[256,512]{1,0:T(8,128)(2,1)S(1)} %copy-done.5, bf16[256,512]{1,0:T(8,128)(2,1)S(1)} %collective-permute-done.g1, bf16[256,512]{1,0:T(8,128)(2,1)S(1)} %collective-permute-done.1.g2, ...), custom_call_target="tpu_custom_call" | custom-call | flops 1 | bytes 1 | tf_op jit(solution)/shard_map/grad/pallas_call | solution.py:22
  48.5 3.4 %taps0.1.refs_6_ = f32[64,128]{1,0:T(8,128)S(1)} custom-call(s32[4]{0:T(128)S(1)} %pad_add_fusion.place_ref.refs_0_, bf16[1024,128]{1,0:T(8,128)(2,1)S(1)} %get-tuple-element.51.refs_1_.fg0_ref, bf16[1024,128]{1,0:T(8,128)(2,1)S(1)} %get-tuple-element.47.refs_2_.fg1_ref, bf16[1024,128]{1,0:T(8,128)(2,1)S(1)} %get-tuple-element.48.refs_3_, ...), custom_call_target="tpu_custom_call" | custom-call | flops 1 | bytes 1 | tf_op jit(solution)/shard_map/taps0/pallas_call | solution.py:22
  51.9 5.8 %collective-permute-start.12 = (bf16[1024,128]{1,0:T(8,128)(2,1)S(1)}, bf16[1024,128]{1,0:T(8,128)(2,1)S(1)}, u32[]{:S(2)}, u32[]{:S(2)}) collective-permute-start(bf16[1024,128]{1,0:T(8,128)(2,1)S(1)} %get-tuple-element.51.refs_1_.fg0_ref), channel_id=1, source_target_pairs={{8,0},{16,8},{24,16},{32,24},{40,32},{48,40},{56,48},{64,56},{72,6... | collective-permute-start | bytes 786440 | tf_op jit(solution)/shard_map/after/ppermute | solution.py:216
  58.9 3.4 %collective-permute-done.7 = f32[64,128]{1,0:T(8,128)S(1)} collective-permute-done((f32[64,128]{1,0:T(8,128)S(1)}, f32[64,128]{1,0:T(8,128)S(1)}, u32[]{:S(2)}, u32[]{:S(2)}) %collective-permute-start.7) | collective-permute-done | bytes 32800 | tf_op jit(solution)/shard_map/taps_8/ppermute | solution.py:216
  62.3 1.1 %collective-permute-start.8 = (f32[64,128]{1,0:T(8,128)S(1)}, f32[64,128]{1,0:T(8,128)S(1)}, u32[]{:S(2)}, u32[]{:S(2)}) collective-permute-start(f32[64,128]{1,0:T(8,128)S(1)} %add.41), channel_id=1, source_target_pairs={{0,128},{8,136},{16,144},{24,152},{32,160},{40,168},{48,176},{56,1... | collective-permute-start | bytes 98312 | tf_op jit(solution)/shard_map/taps_16/ppermute | solution.py:216
  63.4 4.3 %collective-permute-done.8 = f32[64,128]{1,0:T(8,128)S(1)} collective-permute-done((f32[64,128]{1,0:T(8,128)S(1)}, f32[64,128]{1,0:T(8,128)S(1)}, u32[]{:S(2)}, u32[]{:S(2)}) %collective-permute-start.8) | collective-permute-done | bytes 32800 | tf_op jit(solution)/shard_map/taps_16/ppermute | solution.py:216
  67.7 5.4 %collective-permute-done.9 = f32[64,128]{1,0:T(8,128)S(1)} collective-permute-done((f32[64,128]{1,0:T(8,128)S(1)}, f32[64,128]{1,0:T(8,128)S(1)}, u32[]{:S(2)}, u32[]{:S(2)}) %collective-permute-start.9) | collective-permute-done | bytes 32800 | tf_op jit(solution)/shard_map/taps_2/ppermute | solution.py:216
  73.1 3.9 %collective-permute-done.10 = f32[64,128]{1,0:T(8,128)S(1)} collective-permute-done((f32[64,128]{1,0:T(8,128)S(1)}, f32[64,128]{1,0:T(8,128)S(1)}, u32[]{:S(2)}, u32[]{:S(2)}) %collective-permute-start.10) | collective-permute-done | bytes 32800 | tf_op jit(solution)/shard_map/taps_1/ppermute | solution.py:216
  78.0 2.7 %backward.1 = (bf16[1024,256]{1,0:T(8,128)(2,1)}, bf16[1024,256]{1,0:T(8,128)(2,1)}, bf16[1024,256]{1,0:T(8,128)(2,1)}) custom-call(bf16[1024,128]{1,0:T(8,128)(2,1)S(1)} %get-tuple-element.51.refs_1_.fg0_ref, bf16[1024,128]{1,0:T(8,128)(2,1)S(1)} %get-tuple-element.47.refs_2_.fg1_ref, bf16[1024,128]{1,0:T(8,128)(2,1)S(1)} %collective-permute-done.12.next_ref, ...), custom_call_target="tpu_custom_call" | custom-call | flops 1 | bytes 1 | tf_op jit(solution)/shard_map/backward/pallas_call | solution.py:22
  80.6 4.3 %collective-permute-done.11 = f32[64,128]{1,0:T(8,128)S(1)} collective-permute-done((f32[64,128]{1,0:T(8,128)S(1)}, f32[64,128]{1,0:T(8,128)S(1)}, u32[]{:S(2)}, u32[]{:S(2)}) %collective-permute-start.11) | collective-permute-done | bytes 32800 | tf_op jit(solution)/shard_map/taps_4/ppermute | solution.py:216
  (46 shorter events, 4.4 us)
Async XLA Ops:
  0.6 10.2 %copy-start.5 = (bf16[256,512]{1,0:T(8,128)(2,1)S(1)}, bf16[256,512]{1,0:T(8,128)(2,1)}, u32[]{:S(2)}) copy-start(bf16[256,512]{1,0:T(8,128)(2,1)} %own_ref.1) | copy-start | bytes 786436
  0.6 22.1 %copy-start.6 = (bf16[64,128]{1,0:T(8,128)(2,1)S(1)}, bf16[64,128]{1,0:T(8,128)(2,1)}, u32[]{:S(2)}) copy-start(bf16[64,128]{1,0:T(8,128)(2,1)} %taps_ref.5) | copy-start | bytes 49156
  0.7 22.1 %copy-start.2 = (bf16[1024,256]{1,0:T(8,128)(2,1)S(1)}, bf16[1024,256]{1,0:T(8,128)(2,1)}, u32[]{:S(2)}) copy-start(bf16[1024,256]{1,0:T(8,128)(2,1)} %q_ref.5) | copy-start | bytes 1572868
  0.7 34.2 %collective-permute-start = (bf16[256,512]{1,0:T(8,128)(2,1)}, bf16[256,512]{1,0:T(8,128)(2,1)S(1)}, u32[]{:S(2)}, u32[]{:S(2)}) collective-permute-start(bf16[256,512]{1,0:T(8,128)(2,1)} %own_ref.1), channel_id=1, source_target_pairs={{0,2},{1,3},{2,0},{3,1},{4,6},{5,7},{6,4},{7,5},{8,10},{9,11},{10,... | collective-permute-start | bytes 786440 | tf_op jit(solution)/shard_map/cot1/ppermute | solution.py:216
  2.7 32.2 %collective-permute-start.1 = (bf16[256,512]{1,0:T(8,128)(2,1)}, bf16[256,512]{1,0:T(8,128)(2,1)S(1)}, u32[]{:S(2)}, u32[]{:S(2)}) collective-permute-start(bf16[256,512]{1,0:T(8,128)(2,1)} %own_ref.1), channel_id=1, source_target_pairs={{0,4},{1,5},{2,6},{3,7},{4,0},{5,1},{6,2},{7,3},{8,12},{9,13},{10,... | collective-permute-start | bytes 786440 | tf_op jit(solution)/shard_map/cot2/ppermute | solution.py:216
  7.3 8.1 %collective-permute-start.4 = (bf16[512,128]{1,0:T(8,128)(2,1)S(1)}, bf16[512,128]{1,0:T(8,128)(2,1)S(1)}, u32[]{:S(2)}, u32[]{:S(2)}) collective-permute-start(bf16[512,128]{1,0:T(8,128)(2,1)S(1)} %get-tuple-element.74), channel_id=1, source_target_pairs={{0,8},{1,9},{2,10},{3,11},{4,12},{5,13},{6,14},{7,15},{8,16},{9,17... | collective-permute-start | bytes 393224 | tf_op jit(solution)/shard_map/halo_near/ppermute | solution.py:216
  10.8 24.1 %collective-permute-start.2 = (bf16[256,512]{1,0:T(8,128)(2,1)S(1)}, bf16[256,512]{1,0:T(8,128)(2,1)S(1)}, u32[]{:S(2)}, u32[]{:S(2)}) collective-permute-start(bf16[256,512]{1,0:T(8,128)(2,1)S(1)} %copy-done.5), channel_id=1, source_target_pairs={{0,6},{1,7},{2,4},{3,5},{4,2},{5,3},{6,0},{7,1},{8,14},{9,15},{10,... | collective-permute-start | bytes 786440 | tf_op jit(solution)/shard_map/cot3/ppermute | solution.py:216
  10.9 24.0 %collective-permute-start.3 = (bf16[512,128]{1,0:T(8,128)(2,1)S(1)}, bf16[512,128]{1,0:T(8,128)(2,1)S(1)}, u32[]{:S(2)}, u32[]{:S(2)}) collective-permute-start(bf16[512,128]{1,0:T(8,128)(2,1)S(1)} %get-tuple-element.75), channel_id=1, source_target_pairs={{0,8},{1,9},{2,10},{3,11},{4,12},{5,13},{6,14},{7,15},{8,16},{9,17... | collective-permute-start | bytes 393224 | tf_op jit(solution)/shard_map/halo_direct/ppermute | solution.py:216
  15.4 19.5 %collective-permute-start.5 = (bf16[512,128]{1,0:T(8,128)(2,1)S(1)}, bf16[512,128]{1,0:T(8,128)(2,1)S(1)}, u32[]{:S(2)}, u32[]{:S(2)}) collective-permute-start(bf16[512,128]{1,0:T(8,128)(2,1)S(1)} %collective-permute-done.4.near_ref), channel_id=1, source_target_pairs={{0,32},{1,33},{2,34},{3,35},{4,36},{5,37},{6,38},{7,39},{32,64},{3... | collective-permute-start | bytes 393224 | tf_op jit(solution)/shard_map/halo_far/ppermute | solution.py:216
  26.2 8.8 %copy-start.1 = (bf16[1024,4096]{1,0:T(8,128)(2,1)S(1)}, bf16[1024,4096]{1,0:T(8,128)(2,1)}, u32[]{:S(2)}) copy-start(bf16[1024,4096]{1,0:T(8,128)(2,1)} %w_ref.5) | copy-start | bytes 25165828
  34.9 4.0 %collective-permute-start.14 = (bf16[4,128,512]{2,1,0:T(8,128)(2,1)S(1)}, bf16[4,128,512]{2,1,0:T(8,128)(2,1)S(1)}, u32[]{:S(2)}, u32[]{:S(2)}) collective-permute-start(bf16[4,128,512]{2,1,0:T(8,128)(2,1)S(1)} %get-tuple-element.55), channel_id=1, source_target_pairs={{0,1},{1,0},{2,3},{3,2},{4,5},{5,4},{6,7},{7,6},{8,9},{9,8},{10,11... | collective-permute-start | bytes 1572872 | tf_op jit(solution)/shard_map/out1_swap/ppermute | solution.py:216
  38.0 2.1 %collective-permute-start.13 = (bf16[4,128,512]{2,1,0:T(8,128)(2,1)S(1)}, bf16[4,128,512]{2,1,0:T(8,128)(2,1)S(1)}, u32[]{:S(2)}, u32[]{:S(2)}) collective-permute-start(bf16[4,128,512]{2,1,0:T(8,128)(2,1)S(1)} %get-tuple-element.53), channel_id=1, source_target_pairs={{0,1},{1,0},{2,3},{3,2},{4,5},{5,4},{6,7},{7,6},{8,9},{9,8},{10,11... | collective-permute-start | bytes 1572872 | tf_op jit(solution)/shard_map/out0_swap/ppermute | solution.py:216
  38.7 6.2 %collective-permute-start.6 = (bf16[4,256,512]{2,1,0:T(8,128)(2,1)S(1)}, bf16[4,256,512]{2,1,0:T(8,128)(2,1)S(1)}, u32[]{:S(2)}, u32[]{:S(2)}) collective-permute-start(bf16[4,256,512]{2,1,0:T(8,128)(2,1)S(1)} %pad_maximum_fusion.1), channel_id=1, source_target_pairs={{0,1},{1,0},{2,3},{3,2},{4,5},{5,4},{6,7},{7,6},{8,9},{9,8},{10,11... | collective-permute-start | bytes 3145736 | tf_op jit(solution)/shard_map/cot_swap/ppermute | solution.py:216
  40.5 36.6 %collective-permute-start.15 = (bf16[256,512]{1,0:T(8,128)(2,1)S(1)}, bf16[256,512]{1,0:T(8,128)(2,1)S(1)}, u32[]{:S(2)}, u32[]{:S(2)}) collective-permute-start(bf16[256,512]{1,0:T(8,128)(2,1)S(1)} %get-tuple-element.71), channel_id=1, source_target_pairs={{0,2},{1,3},{2,0},{3,1},{4,6},{5,7},{6,4},{7,5},{8,10},{9,11},{10,... | collective-permute-start | bytes 786440 | tf_op jit(solution)/shard_map/out1/ppermute | solution.py:216
  40.6 36.5 %collective-permute-start.16 = (bf16[256,512]{1,0:T(8,128)(2,1)S(1)}, bf16[256,512]{1,0:T(8,128)(2,1)S(1)}, u32[]{:S(2)}, u32[]{:S(2)}) collective-permute-start(bf16[256,512]{1,0:T(8,128)(2,1)S(1)} %get-tuple-element.70), channel_id=1, source_target_pairs={{0,4},{1,5},{2,6},{3,7},{4,0},{5,1},{6,2},{7,3},{8,12},{9,13},{10,... | collective-permute-start | bytes 786440 | tf_op jit(solution)/shard_map/out2/ppermute | solution.py:216
  43.1 34.0 %collective-permute-start.17 = (bf16[256,512]{1,0:T(8,128)(2,1)S(1)}, bf16[256,512]{1,0:T(8,128)(2,1)S(1)}, u32[]{:S(2)}, u32[]{:S(2)}) collective-permute-start(bf16[256,512]{1,0:T(8,128)(2,1)S(1)} %get-tuple-element.69), channel_id=1, source_target_pairs={{0,6},{1,7},{2,4},{3,5},{4,2},{5,3},{6,0},{7,1},{8,14},{9,15},{10,... | collective-permute-start | bytes 786440 | tf_op jit(solution)/shard_map/out3/ppermute | solution.py:216
  51.9 25.2 %collective-permute-start.12 = (bf16[1024,128]{1,0:T(8,128)(2,1)S(1)}, bf16[1024,128]{1,0:T(8,128)(2,1)S(1)}, u32[]{:S(2)}, u32[]{:S(2)}) collective-permute-start(bf16[1024,128]{1,0:T(8,128)(2,1)S(1)} %get-tuple-element.51.refs_1_.fg0_ref), channel_id=1, source_target_pairs={{8,0},{16,8},{24,16},{32,24},{40,32},{48,40},{56,48},{64,56},{72,6... | collective-permute-start | bytes 786440 | tf_op jit(solution)/shard_map/after/ppermute | solution.py:216
  58.3 19.7 %copy-start.3 = (bf16[1024,256]{1,0:T(8,128)(2,1)S(1)}, bf16[1024,256]{1,0:T(8,128)(2,1)}, u32[]{:S(2)}) copy-start(bf16[1024,256]{1,0:T(8,128)(2,1)} %v_ref.1) | copy-start | bytes 1572868
  58.3 19.7 %copy-start.4 = (bf16[1024,256]{1,0:T(8,128)(2,1)S(1)}, bf16[1024,256]{1,0:T(8,128)(2,1)}, u32[]{:S(2)}) copy-start(bf16[1024,256]{1,0:T(8,128)(2,1)} %k_ref.1) | copy-start | bytes 1572868
  58.3 4.0 %collective-permute-start.7 = (f32[64,128]{1,0:T(8,128)S(1)}, f32[64,128]{1,0:T(8,128)S(1)}, u32[]{:S(2)}, u32[]{:S(2)}) collective-permute-start(f32[64,128]{1,0:T(8,128)S(1)} %taps1.1), channel_id=1, source_target_pairs={{0,64},{8,72},{16,80},{24,88},{32,96},{40,104},{48,112},{56,120},{... | collective-permute-start | bytes 98312 | tf_op jit(solution)/shard_map/taps_8/ppermute | solution.py:216
  62.3 5.4 %collective-permute-start.8 = (f32[64,128]{1,0:T(8,128)S(1)}, f32[64,128]{1,0:T(8,128)S(1)}, u32[]{:S(2)}, u32[]{:S(2)}) collective-permute-start(f32[64,128]{1,0:T(8,128)S(1)} %add.41), channel_id=1, source_target_pairs={{0,128},{8,136},{16,144},{24,152},{32,160},{40,168},{48,176},{56,1... | collective-permute-start | bytes 98312 | tf_op jit(solution)/shard_map/taps_16/ppermute | solution.py:216
  67.7 5.4 %collective-permute-start.9 = (f32[64,128]{1,0:T(8,128)S(1)}, f32[64,128]{1,0:T(8,128)S(1)}, u32[]{:S(2)}, u32[]{:S(2)}) collective-permute-start(f32[64,128]{1,0:T(8,128)S(1)} %add.42), channel_id=1, source_target_pairs={{0,16},{8,24},{16,0},{24,8},{32,48},{40,56},{48,32},{56,40},{64,80... | collective-permute-start | bytes 98312 | tf_op jit(solution)/shard_map/taps_2/ppermute | solution.py:216
  73.1 3.9 %collective-permute-start.10 = (f32[64,128]{1,0:T(8,128)S(1)}, f32[64,128]{1,0:T(8,128)S(1)}, u32[]{:S(2)}, u32[]{:S(2)}) collective-permute-start(f32[64,128]{1,0:T(8,128)S(1)} %add.43), channel_id=1, source_target_pairs={{0,8},{8,0},{16,24},{24,16},{32,40},{40,32},{48,56},{56,48},{64,72... | collective-permute-start | bytes 98312 | tf_op jit(solution)/shard_map/taps_1/ppermute | solution.py:216
  77.1 7.8 %collective-permute-start.11 = (f32[64,128]{1,0:T(8,128)S(1)}, f32[64,128]{1,0:T(8,128)S(1)}, u32[]{:S(2)}, u32[]{:S(2)}) collective-permute-start(f32[64,128]{1,0:T(8,128)S(1)} %add.44), channel_id=1, source_target_pairs={{0,32},{8,40},{16,48},{24,56},{32,0},{40,8},{48,16},{56,24},{64,96... | collective-permute-start | bytes 98312 | tf_op jit(solution)/shard_map/taps_4/ppermute | solution.py:216
  (1 other events, 3.4 us)
